TPU v7x, 32 devices: a whole 2x2x4 slice. The times are simulated.
32 devices in a mesh: az: 8 (over z, x), ax: 4 (over y, core).
Axes of the slice: x: 2, y: 2, z: 4, core: 2. Of those that a mesh axis runs over, the one named last changes fastest.
Arguments:
- state: float32 [1536, 5, 512], P(('az', 'ax')), may hold values from -6 to 6
- velocity: float32 [1536, 3], P(('az', 'ax')), may hold values from -4 to 4
- interp_maps: float32 [1536, 3, 8, 8], P(('az', 'ax')), may hold values from -2 to 2
- neighbours: int32 [1536, 6], P(('az', 'ax')), may hold values from 0 to 479
- send_faces: int32 [1536], P(('az', 'ax')), may hold values from 0 to 287
- owner_device: int32 [1536, 1], P(('az', 'ax')), may hold values from 0 to 7; in each aligned block of 48 rows (0 to 47, 48 to 95, ...) at most 15 rows name the same one
- owner_block: int32 [1536], P(('az', 'ax')), may hold values from 0 to 7
Outputs:
- new_state: float32 [1536, 5, 512], P(('az', 'ax'))
- spectrum: float32 [2, 5, 1024, 128], P(None, None, ('az', 'ax'))
Inputs may be any that keep to these rules, and one draw needn't show every extreme that they name: `owner_device`: in the rows of one device at most 15 elements name the same owner sector, and 15 is reached in some device.
All inputs are finite; a program needn't handle non-finite values.
Results may differ from a plain program's by a relative error of at most 0.0003.
Values sent between devices are 32-bit elements; how exact they have to be, the bound alone decides.
No kernel may reach another device: no remote copies, remote signals or barrier semaphores. Data moves between devices by JAX's collectives and lax.ppermute only.
A program may use at most 64 MiB of HBM per device.

v0:
```python
import math

import jax
import jax.numpy as jnp
import numpy as np
from jax import lax
from jax.sharding import PartitionSpec as P

TB = 2
PB = 4
CB_DEV = 8


time_step = 0.02
penalty = 5.0
highest = lax.Precision.HIGHEST


def spectral_derivative():
    points = np.cos(np.pi * np.arange(8) / 7.0)
    ends = (np.arange(8) == 0) | (np.arange(8) == 7)
    scales = np.where(ends, 2.0, 1.0)
    signs = np.where(np.arange(8) % 2 == 0, 1.0, -1.0)
    differ = points[:, None] - points[None, :]
    offdiag = (
        scales[:, None]
        / scales[None, :]
        * signs[:, None]
        * signs[None, :]
        / np.where(np.eye(8) > 0, 1.0, differ)
    )
    inner = -points / (2.0 * np.where(ends, 1.0, 1.0 - points * points))
    corner = (2.0 * 49.0 + 1.0) / 6.0
    diagonal = np.where(np.arange(8) == 0, corner, np.where(np.arange(8) == 7, -corner, inner))
    return np.where(np.eye(8) > 0, diagonal[:, None], offdiag)


def section_rate(flat_state, velocity, neighbours, send_faces, deriv):
    elements = velocity.shape[0]
    cube = flat_state.reshape(elements, 5, 8, 8, 8)
    along_x = jnp.einsum("ia,ecajk->ecijk", deriv, cube, precision=highest)
    along_y = jnp.einsum("ja,eciak->ecijk", deriv, cube, precision=highest)
    along_z = jnp.einsum("ka,ecija->ecijk", deriv, cube, precision=highest)
    speed = velocity[:, :, None, None, None, None]
    advect = -(speed[:, 0] * along_x + speed[:, 1] * along_y + speed[:, 2] * along_z)
    own_faces = jnp.stack(
        [
            cube[:, :, 0],
            cube[:, :, 7],
            cube[:, :, :, 0],
            cube[:, :, :, 7],
            cube[:, :, :, :, 0],
            cube[:, :, :, :, 7],
        ],
        axis=2,
    ).reshape(elements, 5, 6, 64)
    local_table = own_faces.transpose(0, 2, 1, 3).reshape(elements * 6, 320)
    shared = local_table[send_faces]
    gathered = lax.all_gather(shared, "ax", axis=0, tiled=True)
    tables = jnp.concatenate([local_table, gathered], axis=0)
    facing = tables[neighbours.reshape(-1)].reshape(elements, 6, 5, 64).transpose(0, 2, 1, 3)
    face_jump = (penalty * (facing - own_faces)).reshape(elements, 5, 6, 8, 8)
    result = advect
    result = result.at[:, :, 0].add(face_jump[:, :, 0])
    result = result.at[:, :, 7].add(face_jump[:, :, 1])
    result = result.at[:, :, :, 0].add(face_jump[:, :, 2])
    result = result.at[:, :, :, 7].add(face_jump[:, :, 3])
    result = result.at[:, :, :, :, 0].add(face_jump[:, :, 4])
    result = result.at[:, :, :, :, 7].add(face_jump[:, :, 5])
    return result.reshape(elements * 5, 512)


def interpolate(flat_state, interp_maps):
    elements = interp_maps.shape[0]
    node_cube = flat_state.reshape(elements, 5, 8, 64)
    radial = jnp.einsum("erx,ecxm->ecrm", interp_maps[:, 1], node_cube, precision=highest)
    paired = jnp.einsum("ety,eqz->etqyz", interp_maps[:, 0], interp_maps[:, 2]).reshape(
        elements, 64, 64
    )
    mapped = jnp.einsum("eam,ecrm->ecra", paired, radial, precision=highest)
    return mapped.reshape(elements, 5, 8, 8, 8).transpose(0, 1, 3, 2, 4).reshape(elements, 2560)


def per_device(state, velocity, interp_maps, neighbours, send_faces, owner_device, owner_block):
    elements = state.shape[0]
    deriv = jnp.asarray(spectral_derivative(), jnp.float32)
    flat_state = state.reshape(elements * 5, 512)
    first_section = flat_state + time_step * section_rate(
        flat_state, velocity, neighbours, send_faces, deriv
    )
    second = 0.5 * (
        flat_state
        + first_section
        + time_step * section_rate(first_section, velocity, neighbours, send_faces, deriv)
    )
    block_rows = interpolate(second, interp_maps)
    sector = owner_device[:, 0]
    sectors_count = lax.axis_size("az")
    capacity = max(2, 5 * elements // (2 * sectors_count))
    onehot_sector = (sector[:, None] == jnp.arange(sectors_count, dtype=jnp.int32)[None, :]).astype(
        jnp.int32
    )
    place_rank = jnp.sum(
        (jnp.cumsum(onehot_sector, axis=0) - onehot_sector) * onehot_sector, axis=1
    )
    slot_index = sector * capacity + place_rank
    picked = jnp.arange(sectors_count * capacity, dtype=jnp.int32)[:, None] == slot_index[None, :]
    packed = jnp.dot(
        picked.astype(jnp.float32),
        block_rows,
        precision=highest,
        preferred_element_type=jnp.float32,
    )
    labels = jnp.sum(jnp.where(picked, owner_block[None, :] + 1, 0), axis=1) - 1
    payload, markers = (
        lax.all_to_all(
            packed.reshape(sectors_count, capacity, 2560),
            "az",
            split_axis=0,
            concat_axis=0,
            tiled=True,
        ),
        lax.all_to_all(
            labels.reshape(sectors_count, capacity), "az", split_axis=0, concat_axis=0, tiled=True
        ),
    )
    matches = (jnp.arange(CB_DEV, dtype=jnp.int32)[:, None] == markers.reshape(1, -1)).astype(
        jnp.float32
    )
    cylinder = jnp.dot(
        matches, payload.reshape(-1, 2560), precision=highest, preferred_element_type=jnp.float32
    )
    sector_cube = (
        cylinder.reshape(TB, PB, 5, 8, 64).transpose(2, 1, 4, 0, 3).reshape(5, PB * 64, TB * 8)
    )
    cycle_data = lax.all_to_all(sector_cube, "az", split_axis=1, concat_axis=2, tiled=True)
    cycle_length = cycle_data.shape[2]
    angle_index = jnp.arange(cycle_length, dtype=jnp.int32)
    phase = angle_index[:, None] * angle_index[None, :] % cycle_length
    angle = phase.astype(jnp.float32) * (2.0 * math.pi / cycle_length)
    dft_table = jnp.concatenate([jnp.cos(angle), -jnp.sin(angle)], axis=1) * cycle_length ** (-0.5)
    coeffs = jnp.dot(
        cycle_data.reshape(-1, cycle_length),
        dft_table,
        precision=highest,
        preferred_element_type=jnp.float32,
    )
    spectrum = coeffs.reshape(5, -1, 2, cycle_length).transpose(2, 0, 1, 3)
    return (second.reshape(elements, 5, 512), spectrum)


def solution(mesh):
    return jax.shard_map(
        per_device,
        mesh=mesh,
        in_specs=(
            P(("az", "ax"), None, None),
            P(("az", "ax"), None),
            P(("az", "ax"), None, None, None),
            P(("az", "ax"), None),
            P(("az", "ax")),
            P(("az", "ax"), None),
            P(("az", "ax")),
        ),
        out_specs=(P(("az", "ax"), None, None), P(None, None, ("az", "ax"), None)),
        check_vma=False,
    )
```

profile of v0, /device:TPU:0, one launch (start us, length us, event | category | flops | bytes accessed | tf_op | source)
XLA Modules:
  0.0 216.5 jit_solution(16141313651623083034)
XLA Ops:
  3.7 7.3 %all-to-all-start = ((s32[8,1,15]{2,1,0:T(1,128)}), s32[8,1,15]{2,1,0:T(1,128)S(1)}, u32[]{:S(2)}, u32[]{:S(2)}) async-start(s32[8,1,15]{2,1,0:T(1,128)} %bitcast.54), calls=%async_computation | async-start | bytes 8192 | tf_op jit(solution)/shard_map/all_to_all | solution.py:123
  11.0 1.4 copy.167
  12.4 1.2 fusion.63
  13.6 2.3 %fusion.14 = f32[8,48,5,8,8]{1,0,4,3,2:T(8,128)} fusion(f32[8,8,1,1,1]{1,0,4,3,2:T(8,128)S(1)} %copy-done.9, f32[48,5,8,8,8]{0,4,3,2,1:T(8,128)S(1)} %bitcast.207), kind=kOutput, calls=%fused_computation.27 | convolution fusion | flops 11796480 | bytes 983296 | tf_op jit(solution)/shard_map/ja,eciak->ecijk/dot_general | solution.py:42
  20.3 2.7 %copy.155 = f32[48,6,5,64]{3,2,1,0:T(8,128)} copy(f32[48,6,5,64]{0,3,2,1:T(8,128)} %bitcast.17) | data formatting | bytes 737280 | tf_op jit(solution)/shard_map/transpose | solution.py:57
  23.0 1.5 reshape.656
  25.3 5.9 %all-gather = f32[192,320]{1,0:T(8,128)S(1)} all-gather(f32[48,320]{1,0:T(8,128)S(1)} %gather_fusion), channel_id=2, replica_groups=mesh['az'=8,'ax'=4] {'ax'}, dimensions={0}, use_global_device_ids=true | all-gather | bytes 307200 | tf_op jit(solution)/shard_map/all_gather | solution.py:59
  31.2 1.1 pad_maximum_fusion
  32.6 2.2 gather_fusion.1
  34.7 2.2 %reshape.658 = f32[48,6,5,64]{3,2,1,0:T(8,128)} reshape(f32[288,320]{1,0:T(8,128)} %gather_fusion.1) | data formatting | bytes 737280 | tf_op jit(solution)/shard_map/reshape | solution.py:61
  36.9 2.6 %copy.157 = f32[48,6,5,64]{0,3,2,1:T(8,128)} copy(f32[48,6,5,64]{3,2,1,0:T(8,128)} %reshape.658) | data formatting | bytes 737280 | tf_op jit(solution)/shard_map/reshape | solution.py:61
  39.5 1.6 fusion.23
  42.5 4.3 %fusion.7 = f32[48,5,8,8,8]{0,2,4,3,1:T(8,128)} fusion(f32[8,8,1,1,1]{1,0,4,3,2:T(8,128)S(1)} %copy-done.9, f32[8,48,5,8,8]{1,0,4,3,2:T(8,128)S(1)} %fusion.63, f32[8,48,5,8,8]{1,0,4,3,2:T(8,128)S(1)} %copy-done.5, f32[48,5,8,8,8]{0,4,3,2,1:T(8,128)S(1)} %bitcast.213, f32[48]{0:T(128)S(1)} %get-tuple-element.180, f32[48]{0:T(128)S(1)} %get-tuple-element.181, ...), kind=kOutput, calls=%fused_computation.15 | convolution fusion | flops 12533760 | bytes 1966912 | tf_op jit(solution)/shard_map/ia,ecajk->ecijk/dot_general | solution.py:41
  46.8 1.5 slice_add_fusion.11
  48.3 5.5 %scatter-add.40 = f32[48,5,8,8,8]{0,2,4,3,1:T(8,128)} dynamic-update-slice(f32[48,5,8,8,8]{0,2,4,3,1:T(8,128)} %fusion.7, f32[48,5,1,8,8]{0,2,4,3,1:T(1,128)S(1)} %slice_add_fusion.11, s32[]{:T(128)} %constant.309.clone.1, s32[]{:T(128)} %constant.309.clone.1, s32[]{:T(128)} %constant.309.clone.1, s32[]{:T(128)} %constant.309.clone.1, s32[]{:T(128)} %constant.309.clone.1) | dynamic-update-slice | bytes 122884 | tf_op jit(solution)/shard_map/scatter-add | solution.py:64
  53.9 1.6 slice_add_fusion.10
  55.5 5.5 %scatter-add.41 = f32[48,5,8,8,8]{0,2,4,3,1:T(8,128)} dynamic-update-slice(f32[48,5,8,8,8]{0,2,4,3,1:T(8,128)} %scatter-add.40, f32[48,5,1,8,8]{0,2,4,3,1:T(1,128)S(1)} %slice_add_fusion.10, s32[]{:T(128)} %constant.309.clone.1, s32[]{:T(128)} %constant.309.clone.1, s32[]{:T(128)} %constant.313.clone.1, s32[]{:T(128)} %constant.309.clone.1, s32[]{:T(128)} %constant.309.clone.1) | dynamic-update-slice | bytes 122884 | tf_op jit(solution)/shard_map/scatter-add | solution.py:65
  61.0 1.6 fusion.34
  62.7 1.6 fusion.33
  64.3 1.6 fusion.32
  65.9 1.6 fusion.31
  67.6 3.3 %broadcast_multiply_fusion.2 = (f32[48,5,8,8,8]{0,2,4,3,1:T(8,128)}, f32[48,5,8,8,8]{0,2,4,3,1:T(8,128)S(1)}) fusion(f32[48,5,8,8,8]{0,2,4,3,1:T(8,128)} %fusion.31, f32[48,5,8,8,8]{0,4,3,2,1:T(8,128)S(1)} %bitcast.214), kind=kLoop, calls=%fused_computation.46 | loop fusion | flops 245760 | bytes 1966080 | tf_op jit(solution)/shard_map/mul | solution.py:88
  70.8 2.4 %fusion.10 = f32[48,5,8,8,8]{0,4,3,2,1:T(8,128)} fusion(f32[8,8,1,1,1]{1,0,4,3,2:T(8,128)S(1)} %copy-done.9, f32[48,5,8,8,8]{0,2,4,3,1:T(8,128)S(1)} %get-tuple-element.155), kind=kOutput, calls=%fused_computation.20 | convolution fusion | flops 11796480 | bytes 983296 | tf_op jit(solution)/shard_map/ka,ecija->ecijk/dot_general | solution.py:43
  73.2 3.1 %fusion.12 = f32[48,5,8,8,8]{0,4,3,2,1:T(8,128)} fusion(f32[8,8,1,1,1]{1,0,4,3,2:T(8,128)S(1)} %copy-done.9, f32[48,5,8,8,8]{0,2,4,3,1:T(8,128)S(1)} %get-tuple-element.155), kind=kOutput, calls=%fused_computation.23 | convolution fusion | flops 11796480 | bytes 983296 | tf_op jit(solution)/shard_map/ja,eciak->ecijk/dot_general | solution.py:42
  78.0 1.2 reshape.671
  79.2 1.6 constant_dynamic-update-slice_fusion.3
  80.8 1.6 constant_dynamic-update-slice_fusion.2
  82.4 1.6 bitcast_dynamic-update-slice_fusion.3
  84.0 1.6 bitcast_dynamic-update-slice_fusion.2
  87.0 2.7 %copy.177 = f32[48,6,5,64]{3,2,1,0:T(8,128)} copy(f32[48,6,5,64]{0,3,2,1:T(8,128)} %bitcast.39) | data formatting | bytes 737280 | tf_op jit(solution)/shard_map/transpose | solution.py:57
  89.8 1.5 reshape.664
  92.0 6.0 %all-gather.1 = f32[192,320]{1,0:T(8,128)S(1)} all-gather(f32[48,320]{1,0:T(8,128)S(1)} %gather_fusion.2), channel_id=3, replica_groups=mesh['az'=8,'ax'=4] {'ax'}, dimensions={0}, use_global_device_ids=true | all-gather | bytes 307200 | tf_op jit(solution)/shard_map/all_gather | solution.py:59
  99.1 2.4 %gather_fusion.3 = f32[288,320]{1,0:T(8,128)} fusion(f32[480,320]{1,0:T(8,128)S(1)} %pad_maximum_fusion.1, s32[1024]{0:T(1024)S(1)} %pad_clamp_fusion), kind=kCustom, calls=%fused_computation.3 | custom fusion | bytes 738432 | tf_op jit(solution)/shard_map/gather | solution.py:61
  101.5 2.2 %reshape.665 = f32[48,6,5,64]{3,2,1,0:T(8,128)} reshape(f32[288,320]{1,0:T(8,128)} %gather_fusion.3) | data formatting | bytes 737280 | tf_op jit(solution)/shard_map/reshape | solution.py:61
  103.7 2.6 %copy.178 = f32[48,6,5,64]{0,3,2,1:T(8,128)} copy(f32[48,6,5,64]{3,2,1,0:T(8,128)} %reshape.665) | data formatting | bytes 737280 | tf_op jit(solution)/shard_map/reshape | solution.py:61
  106.3 1.7 fusion.21
  108.2 1.2 copy-done.3
  109.4 2.6 %fusion.3 = f32[48,5,8,8,8]{0,2,4,3,1:T(8,128)S(1)} fusion(f32[48,5,8,8,8]{0,2,4,3,1:T(8,128)S(1)} %get-tuple-element.155, f32[8,8,1,1,1]{1,0,4,3,2:T(8,128)S(1)} %copy-done.9, f32[48,5,8,8,8]{0,4,3,2,1:T(8,128)S(1)} %copy-done.3, f32[48,5,8,8,8]{0,4,3,2,1:T(8,128)S(1)} %copy-done.4, f32[48]{0:T(128)S(1)} %get-tuple-element.180, ...), kind=kOutput, calls=%fused_computation.10 | convolution fusion | flops 12533760 | bytes 1966912 | tf_op jit(solution)/shard_map/ia,ecajk->ecijk/dot_general | solution.py:41
  113.2 5.5 %scatter-add.50 = f32[48,5,8,8,8]{0,2,4,3,1:T(8,128)} dynamic-update-slice(f32[48,5,8,8,8]{0,2,4,3,1:T(8,128)} %copy-done.1, f32[48,5,1,8,8]{0,2,4,3,1:T(1,128)S(1)} %slice_add_fusion.5, s32[]{:T(128)} %constant.309.clone.1, s32[]{:T(128)} %constant.309.clone.1, s32[]{:T(128)} %constant.309.clone.1, s32[]{:T(128)} %constant.309.clone.1, s32[]{:T(128)} %constant.309.clone.1) | dynamic-update-slice | bytes 122884 | tf_op jit(solution)/shard_map/scatter-add | solution.py:64
  118.7 1.5 slice_add_fusion.4
  120.3 5.5 %scatter-add.51 = f32[48,5,8,8,8]{0,2,4,3,1:T(8,128)} dynamic-update-slice(f32[48,5,8,8,8]{0,2,4,3,1:T(8,128)} %scatter-add.50, f32[48,5,1,8,8]{0,2,4,3,1:T(1,128)S(1)} %slice_add_fusion.4, s32[]{:T(128)} %constant.309.clone.1, s32[]{:T(128)} %constant.309.clone.1, s32[]{:T(128)} %constant.313.clone.1, s32[]{:T(128)} %constant.309.clone.1, s32[]{:T(128)} %constant.309.clone.1) | dynamic-update-slice | bytes 122884 | tf_op jit(solution)/shard_map/scatter-add | solution.py:65
  125.8 1.6 fusion.30
  127.4 1.6 fusion.29
  129.1 1.6 fusion.28
  130.7 1.6 fusion.27
  132.3 2.6 %broadcast_multiply_fusion.1 = f32[48,5,8,8,8]{0,2,4,3,1:T(8,128)} fusion(f32[48,5,8,8,8]{0,2,4,3,1:T(8,128)} %fusion.27), kind=kLoop, calls=%fused_computation.45 | loop fusion | flops 122880 | bytes 983040 | tf_op jit(solution)/shard_map/mul | solution.py:94
  134.9 2.8 %copy.191 = f32[48,5,8,64]{3,2,1,0:T(8,128)} copy(f32[48,5,8,64]{0,2,3,1:T(8,128)} %bitcast.216) | data formatting | bytes 983040 | tf_op jit(solution)/shard_map/mul | solution.py:94
  137.7 1.4 copy.189
  139.3 1.6 broadcast_multiply_fusion
  140.9 3.4 %copy.207 = f32[48,64,64,1]{2,1,3,0:T(8,128)} copy(f32[48,64,64,1]{0,2,1,3:T(8,128)} %bitcast.217) | data formatting | bytes 1572864 | tf_op jit(solution)/shard_map/reshape | solution.py:77
  144.3 3.1 %convolution_bitcast_fusion = f32[48,5,8,64]{3,2,1,0:T(8,128)S(1)} fusion(f32[48,5,8,64]{3,2,1,0:T(8,128)} %copy.191, f32[48,5,8,64]{3,2,1,0:T(8,128)} %copy.189, f32[48,5,8,64]{3,2,0,1:T(8,128)} %reshape.671, f32[48,1,8,8]{3,2,0,1:T(8,128)S(1)} %copy.242), kind=kOutput, calls=%fused_computation.16 | convolution fusion | flops 12288000 | bytes 1978368 | tf_op jit(solution)/shard_map/erx,ecxm->ecrm/dot_general | solution.py:76
  147.4 3.5 %fusion.64 = f32[48,5,8,64]{3,2,1,0:T(8,128)} fusion(f32[48,5,8,64]{3,2,1,0:T(8,128)S(1)} %convolution_bitcast_fusion, f32[48,64,64,1]{2,1,3,0:T(8,128)S(1)} %copy-done.2), kind=kOutput, calls=%fused_computation.141 | convolution fusion | flops 94371840 | bytes 1769472 | tf_op jit(solution)/shard_map/eam,ecrm->ecra/dot_general | solution.py:80
  150.9 2.7 %copy.194 = f32[48,5,8,64]{0,3,2,1:T(8,128)} copy(f32[48,5,8,64]{3,2,1,0:T(8,128)} %fusion.64) | data formatting | bytes 983040 | tf_op jit(solution)/shard_map/eam,ecrm->ecra/dot_general | solution.py:80
  153.6 1.5 copy.195
  155.1 1.9 fusion.45
  157.1 6.0 %all-to-all-start.1 = ((f32[8,15,2560]{2,1,0:T(8,128)}), f32[8,15,2560]{2,1,0:T(8,128)}, u32[]{:S(2)}, u32[]{:S(2)}) async-start(f32[8,15,2560]{2,1,0:T(8,128)} %fusion.45), calls=%async_computation.1 | async-start | bytes 2621440 | tf_op jit(solution)/shard_map/all_to_all | solution.py:116
  163.1 1.6 copy.186
  166.4 28.7 %all-to-all-done.1 = f32[8,15,2560]{2,1,0:T(8,128)} async-done(((f32[8,15,2560]{2,1,0:T(8,128)}), f32[8,15,2560]{2,1,0:T(8,128)}, u32[]{:S(2)}, u32[]{:S(2)}) %all-to-all-start.1) | async-done | bytes 1228832 | tf_op jit(solution)/shard_map/all_to_all | solution.py:116
  195.1 2.5 %reshape.675 = f32[120,2560]{1,0:T(8,128)} reshape(f32[8,15,2560]{2,1,0:T(8,128)} %all-to-all-done.1) | data formatting | bytes 2457600 | tf_op jit(solution)/shard_map/reshape | solution.py:131
  197.6 1.7 copy.197
  199.3 1.6 convolution_bitcast_fusion.2
  202.5 3.6 %all-to-all-start.2 = ((f32[8,1,2560]{2,1,0:T(1,128)}), f32[8,1,2560]{2,1,0:T(1,128)S(1)}, u32[]{:S(2)}, u32[]{:S(2)}) async-start(f32[8,1,2560]{2,1,0:T(1,128)} %reshape.731), calls=%async_computation.2 | async-start | bytes 163840 | tf_op jit(solution)/shard_map/all_to_all | solution.py:136
  206.4 1.2 copy.203
  207.6 5.6 %all-to-all-done.2 = f32[8,1,2560]{2,1,0:T(1,128)S(1)} async-done(((f32[8,1,2560]{2,1,0:T(1,128)}), f32[8,1,2560]{2,1,0:T(1,128)S(1)}, u32[]{:S(2)}, u32[]{:S(2)}) %all-to-all-start.2) | async-done | bytes 81952 | tf_op jit(solution)/shard_map/all_to_all | solution.py:136
  (81 shorter events, 23.1 us)
Async XLA Ops:
  0.6 11.8 %copy-start.9 = (f32[8,8,1,1,1]{1,0,4,3,2:T(8,128)S(1)}, f32[8,8,1,1,1]{1,0,4,3,2:T(8,128)}, u32[]{:S(2)}) copy-start(f32[8,8,1,1,1]{1,0,4,3,2:T(8,128)} %constant.332) | copy-start | bytes 772
  3.7 153.3 %all-to-all-start = ((s32[8,1,15]{2,1,0:T(1,128)}), s32[8,1,15]{2,1,0:T(1,128)S(1)}, u32[]{:S(2)}, u32[]{:S(2)}) async-start(s32[8,1,15]{2,1,0:T(1,128)} %bitcast.54), calls=%async_computation | async-start | bytes 8192 | tf_op jit(solution)/shard_map/all_to_all | solution.py:123
  13.6 3.3 %copy-start.12 = (f32[48,3]{0,1:T(4,128)S(1)}, f32[48,3]{0,1:T(4,128)}, u32[]{:S(2)}) copy-start(f32[48,3]{0,1:T(4,128)} %param.33) | copy-start | bytes 1732
  23.0 1.5 copy-start.13
  24.5 0.8 copy-start.6
  24.5 7.8 %copy-start.11 = (s32[48,6]{0,1:T(8,128)S(1)}, s32[48,6]{0,1:T(8,128)}, u32[]{:S(2)}) copy-start(s32[48,6]{0,1:T(8,128)} %param.35) | copy-start | bytes 3460
  41.1 1.4 copy-start.5
  76.3 1.7 copy-start.8
  91.2 0.8 copy-start.7
  106.3 1.9 copy-start.4
  108.0 1.4 copy-start.3
  112.0 1.1 copy-start.1
  134.9 2.8 %copy-start = (f32[48,5,8,8,8]{0,2,4,3,1:T(8,128)S(1)}, f32[48,5,8,8,8]{0,2,4,3,1:T(8,128)}, u32[]{:S(2)}) copy-start(f32[48,5,8,8,8]{0,2,4,3,1:T(8,128)} %get-tuple-element.154) | copy-start | bytes 1474564
  137.7 1.4 copy-start.10
  144.3 3.1 %copy-start.2 = (f32[48,64,64,1]{2,1,3,0:T(8,128)S(1)}, f32[48,64,64,1]{2,1,3,0:T(8,128)}, u32[]{:S(2)}) copy-start(f32[48,64,64,1]{2,1,3,0:T(8,128)} %copy.207) | copy-start | bytes 2359300
  157.1 38.0 %all-to-all-start.1 = ((f32[8,15,2560]{2,1,0:T(8,128)}), f32[8,15,2560]{2,1,0:T(8,128)}, u32[]{:S(2)}, u32[]{:S(2)}) async-start(f32[8,15,2560]{2,1,0:T(8,128)} %fusion.45), calls=%async_computation.1 | async-start | bytes 2621440 | tf_op jit(solution)/shard_map/all_to_all | solution.py:116
  202.5 10.7 %all-to-all-start.2 = ((f32[8,1,2560]{2,1,0:T(1,128)}), f32[8,1,2560]{2,1,0:T(1,128)S(1)}, u32[]{:S(2)}, u32[]{:S(2)}) async-start(f32[8,1,2560]{2,1,0:T(1,128)} %reshape.731), calls=%async_computation.2 | async-start | bytes 163840 | tf_op jit(solution)/shard_map/all_to_all | solution.py:136
where the time goes:
time: 218 us; the launch traced here: 217 us
  local copies, waits for them, and re-layouts  90.2 us (41%)
  other arithmetic  35.4 us (16%)
  waiting for transfers between devices  34.2 us (16%)
  matrix products  26.8 us (12%)
  starting transfers between devices  16.9 us (8%)
  blocking collectives  12 us (6%)
    all_to_all x1, waiting for transfers between devices, per_device(): lax.all_to_all(packed.reshape(sectors_count, capacity, 2560), 'az', split...  28.7 us
    unnamed x45, local copies, waits for them, and re-layouts  18.4 us
    all_gather x2, blocking collectives, section_rate(): gathered = lax.all_gather(shared, 'ax', axis=0, tiled=True)  12 us
    scatter-add x2, local copies, waits for them, and re-layouts, section_rate(): result = result.at[:, :, 0].add(face_jump[:, :, 0])  11.1 us
    scatter-add x2, local copies, waits for them, and re-layouts, section_rate(): result = result.at[:, :, 7].add(face_jump[:, :, 1])  11.1 us
    reshape x4, local copies, waits for them, and re-layouts, section_rate(): tables[neighbours.reshape(-1)].reshape(elements, 6, 5, 64)  9.55 us
    all_to_all x1, starting transfers between devices, per_device(): lax.all_to_all(labels.reshape(sectors_count, capacity), 'az', split_axis=...  7.25 us
    dot_general x2, matrix products, section_rate(): along_x = jnp.einsum('ia,ecajk->ecijk', deriv, cube, precision=highest)  6.9 us
  transfers between devices with their start and end apart: 3, of which 2 were waited for; matrix products, arithmetic and copies ran while one was open for 63% of the time, Pallas kernels for 0%

commit v1 on v0

v1 whole, which is shorter than its diff:
```python
import functools
import math

import jax
import jax.numpy as jnp
import numpy as np
from jax import lax
from jax.experimental import pallas as pl
from jax.experimental.pallas import tpu as pltpu
from jax.sharding import PartitionSpec as P

TB = 2
PB = 4
FIELDS = 5
time_step = 0.02
penalty = 5.0
highest = lax.Precision.HIGHEST
f32 = jnp.float32
bf16 = jnp.bfloat16


def spectral_derivative():
    points = np.cos(np.pi * np.arange(8) / 7.0)
    ends = (np.arange(8) == 0) | (np.arange(8) == 7)
    scales = np.where(ends, 2.0, 1.0)
    signs = np.where(np.arange(8) % 2 == 0, 1.0, -1.0)
    differ = points[:, None] - points[None, :]
    offdiag = (
        scales[:, None]
        / scales[None, :]
        * signs[:, None]
        * signs[None, :]
        / np.where(np.eye(8) > 0, 1.0, differ)
    )
    inner = -points / (2.0 * np.where(ends, 1.0, 1.0 - points * points))
    corner = (2.0 * 49.0 + 1.0) / 6.0
    diagonal = np.where(np.arange(8) == 0, corner, np.where(np.arange(8) == 7, -corner, inner))
    return np.where(np.eye(8) > 0, diagonal[:, None], offdiag)


def np_split(table):
    table = np.asarray(table, np.float32)
    high = table.astype(jnp.bfloat16)
    low = (table - high.astype(np.float32)).astype(jnp.bfloat16)
    return high, low


def face_nodes():
    grid = np.arange(512).reshape(8, 8, 8)
    faces = [grid[0], grid[7], grid[:, 0], grid[:, 7], grid[:, :, 0], grid[:, :, 7]]
    return [square.reshape(-1) for square in faces]


def make_tables():
    deriv = spectral_derivative()
    along_x = np.kron(deriv, np.eye(64)).T
    in_tile_y = np.kron(np.eye(2), np.kron(deriv, np.eye(8))).T
    in_tile_z = np.kron(np.eye(16), deriv).T
    picks = face_nodes()
    nodes = np.arange(512)
    extract = np.concatenate(
        [nodes[:, None] == np.tile(square, 2)[None, :] for square in picks], axis=1
    ).astype(jnp.bfloat16)
    lift = np.concatenate(
        [square[:, None] == nodes[None, :] for square in picks], axis=0
    ).astype(jnp.bfloat16)
    count = lift.astype(np.float32).sum(axis=0)[None, :]
    x_high, x_low = np_split(along_x)
    yz_high, yz_low = np_split(np.concatenate([in_tile_y, in_tile_z], axis=1))
    return dict(
        x_high=x_high,
        x_low=x_low,
        yz_high=yz_high,
        yz_low=yz_low,
        extract=extract,
        lift=lift,
        count=count.astype(np.float32),
    )


def split(value):
    high = value.astype(bf16)
    return high, (value - high.astype(f32)).astype(bf16)


def dot(a, b):
    return jnp.dot(a, b, preferred_element_type=f32)


def low_half(shape):
    return lax.broadcasted_iota(jnp.int32, shape, len(shape) - 1) < 64


def local_key(elements):
    lane = lax.broadcasted_iota(jnp.int32, (1, 6 * elements), 1)
    face = jnp.zeros_like(lane)
    for f in range(1, 6):
        face = face + (lane >= f * elements).astype(jnp.int32)
    return 6 * (lane - face * elements) + face


def column(row_ref):
    return row_ref[...].astype(f32).T


def pick_rows(names, keys):
    return jnp.where(names == keys.astype(f32), 1.0, 0.0).astype(bf16)


def face_tables(fields, extract):
    elements = fields.shape[0] // FIELDS
    parts = []
    for part in split(fields):
        faces = dot(part, extract).astype(bf16)
        rows = [
            jnp.concatenate(
                [
                    faces[c * elements : (c + 1) * elements, f * 128 : (f + 1) * 128]
                    for c in range(FIELDS)
                ],
                axis=1,
            )
            for f in range(6)
        ]
        parts.append(jnp.concatenate(rows, axis=0))
    return parts


def share_rows(table_high, table_low, send_ref, out_ref):
    elements = send_ref.shape[1]
    picked = pick_rows(column(send_ref), local_key(elements))
    rows = dot(picked, table_high) + dot(picked, table_low)
    field = [rows[:, c * 128 : (c + 1) * 128] for c in range(FIELDS)]
    half = low_half((elements, 128))
    out_ref[0:elements, :] = jnp.where(half, field[0], field[1])
    out_ref[elements : 2 * elements, :] = jnp.where(half, field[2], field[3])
    middle = elements // 2
    out_ref[2 * elements :, :] = jnp.where(
        half[:middle], field[4][:middle], field[4][middle:]
    )


def unpack_rows(ref, elements):
    half = low_half((elements, 128))
    middle = elements // 2
    fields = []
    for first in range(2):
        both = ref[first * elements : (first + 1) * elements, :]
        turned = pltpu.roll(both, 64, 1)
        fields.append(jnp.where(half, both, turned))
        fields.append(jnp.where(half, turned, both))
    both = ref[2 * elements :, :]
    turned = pltpu.roll(both, 64, 1)
    fields.append(
        jnp.concatenate(
            [jnp.where(half[:middle], both, turned), jnp.where(half[:middle], turned, both)],
            axis=0,
        )
    )
    return jnp.concatenate(fields, axis=1)


def lift_rows(picked, tables, lift, elements):
    half = low_half((elements, 128))
    total = None
    for table in tables:
        facing = dot(picked, table)
        field_rows = []
        for c in range(FIELDS):
            blocks = [
                facing[f * elements : (f + 1) * elements, c * 128 : (c + 1) * 128]
                for f in range(6)
            ]
            pairs = [jnp.where(half, blocks[f], blocks[f + 1]) for f in range(0, 6, 2)]
            field_rows.append(jnp.concatenate(pairs, axis=1))
        part = dot(jnp.concatenate(field_rows, axis=0).astype(bf16), lift)
        total = part if total is None else total + part
    return total


def local_rate(fields, velocity_ref, neigh_ref, tables, x_high, x_low, yz_high, yz_low, lift, count):
    elements = neigh_ref.shape[1]
    high, low = split(fields)
    along_x = dot(high, x_high) + dot(low, x_high) + dot(high, x_low)
    speed = velocity_ref[...].T
    speeds = [
        jnp.concatenate(
            [jnp.broadcast_to(speed[:, d : d + 1], (elements, 128))] * FIELDS, axis=0
        )
        for d in range(3)
    ]
    tiles = []
    for j in range(4):
        lanes = slice(j * 128, (j + 1) * 128)
        both = dot(high[:, lanes], yz_high) + dot(low[:, lanes], yz_high) + dot(high[:, lanes], yz_low)
        tiles.append(
            speeds[0] * along_x[:, lanes] + speeds[1] * both[:, :128] + speeds[2] * both[:, 128:]
        )
    names = column(neigh_ref)
    keys = local_key(elements)
    picked = jnp.concatenate([pick_rows(names[:, f : f + 1], keys) for f in range(6)], axis=0)
    lifted = lift_rows(picked, tables, lift, elements)
    return penalty * (lifted - count * fields) - jnp.concatenate(tiles, axis=1)


def remote_terms(me, neigh_ref, shared_refs, lift):
    elements = neigh_ref.shape[1]
    names = column(neigh_ref)
    lane = lax.broadcasted_iota(jnp.int32, (1, elements), 1)
    keys = jnp.concatenate(
        [6 * elements + (me ^ m) * elements + lane for m in range(len(shared_refs))], axis=1
    )
    picked = jnp.concatenate([pick_rows(names[:, f : f + 1], keys) for f in range(6)], axis=0)
    table = jnp.concatenate([unpack_rows(ref, elements) for ref in shared_refs], axis=0)
    return lift_rows(picked, split(table), lift, elements)


def rows_of(ref):
    fields, elements, nodes = ref.shape
    return ref[...].reshape(fields * elements, nodes)


def share_kernel(state_ref, send_ref, extract_ref, high_ref, low_ref, shared_ref):
    high, low = face_tables(rows_of(state_ref), extract_ref[...])
    high_ref[...] = high
    low_ref[...] = low
    share_rows(high, low, send_ref, shared_ref)


def first_local_kernel(
    state_ref, velocity_ref, neigh_ref, high_ref, low_ref,
    x_high, x_low, yz_high, yz_low, lift, count, out_ref,
):
    fields = rows_of(state_ref)
    rate = local_rate(
        fields, velocity_ref, neigh_ref, (high_ref[...], low_ref[...]),
        x_high[...], x_low[...], yz_high[...], yz_low[...], lift[...], count[...],
    )
    out_ref[...] = (fields + time_step * rate).reshape(out_ref.shape)


def first_finish_kernel(base_ref, neigh_ref, send_ref, lift, extract, *refs):
    shared_refs, (first_ref, high_ref, low_ref, shared_ref) = refs[:-4], refs[-4:]
    me = lax.axis_index("ax")
    terms = remote_terms(me, neigh_ref, shared_refs, lift[...])
    first = rows_of(base_ref) + (time_step * penalty) * terms
    first_ref[...] = first.reshape(first_ref.shape)
    high, low = face_tables(first, extract[...])
    high_ref[...] = high
    low_ref[...] = low
    share_rows(high, low, send_ref, shared_ref)


def second_local_kernel(
    state_ref, first_ref, velocity_ref, neigh_ref, high_ref, low_ref,
    x_high, x_low, yz_high, yz_low, lift, count, out_ref,
):
    fields = rows_of(first_ref)
    rate = local_rate(
        fields, velocity_ref, neigh_ref, (high_ref[...], low_ref[...]),
        x_high[...], x_low[...], yz_high[...], yz_low[...], lift[...], count[...],
    )
    out_ref[...] = (0.5 * (rows_of(state_ref) + fields + time_step * rate)).reshape(out_ref.shape)


def maps_kernel(maps_ref, device_ref, block_ref, radial_ref, axial_ref, high_ref, low_ref):
    elements = maps_ref.shape[2]
    row = lax.broadcasted_iota(jnp.int32, (elements, 128), 0)
    lane = lax.broadcasted_iota(jnp.int32, (elements, 128), 1)
    twice = ((lane & 63) == row).astype(f32)
    radial_ref[...] = jnp.dot(maps_ref[1], twice, precision=highest, preferred_element_type=f32)
    axial = jnp.dot(maps_ref[2], twice, precision=highest, preferred_element_type=f32)
    row64 = lax.broadcasted_iota(jnp.int32, (64, 64), 0)
    lane64 = lax.broadcasted_iota(jnp.int32, (64, 64), 1)
    swap = ((row64 >> 3) + 8 * (row64 & 7) == lane64).astype(f32)
    axial_ref[...] = jnp.dot(swap, axial, precision=highest, preferred_element_type=f32)
    azimuthal = maps_ref[0].T
    row_t = lax.broadcasted_iota(jnp.int32, (64, 128), 0)
    lane_t = lax.broadcasted_iota(jnp.int32, (64, 128), 1)
    places = device_ref[...].astype(f32).T
    blocks = block_ref[...].astype(f32).T
    theta_lanes = high_ref.shape[1] // PB
    high_ref[...] = jnp.zeros_like(high_ref)
    low_ref[...] = jnp.zeros_like(low_ref)
    upper = (blocks >= PB).astype(f32)
    sector_key = places * TB + upper
    plane_key = blocks - PB * upper
    for y in range(8):
        tile_t = ((row_t >> 3) == (lane_t & 7)) & ((row_t & 7) == y)
        values = jnp.dot(
            azimuthal, tile_t.astype(f32), precision=highest, preferred_element_type=f32
        )
        value_high, value_low = split(values)
        rows = pl.ds((y // 2) * 128 + (y % 2) * 64, elements)
        for pb in range(PB):
            for tile in range(theta_lanes // 128):
                here = ((lane + tile * 128) >> 3).astype(f32)
                mine = (sector_key == here) & (plane_key == pb)
                lanes = pl.ds(pb * theta_lanes + tile * 128, 128)
                high_ref[rows, lanes] = jnp.where(mine, value_high.astype(f32), 0.0).astype(bf16)
                low_ref[rows, lanes] = jnp.where(mine, value_low.astype(f32), 0.0).astype(bf16)


def sample_kernel(base_ref, neigh_ref, lift, radial_ref, axial_ref, high_ref, low_ref, *refs):
    sectors = high_ref.shape[1] // (PB * TB * 8)
    shares = lax.axis_size("ax")
    shared_refs = refs[:shares]
    new_ref, out_refs = refs[shares], refs[shares + 1 : shares + 1 + sectors]
    turned_ref, mapped_ref, parts_ref = refs[shares + 1 + sectors :]
    elements = neigh_ref.shape[1]
    me = lax.axis_index("ax")
    terms = remote_terms(me, neigh_ref, shared_refs, lift[...])
    new_state = rows_of(base_ref) + (0.5 * time_step * penalty) * terms
    new_ref[...] = new_state.reshape(new_ref.shape)
    gap = jnp.zeros((64 - elements, 128), f32)
    for c in range(FIELDS):
        for j in range(4):
            part = new_state[c * elements : (c + 1) * elements, j * 128 : (j + 1) * 128]
            after = pltpu.roll(part, 120, 1)
            turned_ref[c, j] = jnp.concatenate([part, gap, after, gap], axis=0).T
    radial = radial_ref[...]
    axial = axial_ref[...]
    for c in range(FIELDS):
        for yy in range(4):
            inputs = []
            for x in range(8):
                start = (x % 2) * 64 + 16 * yy
                inputs.append(turned_ref[c, x // 2, start : start + 8, :])
            for r in range(8):
                mixed = radial[8 * r : 8 * r + 1, :] * inputs[0]
                for x in range(1, 8):
                    mixed = mixed + radial[8 * r + x : 8 * r + x + 1, :] * inputs[x]
                value = axial[0:8, :] * mixed[0:1, :]
                for z in range(1, 8):
                    value = value + axial[8 * z : 8 * z + 8, :] * mixed[z : z + 1, :]
                row = (c * 8 + r) * 8
                mapped_ref[row : row + 8, yy * 128 : (yy + 1) * 128] = value
    mapped_high, mapped_low = split(mapped_ref[...])
    theta_lanes = high_ref.shape[1] // PB
    groups = sectors // PB
    rows = 64 // groups
    for pb in range(PB):
        lanes = pl.ds(pb * theta_lanes, theta_lanes)
        weight_high = high_ref[:, lanes]
        total = (
            dot(mapped_high, weight_high)
            + dot(mapped_low, weight_high)
            + dot(mapped_high, low_ref[:, lanes])
        )
        for g in range(groups):
            for c in range(FIELDS):
                start = c * 64 + g * rows
                parts_ref[pb * groups + g, c * rows : (c + 1) * rows, :] = total[start : start + rows]
    owner = lax.axis_index("az")
    for m in range(sectors):
        out_refs[m][...] = parts_ref[owner ^ m]


def fourier_kernel(high_ref, low_ref, *refs):
    out_ref = refs[-1]
    total = refs[0][...]
    for ref in refs[1:-1]:
        total = total + ref[...]
    high, low = split(total)
    weight = high_ref[...]
    coeffs = dot(high, weight) + dot(low, weight) + dot(high, low_ref[...])
    width = total.shape[1]
    rows = total.shape[0] // FIELDS
    for k in range(2):
        for c in range(FIELDS):
            out_ref[k, c] = coeffs[c * rows : (c + 1) * rows, k * width : (k + 1) * width]


def shape(dims, dtype=f32):
    return jax.ShapeDtypeStruct(dims, dtype)


def call(kernel, outs, *args, scratch=(), flops=0):
    size = sum(math.prod(a.shape) * a.dtype.itemsize for a in list(args) + list(outs))
    return pl.pallas_call(
        kernel,
        out_shape=outs,
        scratch_shapes=list(scratch),
        cost_estimate=pl.CostEstimate(flops=flops, bytes_accessed=size, transcendentals=0),
        compiler_params=pltpu.CompilerParams(vmem_limit_bytes=48 * 1024 * 1024),
    )(*args)


def exchange(value, axis):
    size = lax.axis_size(axis)
    return [value] + [
        lax.ppermute(value, axis, [(i, i ^ m) for i in range(size)]) for m in range(size - 1, 0, -1)
    ][::-1]


def per_device(state, velocity, interp_maps, neighbours, send_faces, owner_device, owner_block):
    elements = state.shape[0]
    sectors = lax.axis_size("az")
    fields = state.transpose(1, 0, 2)
    speed = velocity.T
    names = neighbours.T
    maps = interp_maps.transpose(1, 2, 3, 0).reshape(3, 64, elements)
    sends = send_faces.reshape(1, elements)
    tables = {name: jnp.asarray(value) for name, value in make_tables().items()}
    rate_tables = [tables[k] for k in ("x_high", "x_low", "yz_high", "yz_low", "lift", "count")]
    cube = shape(fields.shape)
    face_rows = shape((6 * elements, FIELDS * 128), bf16)
    travel = shape((FIELDS * elements // 2, 128))
    high, low, shared = call(
        share_kernel, (face_rows, face_rows, travel), fields, sends, tables["extract"],
        flops=400_000_000,
    )
    others = exchange(shared, "ax")
    base = call(
        first_local_kernel, (cube,), fields, speed, names, high, low, *rate_tables,
        flops=1_000_000_000,
    )[0]
    first, high, low, shared = call(
        first_finish_kernel, (cube, face_rows, face_rows, travel),
        base, names, sends, tables["lift"], tables["extract"], *others,
        flops=600_000_000,
    )
    others = exchange(shared, "ax")
    base = call(
        second_local_kernel, (cube,), fields, first, speed, names, high, low, *rate_tables,
        flops=1_000_000_000,
    )[0]
    lanes = sectors * TB * 8
    weights = shape((512, PB * lanes), bf16)
    radial, axial, weight_high, weight_low = call(
        maps_kernel, (shape((64, 128)), shape((64, 128)), weights, weights),
        maps, owner_device.reshape(1, elements), owner_block.reshape(1, elements),
        flops=100_000_000,
    )
    rows = FIELDS * 64 * PB // sectors
    pieces = call(
        sample_kernel, (cube,) + (shape((rows, lanes)),) * sectors,
        base, names, tables["lift"], radial, axial, weight_high, weight_low, *others,
        scratch=(
            pltpu.VMEM((FIELDS, 4, 128, 128), f32),
            pltpu.VMEM((FIELDS * 64, 512), f32),
            pltpu.VMEM((sectors, rows, lanes), f32),
        ),
        flops=800_000_000,
    )
    new_state, pieces = pieces[0], pieces[1:]
    arrived = [pieces[0]] + [
        lax.ppermute(pieces[m], "az", [(i, i ^ m) for i in range(sectors)])
        for m in range(sectors - 1, 0, -1)
    ]
    angle = 2.0 * np.pi / lanes * (np.outer(np.arange(lanes), np.arange(lanes)) % lanes)
    table = np.concatenate([np.cos(angle), -np.sin(angle)], axis=1) * lanes**-0.5
    table_high, table_low = np_split(table)
    spectrum = call(
        fourier_kernel, (shape((2, FIELDS, rows // FIELDS, lanes)),),
        jnp.asarray(table_high), jnp.asarray(table_low), *arrived,
        flops=100_000_000,
    )[0]
    return new_state.transpose(1, 0, 2), spectrum


def solution(mesh):
    return jax.shard_map(
        per_device,
        mesh=mesh,
        in_specs=(
            P(("az", "ax"), None, None),
            P(("az", "ax"), None),
            P(("az", "ax"), None, None, None),
            P(("az", "ax"), None),
            P(("az", "ax")),
            P(("az", "ax"), None),
            P(("az", "ax")),
        ),
        out_specs=(P(("az", "ax"), None, None), P(None, None, ("az", "ax"), None)),
        check_vma=False,
    )
```

time: 218 us -> 44.9 us (0.21)
  local copies, waits for them, and re-layouts: 90.2 us -> 6.71 us
  other arithmetic: 35.4 us -> 0 us
  waiting for transfers between devices: 34.2 us -> 5.73 us
  matrix products: 26.8 us -> 0 us
  blocking collectives: 12 us -> 0 us
  Pallas kernels: 0 us -> 10.9 us
  starting transfers between devices: 16.9 us -> 20.3 us
    all_to_all x3 -> x0, waiting for transfers between devices: 34.2 us -> none  [the longest x1 28.7 us: per_device(): lax.all_to_all(packed.reshape(sectors_count, capacity, 2560), 'az', split...]
    dot_general x11 -> x0, matrix products: 26.8 us -> none  [the longest x2 6.9 us: section_rate(): along_x = jnp.einsum('ia,ecajk->ecijk', deriv, cube, precision=highest)]
    scatter-add x4 -> x0, local copies, waits for them, and re-layouts: 22.2 us -> none  [the longest x2 11.1 us: section_rate(): result = result.at[:, :, 0].add(face_jump[:, :, 0])]
    ppermute x0 -> x13, starting transfers between devices: none -> 20.3 us  [the longest x7 15 us: per_device(): lax.ppermute(pieces[m], 'az', [(i, i ^ m) for i in range(sectors)])]
    reshape x12 -> x0, local copies, waits for them, and re-layouts: 20.3 us -> none  [the longest x4 9.55 us: section_rate(): tables[neighbours.reshape(-1)].reshape(elements, 6, 5, 64)]
    all_to_all x3 -> x0, starting transfers between devices: 16.9 us -> none  [the longest x1 7.25 us: per_device(): lax.all_to_all(labels.reshape(sectors_count, capacity), 'az', split_axis=...]
    scatter-add x8 -> x0, other arithmetic: 13.1 us -> none  [the longest x2 3.3 us: section_rate(): result = result.at[:, :, :, :, 7].add(face_jump[:, :, 5])]
    all_gather x2 -> x0, blocking collectives: 12 us -> none  [section_rate(): gathered = lax.all_gather(shared, 'ax', axis=0, tiled=True)]
  transfers between devices with their start and end apart: 3 -> 13, of which waited for: 2 -> 4; matrix products, arithmetic and copies ran while one was open for 63% -> 0% of each run, Pallas kernels for 0% -> 9%
where the time goes in v1:
time: 44.9 us; the launch traced here: 44.5 us
  starting transfers between devices  20.3 us (45%)
  Pallas kernels  10.9 us (24%)
  local copies, waits for them, and re-layouts  6.71 us (15%)
  waiting for transfers between devices  5.73 us (13%)
  between operations  0.79 us (2%)
    ppermute x7, starting transfers between devices, per_device(): lax.ppermute(pieces[m], 'az', [(i, i ^ m) for i in range(sectors)])  15 us
    pallas_call x7, Pallas kernels, call(): pl.pallas_call(kernel, out_shape=outs, scratch_shapes=list(scratch), cost...  10.9 us
    unnamed x38, local copies, waits for them, and re-layouts  6.71 us
    ppermute x6, starting transfers between devices, exchange(): lax.ppermute(value, axis, [(i, i ^ m) for i in range(size)])  5.31 us
    ppermute x7, waiting for transfers between devices, per_device(): lax.ppermute(pieces[m], 'az', [(i, i ^ m) for i in range(sectors)])  3.86 us
    ppermute x6, waiting for transfers between devices, exchange(): lax.ppermute(value, axis, [(i, i ^ m) for i in range(size)])  1.87 us
  transfers between devices with their start and end apart: 13, of which 4 were waited for; matrix products, arithmetic and copies ran while one was open for 0% of the time, Pallas kernels for 9%

profile of v1, /device:TPU:0, one launch (start us, length us, event | category | flops | bytes accessed | tf_op | source)
XLA Modules:
  0.0 44.5 jit_solution(6703807251329211697)
XLA Ops:
  0.6 0.0 copy-start.16
  0.6 0.6 %copy-done.16 = s32[48]{0:T(128)S(1)} copy-done((s32[48]{0:T(128)S(1)}, s32[48]{0:T(128)}, u32[]{:S(2)}) %copy-start.16) | copy-done | bytes 216
  1.3 0.0 copy-start.2
  1.3 1.0 %copy-done.2 = f32[48,5,512]{2,0,1:T(8,128)S(1)} copy-done((f32[48,5,512]{2,0,1:T(8,128)S(1)}, f32[48,5,512]{2,0,1:T(8,128)}, u32[]{:S(2)}) %copy-start.2) | copy-done | bytes 491544
  2.3 0.0 copy-start.17
  2.3 1.1 %copy-done.17 = bf16[512,768]{1,0:T(8,128)(2,1)S(1)} copy-done((bf16[512,768]{1,0:T(8,128)(2,1)S(1)}, bf16[512,768]{1,0:T(8,128)(2,1)}, u32[]{:S(2)}) %copy-start.17) | copy-done | bytes 786456
  3.5 0.0 copy-start
  3.5 0.0 copy-start.1
  3.5 0.0 copy-start.3
  3.5 0.8 %shard_map.167 = (bf16[288,640]{1,0:T(8,128)(2,1)S(1)}, bf16[288,640]{1,0:T(8,128)(2,1)S(1)}, f32[120,128]{1,0:T(8,128)S(1)}) custom-call(f32[5,48,512]{2,1,0:T(8,128)S(1)} %bitcast.10, s32[1,48]{1,0:T(1,128)S(1)} %bitcast.22, bf16[512,768]{1,0:T(8,128)(2,1)S(1)} %copy-done.17), custom_call_target="tpu_custom_call" | custom-call | flops 400000000 | bytes 2076864 | tf_op jit(solution)/shard_map/pallas_call | solution.py:380
  4.2 2.5 %collective-permute-start.2 = (f32[120,128]{1,0:T(8,128)S(1)}, f32[120,128]{1,0:T(8,128)S(1)}, u32[]{:S(2)}, u32[]{:S(2)}) collective-permute-start(f32[120,128]{1,0:T(8,128)S(1)} %get-tuple-element.24.refs_0_), channel_id=1, source_target_pairs={{0,3},{1,2},{2,1},{3,0},{4,7},{5,6},{6,5},{7,4},{8,11},{9,10},{10,... | collective-permute-start | bytes 184328 | tf_op jit(solution)/shard_map/ppermute | solution.py:392
  6.7 0.6 %collective-permute-start.1 = (f32[120,128]{1,0:T(8,128)S(1)}, f32[120,128]{1,0:T(8,128)S(1)}, u32[]{:S(2)}, u32[]{:S(2)}) collective-permute-start(f32[120,128]{1,0:T(8,128)S(1)} %get-tuple-element.24.refs_0_), channel_id=1, source_target_pairs={{0,2},{1,3},{2,0},{3,1},{4,6},{5,7},{6,4},{7,5},{8,10},{9,11},{10,... | collective-permute-start | bytes 184328 | tf_op jit(solution)/shard_map/ppermute | solution.py:392
  7.4 0.0 collective-permute-start
  7.4 0.0 copy-start.13
  7.4 0.9 %copy-done.13 = f32[48,3,8,8]{0,3,2,1:T(8,128)S(1)} copy-done((f32[48,3,8,8]{0,3,2,1:T(8,128)S(1)}, f32[48,3,8,8]{0,3,2,1:T(8,128)}, u32[]{:S(2)}) %copy-start.13) | copy-done | bytes 36888
  8.3 0.0 copy-start.14
  8.3 0.7 %copy-done.14 = s32[48,1]{0,1:T(1,128)S(1)} copy-done((s32[48,1]{0,1:T(1,128)S(1)}, s32[48,1]{0,1:T(1,128)}, u32[]{:S(2)}) %copy-start.14) | copy-done | bytes 216
  8.9 0.0 copy-start.15
  9.0 0.7 %copy-done.15 = s32[48]{0:T(128)S(1)} copy-done((s32[48]{0:T(128)S(1)}, s32[48]{0:T(128)}, u32[]{:S(2)}) %copy-start.15) | copy-done | bytes 216
  9.6 0.0 copy-start.8
  9.6 0.6 %shard_map.171 = (f32[64,128]{1,0:T(8,128)S(1)}, f32[64,128]{1,0:T(8,128)S(1)}, bf16[512,512]{1,0:T(8,128)(2,1)S(1)}, bf16[512,512]{1,0:T(8,128)(2,1)S(1)}) custom-call(f32[3,64,48]{2,1,0:T(8,128)S(1)} %bitcast.19, s32[1,48]{1,0:T(1,128)S(1)} %bitcast.20, s32[1,48]{1,0:T(1,128)S(1)} %bitcast.21), custom_call_target="tpu_custom_call" | custom-call | flops 100000000 | bytes 1151360 | tf_op jit(solution)/shard_map/pallas_call | solution.py:380
  10.2 0.0 copy-start.10
  10.2 0.0 copy-start.11
  10.3 0.0 copy-done
  10.3 0.0 copy-done.1
  10.3 0.0 copy-done.3
  10.3 0.2 copy-done.8
  10.4 0.0 copy-done.9
  10.5 0.0 copy-done.12
  10.5 0.5 %copy-done.10 = s32[48,6]{0,1:T(8,128)S(1)} copy-done((s32[48,6]{0,1:T(8,128)S(1)}, s32[48,6]{0,1:T(8,128)}, u32[]{:S(2)}) %copy-start.10) | copy-done | bytes 1176
  10.9 0.0 copy-done.11
  11.0 1.0 %copy-done.4 = bf16[384,512]{1,0:T(8,128)(2,1)S(1)} copy-done((bf16[384,512]{1,0:T(8,128)(2,1)S(1)}, bf16[384,512]{1,0:T(8,128)(2,1)}, u32[]{:S(2)}) %copy-start.4) | copy-done | bytes 393240
  12.0 1.7 %shard_map.168.base_ref = f32[5,48,512]{2,1,0:T(8,128)S(1)} custom-call(f32[5,48,512]{2,1,0:T(8,128)S(1)} %bitcast.11, f32[3,48]{1,0:T(4,128)S(1)} %bitcast.17, s32[6,48]{1,0:T(8,128)S(1)} %bitcast.13, bf16[288,640]{1,0:T(8,128)(2,1)S(1)} %get-tuple-element.22.high_ref, bf16[288,640]{1,0:T(8,128)(2,1)S(1)} %get-tuple-element.23.low_ref, ...), custom_call_target="tpu_custom_call" | custom-call | flops 1000000000 | bytes 3296960 | tf_op jit(solution)/shard_map/pallas_call | solution.py:380
  13.7 0.0 collective-permute-done.2.refs_3_
  13.7 0.0 collective-permute-done.1.refs_2_
  13.7 0.0 collective-permute-done.refs_1_
  13.7 0.0 copy-done.5
  13.8 0.0 copy-done.18
  13.8 1.6 %shard_map.169 = (f32[5,48,512]{2,1,0:T(8,128)S(1)}, bf16[288,640]{1,0:T(8,128)(2,1)S(1)}, bf16[288,640]{1,0:T(8,128)(2,1)S(1)}, f32[120,128]{1,0:T(8,128)S(1)}) custom-call(f32[5,48,512]{2,1,0:T(8,128)S(1)} %shard_map.168.base_ref, s32[6,48]{1,0:T(8,128)S(1)} %bitcast.14, s32[1,48]{1,0:T(1,128)S(1)} %bitcast.23, bf16[384,512]{1,0:T(8,128)(2,1)S(1)} %copy-done.5, ...), custom_call_target="tpu_custom_call" | custom-call | flops 600000000 | bytes 3208512 | tf_op jit(solution)/shard_map/pallas_call | solution.py:380
  15.4 1.5 %collective-permute-start.5 = (f32[120,128]{1,0:T(8,128)S(1)}, f32[120,128]{1,0:T(8,128)S(1)}, u32[]{:S(2)}, u32[]{:S(2)}) collective-permute-start(f32[120,128]{1,0:T(8,128)S(1)} %get-tuple-element.32.refs_0_), channel_id=1, source_target_pairs={{0,3},{1,2},{2,1},{3,0},{4,7},{5,6},{6,5},{7,4},{8,11},{9,10},{10,... | collective-permute-start | bytes 184328 | tf_op jit(solution)/shard_map/ppermute | solution.py:392
  16.9 0.6 %collective-permute-start.4 = (f32[120,128]{1,0:T(8,128)S(1)}, f32[120,128]{1,0:T(8,128)S(1)}, u32[]{:S(2)}, u32[]{:S(2)}) collective-permute-start(f32[120,128]{1,0:T(8,128)S(1)} %get-tuple-element.32.refs_0_), channel_id=1, source_target_pairs={{0,2},{1,3},{2,0},{3,1},{4,6},{5,7},{6,4},{7,5},{8,10},{9,11},{10,... | collective-permute-start | bytes 184328 | tf_op jit(solution)/shard_map/ppermute | solution.py:392
  17.5 0.0 collective-permute-start.3
  17.5 1.8 %shard_map.170.base_ref = f32[5,48,512]{2,1,0:T(8,128)S(1)} custom-call(f32[5,48,512]{2,1,0:T(8,128)S(1)} %bitcast.12, f32[5,48,512]{2,1,0:T(8,128)S(1)} %get-tuple-element.25.first_ref, f32[3,48]{1,0:T(4,128)S(1)} %bitcast.18, s32[6,48]{1,0:T(8,128)S(1)} %bitcast.15, bf16[288,640]{1,0:T(8,128)(2,1)S(1)} %get-tuple-element.26.high_ref, ...), custom_call_target="tpu_custom_call" | custom-call | flops 1000000000 | bytes 3788480 | tf_op jit(solution)/shard_map/pallas_call | solution.py:380
  19.3 0.0 collective-permute-done.5.refs_3_
  19.3 1.9 %collective-permute-done.4.refs_2_ = f32[120,128]{1,0:T(8,128)S(1)} collective-permute-done((f32[120,128]{1,0:T(8,128)S(1)}, f32[120,128]{1,0:T(8,128)S(1)}, u32[]{:S(2)}, u32[]{:S(2)}) %collective-permute-start.4) | collective-permute-done | bytes 61472 | tf_op jit(solution)/shard_map/ppermute | solution.py:392
  21.2 0.0 collective-permute-done.3.refs_1_
  21.2 3.5 %shard_map.172 = (f32[5,48,512]{2,1,0:T(8,128)}, f32[160,128]{1,0:T(8,128)S(1)}, f32[160,128]{1,0:T(8,128)S(1)}, f32[160,128]{1,0:T(8,128)S(1)}, f32[160,128]{1,...) custom-call(f32[5,48,512]{2,1,0:T(8,128)S(1)} %shard_map.170.base_re, ...), custom_call_target="tpu_custom_call" | custom-call | flops 800000000 | bytes 3392640 | tf_op jit(solution)/shard_map/pallas_call | solution.py:380
  24.7 4.6 %collective-permute-start.6 = (f32[160,128]{1,0:T(8,128)S(1)}, f32[160,128]{1,0:T(8,128)S(1)}, u32[]{:S(2)}, u32[]{:S(2)}) collective-permute-start(f32[160,128]{1,0:T(8,128)S(1)} %get-tuple-element.35), channel_id=1, source_target_pairs={{0,28},{4,24},{8,20},{12,16},{16,12},{20,8},{24,4},{28,0},{1,29},{... | collective-permute-start | bytes 245768 | tf_op jit(solution)/shard_map/ppermute | solution.py:448
  29.3 0.2 collective-permute-start.7
  29.5 0.8 %collective-permute-start.8 = (f32[160,128]{1,0:T(8,128)S(1)}, f32[160,128]{1,0:T(8,128)S(1)}, u32[]{:S(2)}, u32[]{:S(2)}) collective-permute-start(f32[160,128]{1,0:T(8,128)S(1)} %get-tuple-element.37), channel_id=1, source_target_pairs={{0,20},{4,16},{8,28},{12,24},{16,4},{20,0},{24,12},{28,8},{1,21},{... | collective-permute-start | bytes 245768 | tf_op jit(solution)/shard_map/ppermute | solution.py:448
  30.3 2.1 %collective-permute-start.9 = (f32[160,128]{1,0:T(8,128)S(1)}, f32[160,128]{1,0:T(8,128)S(1)}, u32[]{:S(2)}, u32[]{:S(2)}) collective-permute-start(f32[160,128]{1,0:T(8,128)S(1)} %get-tuple-element.38), channel_id=1, source_target_pairs={{0,16},{4,20},{8,24},{12,28},{16,0},{20,4},{24,8},{28,12},{1,17},{... | collective-permute-start | bytes 245768 | tf_op jit(solution)/shard_map/ppermute | solution.py:448
  32.3 2.2 %collective-permute-start.10 = (f32[160,128]{1,0:T(8,128)S(1)}, f32[160,128]{1,0:T(8,128)S(1)}, u32[]{:S(2)}, u32[]{:S(2)}) collective-permute-start(f32[160,128]{1,0:T(8,128)S(1)} %get-tuple-element.39), channel_id=1, source_target_pairs={{0,12},{4,8},{8,4},{12,0},{16,28},{20,24},{24,20},{28,16},{1,13},{... | collective-permute-start | bytes 245768 | tf_op jit(solution)/shard_map/ppermute | solution.py:448
  34.6 0.0 collective-permute-done.6.refs_1_
  34.6 3.7 %collective-permute-start.11 = (f32[160,128]{1,0:T(8,128)S(1)}, f32[160,128]{1,0:T(8,128)S(1)}, u32[]{:S(2)}, u32[]{:S(2)}) collective-permute-start(f32[160,128]{1,0:T(8,128)S(1)} %get-tuple-element.40), channel_id=1, source_target_pairs={{0,8},{4,12},{8,0},{12,4},{16,24},{20,28},{24,16},{28,20},{1,9},{5... | collective-permute-start | bytes 245768 | tf_op jit(solution)/shard_map/ppermute | solution.py:448
  38.3 0.0 collective-permute-done.7.refs_2_
  38.3 1.5 %collective-permute-start.12 = (f32[160,128]{1,0:T(8,128)S(1)}, f32[160,128]{1,0:T(8,128)S(1)}, u32[]{:S(2)}, u32[]{:S(2)}) collective-permute-start(f32[160,128]{1,0:T(8,128)S(1)} %get-tuple-element.41), channel_id=1, source_target_pairs={{0,4},{4,0},{8,12},{12,8},{16,20},{20,16},{24,28},{28,24},{1,5},{5... | collective-permute-start | bytes 245768 | tf_op jit(solution)/shard_map/ppermute | solution.py:448
  39.7 2.4 %collective-permute-done.8.refs_3_ = f32[160,128]{1,0:T(8,128)S(1)} collective-permute-done((f32[160,128]{1,0:T(8,128)S(1)}, f32[160,128]{1,0:T(8,128)S(1)}, u32[]{:S(2)}, u32[]{:S(2)}) %collective-permute-start.8) | collective-permute-done | bytes 81952 | tf_op jit(solution)/shard_map/ppermute | solution.py:448
  42.2 0.9 %collective-permute-done.9.refs_4_ = f32[160,128]{1,0:T(8,128)S(1)} collective-permute-done((f32[160,128]{1,0:T(8,128)S(1)}, f32[160,128]{1,0:T(8,128)S(1)}, u32[]{:S(2)}, u32[]{:S(2)}) %collective-permute-start.9) | collective-permute-done | bytes 81952 | tf_op jit(solution)/shard_map/ppermute | solution.py:448
  43.1 0.0 collective-permute-done.10.refs_5_
  43.1 0.5 %collective-permute-done.11.refs_6_ = f32[160,128]{1,0:T(8,128)S(1)} collective-permute-done((f32[160,128]{1,0:T(8,128)S(1)}, f32[160,128]{1,0:T(8,128)S(1)}, u32[]{:S(2)}, u32[]{:S(2)}) %collective-permute-start.11) | collective-permute-done | bytes 81952 | tf_op jit(solution)/shard_map/ppermute | solution.py:448
  43.6 0.0 collective-permute-done.12.refs_7_
  43.6 0.0 copy-done.6
  43.6 0.0 copy-done.7
  43.6 0.9 %shard_map.173 = f32[2,5,32,128]{3,2,1,0:T(8,128)} custom-call(bf16[128,256]{1,0:T(8,128)(2,1)S(1)} %copy-done.7, bf16[128,256]{1,0:T(8,128)(2,1)S(1)} %copy-done.6, f32[160,128]{1,0:T(8,128)S(1)} %get-tuple-element.34.refs_0_, f32[160,128]{1,0:T(8,128)S(1)} %collective-permute-done.6.refs_1_, f32[160,128]{1,0:T(8,128)S(1)} %collective-permute-done.7.refs_2_, ...), custom_call_target="tpu_custom_call" | custom-call | flops 100000000 | bytes 950272 | tf_op jit(solution)/shard_map/pallas_call | solution.py:380
  (7 shorter events, 0.0 us)
Async XLA Ops:
  0.6 0.7 %copy-start.16 = (s32[48]{0:T(128)S(1)}, s32[48]{0:T(128)}, u32[]{:S(2)}) copy-start(s32[48]{0:T(128)} %param.20) | copy-start | bytes 580
  1.3 1.0 %copy-start.2 = (f32[48,5,512]{2,0,1:T(8,128)S(1)}, f32[48,5,512]{2,0,1:T(8,128)}, u32[]{:S(2)}) copy-start(f32[48,5,512]{2,0,1:T(8,128)} %param.16) | copy-start | bytes 1474564
  2.3 1.1 %copy-start.17 = (bf16[512,768]{1,0:T(8,128)(2,1)S(1)}, bf16[512,768]{1,0:T(8,128)(2,1)}, u32[]{:S(2)}) copy-start(bf16[512,768]{1,0:T(8,128)(2,1)} %constant.22.clone.extract_ref.extract) | copy-start | bytes 2359300
  3.5 6.8 %copy-start = (bf16[512,512]{1,0:T(8,128)(2,1)S(1)}, bf16[512,512]{1,0:T(8,128)(2,1)}, u32[]{:S(2)}) copy-start(bf16[512,512]{1,0:T(8,128)(2,1)} %constant.19.clone.x_low) | copy-start | bytes 1572868
  3.5 6.8 %copy-start.1 = (bf16[512,512]{1,0:T(8,128)(2,1)S(1)}, bf16[512,512]{1,0:T(8,128)(2,1)}, u32[]{:S(2)}) copy-start(bf16[512,512]{1,0:T(8,128)(2,1)} %constant.18.clone.x_high) | copy-start | bytes 1572868
  3.5 6.8 %copy-start.3 = (f32[48,5,512]{2,0,1:T(8,128)S(1)}, f32[48,5,512]{2,0,1:T(8,128)}, u32[]{:S(2)}) copy-start(f32[48,5,512]{2,0,1:T(8,128)} %param.16) | copy-start | bytes 1474564
  4.2 9.5 %collective-permute-start.2 = (f32[120,128]{1,0:T(8,128)S(1)}, f32[120,128]{1,0:T(8,128)S(1)}, u32[]{:S(2)}, u32[]{:S(2)}) collective-permute-start(f32[120,128]{1,0:T(8,128)S(1)} %get-tuple-element.24.refs_0_), channel_id=1, source_target_pairs={{0,3},{1,2},{2,1},{3,0},{4,7},{5,6},{6,5},{7,4},{8,11},{9,10},{10,... | collective-permute-start | bytes 184328 | tf_op jit(solution)/shard_map/ppermute | solution.py:392
  6.7 7.0 %collective-permute-start.1 = (f32[120,128]{1,0:T(8,128)S(1)}, f32[120,128]{1,0:T(8,128)S(1)}, u32[]{:S(2)}, u32[]{:S(2)}) collective-permute-start(f32[120,128]{1,0:T(8,128)S(1)} %get-tuple-element.24.refs_0_), channel_id=1, source_target_pairs={{0,2},{1,3},{2,0},{3,1},{4,6},{5,7},{6,4},{7,5},{8,10},{9,11},{10,... | collective-permute-start | bytes 184328 | tf_op jit(solution)/shard_map/ppermute | solution.py:392
  7.4 6.4 %collective-permute-start = (f32[120,128]{1,0:T(8,128)S(1)}, f32[120,128]{1,0:T(8,128)S(1)}, u32[]{:S(2)}, u32[]{:S(2)}) collective-permute-start(f32[120,128]{1,0:T(8,128)S(1)} %get-tuple-element.24.refs_0_), channel_id=1, source_target_pairs={{0,1},{1,0},{2,3},{3,2},{4,5},{5,4},{6,7},{7,6},{8,9},{9,8},{10,11... | collective-permute-start | bytes 184328 | tf_op jit(solution)/shard_map/ppermute | solution.py:392
  7.4 0.9 %copy-start.13 = (f32[48,3,8,8]{0,3,2,1:T(8,128)S(1)}, f32[48,3,8,8]{0,3,2,1:T(8,128)}, u32[]{:S(2)}) copy-start(f32[48,3,8,8]{0,3,2,1:T(8,128)} %param.18) | copy-start | bytes 110596
  8.3 0.7 %copy-start.14 = (s32[48,1]{0,1:T(1,128)S(1)}, s32[48,1]{0,1:T(1,128)}, u32[]{:S(2)}) copy-start(s32[48,1]{0,1:T(1,128)} %param.21) | copy-start | bytes 580
  8.9 0.7 %copy-start.15 = (s32[48]{0:T(128)S(1)}, s32[48]{0:T(128)}, u32[]{:S(2)}) copy-start(s32[48]{0:T(128)} %param.22) | copy-start | bytes 580
  9.6 0.8 %copy-start.8 = (bf16[128,256]{1,0:T(8,128)(2,1)S(1)}, bf16[128,256]{1,0:T(8,128)(2,1)}, u32[]{:S(2)}) copy-start(bf16[128,256]{1,0:T(8,128)(2,1)} %constant.21.clone.yz_low) | copy-start | bytes 196612
  9.6 0.9 %copy-start.9 = (bf16[128,256]{1,0:T(8,128)(2,1)S(1)}, bf16[128,256]{1,0:T(8,128)(2,1)}, u32[]{:S(2)}) copy-start(bf16[128,256]{1,0:T(8,128)(2,1)} %constant.20.clone.yz_high) | copy-start | bytes 196612
  9.6 0.9 %copy-start.12 = (f32[1,512]{1,0:T(1,128)S(1)}, f32[1,512]{1,0:T(1,128)}, u32[]{:S(2)}) copy-start(f32[1,512]{1,0:T(1,128)} %constant.24.clone.count) | copy-start | bytes 6148
  10.2 0.7 %copy-start.10 = (s32[48,6]{0,1:T(8,128)S(1)}, s32[48,6]{0,1:T(8,128)}, u32[]{:S(2)}) copy-start(s32[48,6]{0,1:T(8,128)} %param.19) | copy-start | bytes 3460
  10.2 0.7 %copy-start.11 = (f32[48,3]{0,1:T(4,128)S(1)}, f32[48,3]{0,1:T(4,128)}, u32[]{:S(2)}) copy-start(f32[48,3]{0,1:T(4,128)} %param.17) | copy-start | bytes 1732
  11.0 1.0 %copy-start.4 = (bf16[384,512]{1,0:T(8,128)(2,1)S(1)}, bf16[384,512]{1,0:T(8,128)(2,1)}, u32[]{:S(2)}) copy-start(bf16[384,512]{1,0:T(8,128)(2,1)} %constant.23.clone.lift) | copy-start | bytes 1179652
  12.0 1.8 %copy-start.5 = (bf16[384,512]{1,0:T(8,128)(2,1)S(1)}, bf16[384,512]{1,0:T(8,128)(2,1)}, u32[]{:S(2)}) copy-start(bf16[384,512]{1,0:T(8,128)(2,1)} %constant.23.clone.lift) | copy-start | bytes 1179652
  12.0 1.8 %copy-start.18 = (bf16[512,768]{1,0:T(8,128)(2,1)S(1)}, bf16[512,768]{1,0:T(8,128)(2,1)}, u32[]{:S(2)}) copy-start(bf16[512,768]{1,0:T(8,128)(2,1)} %constant.22.clone.extract_ref.extract) | copy-start | bytes 2359300
  15.4 3.9 %collective-permute-start.5 = (f32[120,128]{1,0:T(8,128)S(1)}, f32[120,128]{1,0:T(8,128)S(1)}, u32[]{:S(2)}, u32[]{:S(2)}) collective-permute-start(f32[120,128]{1,0:T(8,128)S(1)} %get-tuple-element.32.refs_0_), channel_id=1, source_target_pairs={{0,3},{1,2},{2,1},{3,0},{4,7},{5,6},{6,5},{7,4},{8,11},{9,10},{10,... | collective-permute-start | bytes 184328 | tf_op jit(solution)/shard_map/ppermute | solution.py:392
  16.9 4.3 %collective-permute-start.4 = (f32[120,128]{1,0:T(8,128)S(1)}, f32[120,128]{1,0:T(8,128)S(1)}, u32[]{:S(2)}, u32[]{:S(2)}) collective-permute-start(f32[120,128]{1,0:T(8,128)S(1)} %get-tuple-element.32.refs_0_), channel_id=1, source_target_pairs={{0,2},{1,3},{2,0},{3,1},{4,6},{5,7},{6,4},{7,5},{8,10},{9,11},{10,... | collective-permute-start | bytes 184328 | tf_op jit(solution)/shard_map/ppermute | solution.py:392
  17.5 3.7 %collective-permute-start.3 = (f32[120,128]{1,0:T(8,128)S(1)}, f32[120,128]{1,0:T(8,128)S(1)}, u32[]{:S(2)}, u32[]{:S(2)}) collective-permute-start(f32[120,128]{1,0:T(8,128)S(1)} %get-tuple-element.32.refs_0_), channel_id=1, source_target_pairs={{0,1},{1,0},{2,3},{3,2},{4,5},{5,4},{6,7},{7,6},{8,9},{9,8},{10,11... | collective-permute-start | bytes 184328 | tf_op jit(solution)/shard_map/ppermute | solution.py:392
  21.2 22.4 %copy-start.6 = (bf16[128,256]{1,0:T(8,128)(2,1)S(1)}, bf16[128,256]{1,0:T(8,128)(2,1)}, u32[]{:S(2)}) copy-start(bf16[128,256]{1,0:T(8,128)(2,1)} %constant.26.clone.low_ref) | copy-start | bytes 196612
  21.2 22.4 %copy-start.7 = (bf16[128,256]{1,0:T(8,128)(2,1)S(1)}, bf16[128,256]{1,0:T(8,128)(2,1)}, u32[]{:S(2)}) copy-start(bf16[128,256]{1,0:T(8,128)(2,1)} %constant.25.clone.high_ref) | copy-start | bytes 196612
  24.7 9.9 %collective-permute-start.6 = (f32[160,128]{1,0:T(8,128)S(1)}, f32[160,128]{1,0:T(8,128)S(1)}, u32[]{:S(2)}, u32[]{:S(2)}) collective-permute-start(f32[160,128]{1,0:T(8,128)S(1)} %get-tuple-element.35), channel_id=1, source_target_pairs={{0,28},{4,24},{8,20},{12,16},{16,12},{20,8},{24,4},{28,0},{1,29},{... | collective-permute-start | bytes 245768 | tf_op jit(solution)/shard_map/ppermute | solution.py:448
  29.3 9.0 %collective-permute-start.7 = (f32[160,128]{1,0:T(8,128)S(1)}, f32[160,128]{1,0:T(8,128)S(1)}, u32[]{:S(2)}, u32[]{:S(2)}) collective-permute-start(f32[160,128]{1,0:T(8,128)S(1)} %get-tuple-element.36), channel_id=1, source_target_pairs={{0,24},{4,28},{8,16},{12,20},{16,8},{20,12},{24,0},{28,4},{1,25},{... | collective-permute-start | bytes 245768 | tf_op jit(solution)/shard_map/ppermute | solution.py:448
  29.5 12.7 %collective-permute-start.8 = (f32[160,128]{1,0:T(8,128)S(1)}, f32[160,128]{1,0:T(8,128)S(1)}, u32[]{:S(2)}, u32[]{:S(2)}) collective-permute-start(f32[160,128]{1,0:T(8,128)S(1)} %get-tuple-element.37), channel_id=1, source_target_pairs={{0,20},{4,16},{8,28},{12,24},{16,4},{20,0},{24,12},{28,8},{1,21},{... | collective-permute-start | bytes 245768 | tf_op jit(solution)/shard_map/ppermute | solution.py:448
  30.3 12.8 %collective-permute-start.9 = (f32[160,128]{1,0:T(8,128)S(1)}, f32[160,128]{1,0:T(8,128)S(1)}, u32[]{:S(2)}, u32[]{:S(2)}) collective-permute-start(f32[160,128]{1,0:T(8,128)S(1)} %get-tuple-element.38), channel_id=1, source_target_pairs={{0,16},{4,20},{8,24},{12,28},{16,0},{20,4},{24,8},{28,12},{1,17},{... | collective-permute-start | bytes 245768 | tf_op jit(solution)/shard_map/ppermute | solution.py:448
  32.3 10.7 %collective-permute-start.10 = (f32[160,128]{1,0:T(8,128)S(1)}, f32[160,128]{1,0:T(8,128)S(1)}, u32[]{:S(2)}, u32[]{:S(2)}) collective-permute-start(f32[160,128]{1,0:T(8,128)S(1)} %get-tuple-element.39), channel_id=1, source_target_pairs={{0,12},{4,8},{8,4},{12,0},{16,28},{20,24},{24,20},{28,16},{1,13},{... | collective-permute-start | bytes 245768 | tf_op jit(solution)/shard_map/ppermute | solution.py:448
  34.6 9.0 %collective-permute-start.11 = (f32[160,128]{1,0:T(8,128)S(1)}, f32[160,128]{1,0:T(8,128)S(1)}, u32[]{:S(2)}, u32[]{:S(2)}) collective-permute-start(f32[160,128]{1,0:T(8,128)S(1)} %get-tuple-element.40), channel_id=1, source_target_pairs={{0,8},{4,12},{8,0},{12,4},{16,24},{20,28},{24,16},{28,20},{1,9},{5... | collective-permute-start | bytes 245768 | tf_op jit(solution)/shard_map/ppermute | solution.py:448
  38.3 5.3 %collective-permute-start.12 = (f32[160,128]{1,0:T(8,128)S(1)}, f32[160,128]{1,0:T(8,128)S(1)}, u32[]{:S(2)}, u32[]{:S(2)}) collective-permute-start(f32[160,128]{1,0:T(8,128)S(1)} %get-tuple-element.41), channel_id=1, source_target_pairs={{0,4},{4,0},{8,12},{12,8},{16,20},{20,16},{24,28},{28,24},{1,5},{5... | collective-permute-start | bytes 245768 | tf_op jit(solution)/shard_map/ppermute | solution.py:448

commit v2 on v1

--- a/solution.py
+++ b/solution.py
@@ -38,44 +38,32 @@
     return np.where(np.eye(8) > 0, diagonal[:, None], offdiag)
 
 
-def np_split(table):
-    table = np.asarray(table, np.float32)
-    high = table.astype(jnp.bfloat16)
-    low = (table - high.astype(np.float32)).astype(jnp.bfloat16)
-    return high, low
-
-
-def face_nodes():
-    grid = np.arange(512).reshape(8, 8, 8)
-    faces = [grid[0], grid[7], grid[:, 0], grid[:, 7], grid[:, :, 0], grid[:, :, 7]]
-    return [square.reshape(-1) for square in faces]
-
-
-def make_tables():
+def tile_tables():
     deriv = spectral_derivative()
-    along_x = np.kron(deriv, np.eye(64)).T
-    in_tile_y = np.kron(np.eye(2), np.kron(deriv, np.eye(8))).T
-    in_tile_z = np.kron(np.eye(16), deriv).T
-    picks = face_nodes()
-    nodes = np.arange(512)
-    extract = np.concatenate(
-        [nodes[:, None] == np.tile(square, 2)[None, :] for square in picks], axis=1
-    ).astype(jnp.bfloat16)
-    lift = np.concatenate(
-        [square[:, None] == nodes[None, :] for square in picks], axis=0
-    ).astype(jnp.bfloat16)
-    count = lift.astype(np.float32).sum(axis=0)[None, :]
-    x_high, x_low = np_split(along_x)
-    yz_high, yz_low = np_split(np.concatenate([in_tile_y, in_tile_z], axis=1))
-    return dict(
-        x_high=x_high,
-        x_low=x_low,
-        yz_high=yz_high,
-        yz_low=yz_low,
-        extract=extract,
-        lift=lift,
-        count=count.astype(np.float32),
-    )
+    along_y = np.kron(np.eye(2), np.kron(deriv, np.eye(8))).T
+    along_z = np.kron(np.eye(16), deriv).T
+    return np.concatenate([along_y, along_z], axis=1)
+
+
+def face_node(face, position):
+    first, second = position >> 3, position & 7
+    if face < 2:
+        return 448 * face + position
+    if face < 4:
+        return 56 * (face - 2) + 64 * first + second
+    return 7 * (face - 4) + 64 * first + 8 * second
+
+
+def iota(dims, axis):
+    return lax.broadcasted_iota(jnp.int32, dims, axis)
+
+
+def face_counts():
+    node = iota((1, 512), 1)
+    count = jnp.zeros((1, 512), f32)
+    for coordinate in (node >> 6, (node >> 3) & 7, node & 7):
+        count = count + jnp.where((coordinate == 0) | (coordinate == 7), 1.0, 0.0)
+    return count
 
 
 def split(value):
@@ -178,29 +166,53 @@
     return total
 
 
-def local_rate(fields, velocity_ref, neigh_ref, tables, x_high, x_low, yz_high, yz_low, lift, count):
+def x_derivative(fields):
+    deriv = spectral_derivative()
+    half = low_half((1, 128))
+    tiles = [fields[:, 128 * i : 128 * i + 128] for i in range(4)]
+    turned = [pltpu.roll(tile, 64, 1) for tile in tiles]
+    out = []
+    for j in range(4):
+        total = None
+        for i in range(4):
+            same = jnp.where(half, float(deriv[2 * j, 2 * i]), float(deriv[2 * j + 1, 2 * i + 1]))
+            cross = jnp.where(half, float(deriv[2 * j, 2 * i + 1]), float(deriv[2 * j + 1, 2 * i]))
+            part = same * tiles[i] + cross * turned[i]
+            total = part if total is None else total + part
+        out.append(total)
+    return out
+
+
+def local_rate(fields, velocity_ref, neigh_ref, tables, yz_high, yz_low, lift):
     elements = neigh_ref.shape[1]
     high, low = split(fields)
-    along_x = dot(high, x_high) + dot(low, x_high) + dot(high, x_low)
     speed = velocity_ref[...].T
-    speeds = [
-        jnp.concatenate(
-            [jnp.broadcast_to(speed[:, d : d + 1], (elements, 128))] * FIELDS, axis=0
-        )
-        for d in range(3)
-    ]
-    tiles = []
+    speeds = [jnp.broadcast_to(speed[:, d : d + 1], (elements, 128)) for d in range(3)]
+    both = []
     for j in range(4):
         lanes = slice(j * 128, (j + 1) * 128)
-        both = dot(high[:, lanes], yz_high) + dot(low[:, lanes], yz_high) + dot(high[:, lanes], yz_low)
-        tiles.append(
-            speeds[0] * along_x[:, lanes] + speeds[1] * both[:, :128] + speeds[2] * both[:, 128:]
+        both.append(
+            dot(high[:, lanes], yz_high) + dot(low[:, lanes], yz_high) + dot(high[:, lanes], yz_low)
         )
+    chunk = elements // 2
+    rows = []
+    for c in range(FIELDS):
+        for part in range(2):
+            begin = c * elements + part * chunk
+            along_x = x_derivative(fields[begin : begin + chunk])
+            here = [speed_rows[part * chunk : (part + 1) * chunk] for speed_rows in speeds]
+            tiles = [
+                here[0] * along_x[j]
+                + here[1] * both[j][begin : begin + chunk, :128]
+                + here[2] * both[j][begin : begin + chunk, 128:]
+                for j in range(4)
+            ]
+            rows.append(jnp.concatenate(tiles, axis=1))
     names = column(neigh_ref)
     keys = local_key(elements)
     picked = jnp.concatenate([pick_rows(names[:, f : f + 1], keys) for f in range(6)], axis=0)
     lifted = lift_rows(picked, tables, lift, elements)
-    return penalty * (lifted - count * fields) - jnp.concatenate(tiles, axis=1)
+    return penalty * (lifted - face_counts() * fields) - jnp.concatenate(rows, axis=0)
 
 
 def remote_terms(me, neigh_ref, shared_refs, lift):
@@ -220,21 +232,39 @@
     return ref[...].reshape(fields * elements, nodes)
 
 
-def share_kernel(state_ref, send_ref, extract_ref, high_ref, low_ref, shared_ref):
-    high, low = face_tables(rows_of(state_ref), extract_ref[...])
+def load_kernel(*refs):
+    count = 8
+    sources, loaded = refs[:count], refs[count : 2 * count]
+    extract_ref, lift_ref, high_ref, low_ref, shared_ref, sems = refs[2 * count :]
+    copies = [
+        pltpu.make_async_copy(source, target, sems.at[i])
+        for i, (source, target) in enumerate(zip(sources, loaded))
+    ]
+    for copy in copies:
+        copy.start()
+    row, lane = iota((512, 128), 0), iota((512, 128), 1)
+    for f in range(6):
+        here = row == face_node(f, lane & 63)
+        extract_ref[:, f * 128 : (f + 1) * 128] = jnp.where(here, 1.0, 0.0).astype(bf16)
+    row, lane = iota((64, 512), 0), iota((64, 512), 1)
+    for f in range(6):
+        here = face_node(f, row) == lane
+        lift_ref[f * 64 : (f + 1) * 64, :] = jnp.where(here, 1.0, 0.0).astype(bf16)
+    for copy in copies:
+        copy.wait()
+    high, low = face_tables(rows_of(loaded[0]), extract_ref[...])
     high_ref[...] = high
     low_ref[...] = low
-    share_rows(high, low, send_ref, shared_ref)
+    share_rows(high, low, loaded[1], shared_ref)
 
 
 def first_local_kernel(
-    state_ref, velocity_ref, neigh_ref, high_ref, low_ref,
-    x_high, x_low, yz_high, yz_low, lift, count, out_ref,
+    state_ref, velocity_ref, neigh_ref, high_ref, low_ref, yz, lift, out_ref
 ):
     fields = rows_of(state_ref)
     rate = local_rate(
         fields, velocity_ref, neigh_ref, (high_ref[...], low_ref[...]),
-        x_high[...], x_low[...], yz_high[...], yz_low[...], lift[...], count[...],
+        *split(yz[...]), lift[...],
     )
     out_ref[...] = (fields + time_step * rate).reshape(out_ref.shape)
 
@@ -252,13 +282,12 @@
 
 
 def second_local_kernel(
-    state_ref, first_ref, velocity_ref, neigh_ref, high_ref, low_ref,
-    x_high, x_low, yz_high, yz_low, lift, count, out_ref,
+    state_ref, first_ref, velocity_ref, neigh_ref, high_ref, low_ref, yz, lift, out_ref
 ):
     fields = rows_of(first_ref)
     rate = local_rate(
         fields, velocity_ref, neigh_ref, (high_ref[...], low_ref[...]),
-        x_high[...], x_low[...], yz_high[...], yz_low[...], lift[...], count[...],
+        *split(yz[...]), lift[...],
     )
     out_ref[...] = (0.5 * (rows_of(state_ref) + fields + time_step * rate)).reshape(out_ref.shape)
 
@@ -356,14 +385,14 @@
         out_refs[m][...] = parts_ref[owner ^ m]
 
 
-def fourier_kernel(high_ref, low_ref, *refs):
+def fourier_kernel(table_ref, *refs):
     out_ref = refs[-1]
     total = refs[0][...]
     for ref in refs[1:-1]:
         total = total + ref[...]
     high, low = split(total)
-    weight = high_ref[...]
-    coeffs = dot(high, weight) + dot(low, weight) + dot(high, low_ref[...])
+    weight, weight_low = split(table_ref[...])
+    coeffs = dot(high, weight) + dot(low, weight) + dot(high, weight_low)
     width = total.shape[1]
     rows = total.shape[0] // FIELDS
     for k in range(2):
@@ -371,15 +400,23 @@
             out_ref[k, c] = coeffs[c * rows : (c + 1) * rows, k * width : (k + 1) * width]
 
 
+def store_kernel(new_ref, out_ref, sem):
+    copy = pltpu.make_async_copy(new_ref, out_ref, sem)
+    copy.start()
+    copy.wait()
+
+
 def shape(dims, dtype=f32):
     return jax.ShapeDtypeStruct(dims, dtype)
 
 
-def call(kernel, outs, *args, scratch=(), flops=0):
+def call(kernel, outs, *args, scratch=(), flops=0, in_space=pltpu.VMEM, out_space=pltpu.VMEM):
     size = sum(math.prod(a.shape) * a.dtype.itemsize for a in list(args) + list(outs))
     return pl.pallas_call(
         kernel,
         out_shape=outs,
+        in_specs=[pl.BlockSpec(memory_space=in_space)] * len(args),
+        out_specs=tuple([pl.BlockSpec(memory_space=out_space)] * len(outs)),
         scratch_shapes=list(scratch),
         cost_estimate=pl.CostEstimate(flops=flops, bytes_accessed=size, transcendentals=0),
         compiler_params=pltpu.CompilerParams(vmem_limit_bytes=48 * 1024 * 1024),
@@ -396,46 +433,56 @@
 def per_device(state, velocity, interp_maps, neighbours, send_faces, owner_device, owner_block):
     elements = state.shape[0]
     sectors = lax.axis_size("az")
-    fields = state.transpose(1, 0, 2)
-    speed = velocity.T
-    names = neighbours.T
-    maps = interp_maps.transpose(1, 2, 3, 0).reshape(3, 64, elements)
-    sends = send_faces.reshape(1, elements)
-    tables = {name: jnp.asarray(value) for name, value in make_tables().items()}
-    rate_tables = [tables[k] for k in ("x_high", "x_low", "yz_high", "yz_low", "lift", "count")]
-    cube = shape(fields.shape)
+    inputs = (
+        state.transpose(1, 0, 2),
+        send_faces.reshape(1, elements),
+        velocity.T,
+        neighbours.T,
+        interp_maps.transpose(1, 2, 3, 0).reshape(3, 64, elements),
+        owner_device.reshape(1, elements),
+        owner_block.reshape(1, elements),
+    )
+    yz_table = jnp.asarray(tile_tables(), f32)
     face_rows = shape((6 * elements, FIELDS * 128), bf16)
     travel = shape((FIELDS * elements // 2, 128))
-    high, low, shared = call(
-        share_kernel, (face_rows, face_rows, travel), fields, sends, tables["extract"],
+    sources = inputs + (yz_table,)
+    sources = tuple(pltpu.with_memory_space_constraint(a, pltpu.HBM) for a in sources)
+    loaded = call(
+        load_kernel,
+        tuple(shape(a.shape, a.dtype) for a in sources)
+        + (shape((512, 768), bf16), shape((384, 512), bf16), face_rows, face_rows, travel),
+        *sources,
+        scratch=(pltpu.SemaphoreType.DMA((len(sources),)),),
         flops=400_000_000,
-    )
+        in_space=pltpu.HBM,
+    )
+    fields, sends, speed, names, maps, places, blocks, yz, extract, lift, high, low, shared = loaded
+    cube = shape(fields.shape)
     others = exchange(shared, "ax")
     base = call(
-        first_local_kernel, (cube,), fields, speed, names, high, low, *rate_tables,
-        flops=1_000_000_000,
-    )[0]
-    first, high, low, shared = call(
-        first_finish_kernel, (cube, face_rows, face_rows, travel),
-        base, names, sends, tables["lift"], tables["extract"], *others,
-        flops=600_000_000,
-    )
-    others = exchange(shared, "ax")
-    base = call(
-        second_local_kernel, (cube,), fields, first, speed, names, high, low, *rate_tables,
+        first_local_kernel, (cube,), fields, speed, names, high, low, yz, lift,
         flops=1_000_000_000,
     )[0]
     lanes = sectors * TB * 8
     weights = shape((512, PB * lanes), bf16)
     radial, axial, weight_high, weight_low = call(
-        maps_kernel, (shape((64, 128)), shape((64, 128)), weights, weights),
-        maps, owner_device.reshape(1, elements), owner_block.reshape(1, elements),
+        maps_kernel, (shape((64, 128)), shape((64, 128)), weights, weights), maps, places, blocks,
         flops=100_000_000,
     )
+    first, high, low, shared = call(
+        first_finish_kernel, (cube, face_rows, face_rows, travel),
+        base, names, sends, lift, extract, *others,
+        flops=600_000_000,
+    )
+    others = exchange(shared, "ax")
+    base = call(
+        second_local_kernel, (cube,), fields, first, speed, names, high, low, yz, lift,
+        flops=1_000_000_000,
+    )[0]
     rows = FIELDS * 64 * PB // sectors
     pieces = call(
         sample_kernel, (cube,) + (shape((rows, lanes)),) * sectors,
-        base, names, tables["lift"], radial, axial, weight_high, weight_low, *others,
+        base, names, lift, radial, axial, weight_high, weight_low, *others,
         scratch=(
             pltpu.VMEM((FIELDS, 4, 128, 128), f32),
             pltpu.VMEM((FIELDS * 64, 512), f32),
@@ -444,19 +491,21 @@
         flops=800_000_000,
     )
     new_state, pieces = pieces[0], pieces[1:]
+    stored = call(
+        store_kernel, (cube,), new_state, scratch=(pltpu.SemaphoreType.DMA,), out_space=pltpu.HBM
+    )[0]
     arrived = [pieces[0]] + [
         lax.ppermute(pieces[m], "az", [(i, i ^ m) for i in range(sectors)])
         for m in range(sectors - 1, 0, -1)
     ]
     angle = 2.0 * np.pi / lanes * (np.outer(np.arange(lanes), np.arange(lanes)) % lanes)
     table = np.concatenate([np.cos(angle), -np.sin(angle)], axis=1) * lanes**-0.5
-    table_high, table_low = np_split(table)
     spectrum = call(
         fourier_kernel, (shape((2, FIELDS, rows // FIELDS, lanes)),),
-        jnp.asarray(table_high), jnp.asarray(table_low), *arrived,
+        jnp.asarray(table, f32), *arrived,
         flops=100_000_000,
     )[0]
-    return new_state.transpose(1, 0, 2), spectrum
+    return stored.transpose(1, 0, 2), spectrum
 
 
 def solution(mesh):

time: 44.9 us -> 40.1 us (0.89)
  local copies, waits for them, and re-layouts: 6.71 us -> 0.01 us
  waiting for transfers between devices: 5.73 us -> 7.05 us
  Pallas kernels: 10.9 us -> 12 us
    unnamed x38 -> x2, local copies, waits for them, and re-layouts: 6.71 us -> 0.01 us
    ppermute x6, waiting for transfers between devices: 1.87 us -> 3.96 us  [exchange(): lax.ppermute(value, axis, [(i, i ^ m) for i in range(size)])]
    pallas_call x7 -> x8, Pallas kernels: 10.9 us -> 12 us  [call(): pl.pallas_call(kernel, out_shape=outs, in_specs=[pl.BlockSpec(memory_spac...]
    ppermute x7, waiting for transfers between devices: 3.86 us -> 3.09 us  [per_device(): lax.ppermute(pieces[m], 'az', [(i, i ^ m) for i in range(sectors)])]
  transfers between devices with their start and end apart: 13 -> 13, of which waited for: 4 -> 6; matrix products, arithmetic and copies ran while one was open for 0% -> 0% of each run, Pallas kernels for 9% -> 11%
where the time goes in v2:
time: 40.1 us; the launch traced here: 40 us
  starting transfers between devices  20.2 us (50%)
  Pallas kernels  12 us (30%)
  waiting for transfers between devices  7.05 us (18%)
  between operations  0.71 us (2%)
    ppermute x7, starting transfers between devices, per_device(): lax.ppermute(pieces[m], 'az', [(i, i ^ m) for i in range(sectors)])  15.1 us
    pallas_call x8, Pallas kernels, call(): pl.pallas_call(kernel, out_shape=outs, in_specs=[pl.BlockSpec(memory_spac...  12 us
    ppermute x6, starting transfers between devices, exchange(): lax.ppermute(value, axis, [(i, i ^ m) for i in range(size)])  5.08 us
    ppermute x6, waiting for transfers between devices, exchange(): lax.ppermute(value, axis, [(i, i ^ m) for i in range(size)])  3.96 us
    ppermute x7, waiting for transfers between devices, per_device(): lax.ppermute(pieces[m], 'az', [(i, i ^ m) for i in range(sectors)])  3.09 us
  transfers between devices with their start and end apart: 13, of which 6 were waited for; matrix products, arithmetic and copies ran while one was open for 0% of the time, Pallas kernels for 11%

profile of v2, /device:TPU:0, one launch (start us, length us, event | category | flops | bytes accessed | tf_op | source)
XLA Modules:
  0.0 40.0 jit_solution(14941660600754593212)
XLA Ops:
  0.6 2.1 %shard_map.104 = (f32[5,48,512]{2,1,0:T(8,128)S(1)}, s32[1,48]{1,0:T(1,128)S(1)}, f32[3,48]{1,0:T(4,128)S(1)}, s32[6,48]{1,0:T(8,128)S(1)}, f32[3,64,48]{2,1,0:T...) custom-call(f32[5,48,512]{2,1,0:T(8,128)} %bitcast.11, ...), custom_call_target="tpu_custom_call" | custom-call | flops 400000000 | bytes 3301888 | tf_op jit(solution)/shard_map/pallas_call | solution.py:415
  2.7 2.5 %collective-permute-start.2 = (f32[120,128]{1,0:T(8,128)S(1)}, f32[120,128]{1,0:T(8,128)S(1)}, u32[]{:S(2)}, u32[]{:S(2)}) collective-permute-start(f32[120,128]{1,0:T(8,128)S(1)} %get-tuple-element.41.refs_0_), channel_id=1, source_target_pairs={{0,3},{1,2},{2,1},{3,0},{4,7},{5,6},{6,5},{7,4},{8,11},{9,10},{10,... | collective-permute-start | bytes 184328 | tf_op jit(solution)/shard_map/ppermute | solution.py:429
  5.2 0.6 %collective-permute-start.1 = (f32[120,128]{1,0:T(8,128)S(1)}, f32[120,128]{1,0:T(8,128)S(1)}, u32[]{:S(2)}, u32[]{:S(2)}) collective-permute-start(f32[120,128]{1,0:T(8,128)S(1)} %get-tuple-element.41.refs_0_), channel_id=1, source_target_pairs={{0,2},{1,3},{2,0},{3,1},{4,6},{5,7},{6,4},{7,5},{8,10},{9,11},{10,... | collective-permute-start | bytes 184328 | tf_op jit(solution)/shard_map/ppermute | solution.py:429
  5.8 0.0 collective-permute-start
  5.8 0.6 %shard_map.108 = (f32[64,128]{1,0:T(8,128)S(1)}, f32[64,128]{1,0:T(8,128)S(1)}, bf16[512,512]{1,0:T(8,128)(2,1)S(1)}, bf16[512,512]{1,0:T(8,128)(2,1)S(1)}) custom-call(f32[3,64,48]{2,1,0:T(8,128)S(1)} %get-tuple-element.45.maps_ref, s32[1,48]{1,0:T(1,128)S(1)} %get-tuple-element.46.device_ref, s32[1,48]{1,0:T(1,128)S(1)} %get-tuple-element.47.block_ref), custom_call_target="tpu_custom_call" | custom-call | flops 100000000 | bytes 1151360 | tf_op jit(solution)/shard_map/pallas_call | solution.py:415
  6.5 1.6 %shard_map.105.base_ref = f32[5,48,512]{2,1,0:T(8,128)S(1)} custom-call(f32[5,48,512]{2,1,0:T(8,128)S(1)} %get-tuple-element.32.state_ref, f32[3,48]{1,0:T(4,128)S(1)} %get-tuple-element.33.velocity_ref, s32[6,48]{1,0:T(8,128)S(1)} %get-tuple-element.34.neigh_ref, bf16[288,640]{1,0:T(8,128)(2,1)S(1)} %get-tuple-element.35.high_ref, ...), custom_call_target="tpu_custom_call" | custom-call | flops 1000000000 | bytes 2246336 | tf_op jit(solution)/shard_map/pallas_call | solution.py:415
  8.0 0.0 collective-permute-done.2.refs_3_
  8.0 1.7 %collective-permute-done.1.refs_2_ = f32[120,128]{1,0:T(8,128)S(1)} collective-permute-done((f32[120,128]{1,0:T(8,128)S(1)}, f32[120,128]{1,0:T(8,128)S(1)}, u32[]{:S(2)}, u32[]{:S(2)}) %collective-permute-start.1) | collective-permute-done | bytes 61472 | tf_op jit(solution)/shard_map/ppermute | solution.py:429
  9.8 0.0 collective-permute-done.refs_1_
  9.8 1.6 %shard_map.106 = (f32[5,48,512]{2,1,0:T(8,128)S(1)}, bf16[288,640]{1,0:T(8,128)(2,1)S(1)}, bf16[288,640]{1,0:T(8,128)(2,1)S(1)}, f32[120,128]{1,0:T(8,128)S(1)}) custom-call(f32[5,48,512]{2,1,0:T(8,128)S(1)} %shard_map.105.base_ref, s32[6,48]{1,0:T(8,128)S(1)} %get-tuple-element.34.neigh_ref, s32[1,48]{1,0:T(1,128)S(1)} %get-tuple-element.39.send_ref, ...), custom_call_target="tpu_custom_call" | custom-call | flops 600000000 | bytes 3208512 | tf_op jit(solution)/shard_map/pallas_call | solution.py:415
  11.4 1.4 %collective-permute-start.5 = (f32[120,128]{1,0:T(8,128)S(1)}, f32[120,128]{1,0:T(8,128)S(1)}, u32[]{:S(2)}, u32[]{:S(2)}) collective-permute-start(f32[120,128]{1,0:T(8,128)S(1)} %get-tuple-element.52.refs_0_), channel_id=1, source_target_pairs={{0,3},{1,2},{2,1},{3,0},{4,7},{5,6},{6,5},{7,4},{8,11},{9,10},{10,... | collective-permute-start | bytes 184328 | tf_op jit(solution)/shard_map/ppermute | solution.py:429
  12.7 0.4 collective-permute-start.4
  13.1 0.2 collective-permute-start.3
  13.3 1.5 %shard_map.107.base_ref = f32[5,48,512]{2,1,0:T(8,128)S(1)} custom-call(f32[5,48,512]{2,1,0:T(8,128)S(1)} %get-tuple-element.32.state_ref, f32[5,48,512]{2,1,0:T(8,128)S(1)} %get-tuple-element.42.first_ref, f32[3,48]{1,0:T(4,128)S(1)} %get-tuple-element.33.velocity_ref, s32[6,48]{1,0:T(8,128)S(1)} %get-tuple-element.34.neigh_ref, ...), custom_call_target="tpu_custom_call" | custom-call | flops 1000000000 | bytes 2737856 | tf_op jit(solution)/shard_map/pallas_call | solution.py:415
  14.8 0.8 %collective-permute-done.5.refs_3_ = f32[120,128]{1,0:T(8,128)S(1)} collective-permute-done((f32[120,128]{1,0:T(8,128)S(1)}, f32[120,128]{1,0:T(8,128)S(1)}, u32[]{:S(2)}, u32[]{:S(2)}) %collective-permute-start.5) | collective-permute-done | bytes 61472 | tf_op jit(solution)/shard_map/ppermute | solution.py:429
  15.6 1.5 %collective-permute-done.4.refs_2_ = f32[120,128]{1,0:T(8,128)S(1)} collective-permute-done((f32[120,128]{1,0:T(8,128)S(1)}, f32[120,128]{1,0:T(8,128)S(1)}, u32[]{:S(2)}, u32[]{:S(2)}) %collective-permute-start.4) | collective-permute-done | bytes 61472 | tf_op jit(solution)/shard_map/ppermute | solution.py:429
  17.1 0.0 collective-permute-done.3.refs_1_
  17.1 3.0 %shard_map.109 = (f32[5,48,512]{2,1,0:T(8,128)S(1)}, f32[160,128]{1,0:T(8,128)S(1)}, f32[160,128]{1,0:T(8,128)S(1)}, f32[160,128]{1,0:T(8,128)S(1)}, f32[160,128...) custom-call(f32[5,48,512]{2,1,0:T(8,128)S(1)} %shard_map.107.base_re, ...), custom_call_target="tpu_custom_call" | custom-call | flops 800000000 | bytes 3392640 | tf_op jit(solution)/shard_map/pallas_call | solution.py:415
  20.1 4.7 %collective-permute-start.6 = (f32[160,128]{1,0:T(8,128)S(1)}, f32[160,128]{1,0:T(8,128)S(1)}, u32[]{:S(2)}, u32[]{:S(2)}) collective-permute-start(f32[160,128]{1,0:T(8,128)S(1)} %get-tuple-element.55), channel_id=1, source_target_pairs={{0,28},{4,24},{8,20},{12,16},{16,12},{20,8},{24,4},{28,0},{1,29},{... | collective-permute-start | bytes 245768 | tf_op jit(solution)/shard_map/ppermute | solution.py:498
  24.8 0.2 collective-permute-start.7
  25.0 0.8 %collective-permute-start.8 = (f32[160,128]{1,0:T(8,128)S(1)}, f32[160,128]{1,0:T(8,128)S(1)}, u32[]{:S(2)}, u32[]{:S(2)}) collective-permute-start(f32[160,128]{1,0:T(8,128)S(1)} %get-tuple-element.57), channel_id=1, source_target_pairs={{0,20},{4,16},{8,28},{12,24},{16,4},{20,0},{24,12},{28,8},{1,21},{... | collective-permute-start | bytes 245768 | tf_op jit(solution)/shard_map/ppermute | solution.py:498
  25.7 2.1 %collective-permute-start.9 = (f32[160,128]{1,0:T(8,128)S(1)}, f32[160,128]{1,0:T(8,128)S(1)}, u32[]{:S(2)}, u32[]{:S(2)}) collective-permute-start(f32[160,128]{1,0:T(8,128)S(1)} %get-tuple-element.58), channel_id=1, source_target_pairs={{0,16},{4,20},{8,24},{12,28},{16,0},{20,4},{24,8},{28,12},{1,17},{... | collective-permute-start | bytes 245768 | tf_op jit(solution)/shard_map/ppermute | solution.py:498
  27.8 2.2 %collective-permute-start.10 = (f32[160,128]{1,0:T(8,128)S(1)}, f32[160,128]{1,0:T(8,128)S(1)}, u32[]{:S(2)}, u32[]{:S(2)}) collective-permute-start(f32[160,128]{1,0:T(8,128)S(1)} %get-tuple-element.59), channel_id=1, source_target_pairs={{0,12},{4,8},{8,4},{12,0},{16,28},{20,24},{24,20},{28,16},{1,13},{... | collective-permute-start | bytes 245768 | tf_op jit(solution)/shard_map/ppermute | solution.py:498
  30.0 0.0 collective-permute-done.6.refs_1_
  30.1 3.7 %collective-permute-start.11 = (f32[160,128]{1,0:T(8,128)S(1)}, f32[160,128]{1,0:T(8,128)S(1)}, u32[]{:S(2)}, u32[]{:S(2)}) collective-permute-start(f32[160,128]{1,0:T(8,128)S(1)} %get-tuple-element.60), channel_id=1, source_target_pairs={{0,8},{4,12},{8,0},{12,4},{16,24},{20,28},{24,16},{28,20},{1,9},{5... | collective-permute-start | bytes 245768 | tf_op jit(solution)/shard_map/ppermute | solution.py:498
  33.8 0.0 collective-permute-done.7.refs_2_
  33.8 1.4 %collective-permute-start.12 = (f32[160,128]{1,0:T(8,128)S(1)}, f32[160,128]{1,0:T(8,128)S(1)}, u32[]{:S(2)}, u32[]{:S(2)}) collective-permute-start(f32[160,128]{1,0:T(8,128)S(1)} %get-tuple-element.61), channel_id=1, source_target_pairs={{0,4},{4,0},{8,12},{12,8},{16,20},{20,16},{24,28},{28,24},{1,5},{5... | collective-permute-start | bytes 245768 | tf_op jit(solution)/shard_map/ppermute | solution.py:498
  35.2 0.0 copy-start
  35.2 0.8 %shard_map.110 = f32[5,48,512]{2,1,0:T(8,128)} custom-call(f32[5,48,512]{2,1,0:T(8,128)S(1)} %get-tuple-element.53.new_ref), custom_call_target="tpu_custom_call" | custom-call | bytes 983040 | tf_op jit(solution)/shard_map/pallas_call | solution.py:415
  36.0 1.7 %collective-permute-done.8.refs_3_ = f32[160,128]{1,0:T(8,128)S(1)} collective-permute-done((f32[160,128]{1,0:T(8,128)S(1)}, f32[160,128]{1,0:T(8,128)S(1)}, u32[]{:S(2)}, u32[]{:S(2)}) %collective-permute-start.8) | collective-permute-done | bytes 81952 | tf_op jit(solution)/shard_map/ppermute | solution.py:498
  37.7 0.9 %collective-permute-done.9.refs_4_ = f32[160,128]{1,0:T(8,128)S(1)} collective-permute-done((f32[160,128]{1,0:T(8,128)S(1)}, f32[160,128]{1,0:T(8,128)S(1)}, u32[]{:S(2)}, u32[]{:S(2)}) %collective-permute-start.9) | collective-permute-done | bytes 81952 | tf_op jit(solution)/shard_map/ppermute | solution.py:498
  38.6 0.0 collective-permute-done.10.refs_5_
  38.6 0.5 %collective-permute-done.11.refs_6_ = f32[160,128]{1,0:T(8,128)S(1)} collective-permute-done((f32[160,128]{1,0:T(8,128)S(1)}, f32[160,128]{1,0:T(8,128)S(1)}, u32[]{:S(2)}, u32[]{:S(2)}) %collective-permute-start.11) | collective-permute-done | bytes 81952 | tf_op jit(solution)/shard_map/ppermute | solution.py:498
  39.1 0.0 collective-permute-done.12.refs_7_
  39.1 0.0 copy-done
  39.1 0.9 %shard_map.111 = f32[2,5,32,128]{3,2,1,0:T(8,128)} custom-call(f32[128,256]{1,0:T(8,128)S(1)} %copy-done, f32[160,128]{1,0:T(8,128)S(1)} %get-tuple-element.54.refs_0_, f32[160,128]{1,0:T(8,128)S(1)} %collective-permute-done.6.refs_1_, f32[160,128]{1,0:T(8,128)S(1)} %collective-permute-done.7.refs_2_, f32[160,128]{1,0:T(8,128)S(1)} %collective-permute-done.8.refs_3_, ...), custom_call_target="tpu_custom_call" | custom-call | flops 100000000 | bytes 950272 | tf_op jit(solution)/shard_map/pallas_call | solution.py:415
Async XLA Ops:
  2.7 5.3 %collective-permute-start.2 = (f32[120,128]{1,0:T(8,128)S(1)}, f32[120,128]{1,0:T(8,128)S(1)}, u32[]{:S(2)}, u32[]{:S(2)}) collective-permute-start(f32[120,128]{1,0:T(8,128)S(1)} %get-tuple-element.41.refs_0_), channel_id=1, source_target_pairs={{0,3},{1,2},{2,1},{3,0},{4,7},{5,6},{6,5},{7,4},{8,11},{9,10},{10,... | collective-permute-start | bytes 184328 | tf_op jit(solution)/shard_map/ppermute | solution.py:429
  5.2 4.6 %collective-permute-start.1 = (f32[120,128]{1,0:T(8,128)S(1)}, f32[120,128]{1,0:T(8,128)S(1)}, u32[]{:S(2)}, u32[]{:S(2)}) collective-permute-start(f32[120,128]{1,0:T(8,128)S(1)} %get-tuple-element.41.refs_0_), channel_id=1, source_target_pairs={{0,2},{1,3},{2,0},{3,1},{4,6},{5,7},{6,4},{7,5},{8,10},{9,11},{10,... | collective-permute-start | bytes 184328 | tf_op jit(solution)/shard_map/ppermute | solution.py:429
  5.8 3.9 %collective-permute-start = (f32[120,128]{1,0:T(8,128)S(1)}, f32[120,128]{1,0:T(8,128)S(1)}, u32[]{:S(2)}, u32[]{:S(2)}) collective-permute-start(f32[120,128]{1,0:T(8,128)S(1)} %get-tuple-element.41.refs_0_), channel_id=1, source_target_pairs={{0,1},{1,0},{2,3},{3,2},{4,5},{5,4},{6,7},{7,6},{8,9},{9,8},{10,11... | collective-permute-start | bytes 184328 | tf_op jit(solution)/shard_map/ppermute | solution.py:429
  11.4 4.2 %collective-permute-start.5 = (f32[120,128]{1,0:T(8,128)S(1)}, f32[120,128]{1,0:T(8,128)S(1)}, u32[]{:S(2)}, u32[]{:S(2)}) collective-permute-start(f32[120,128]{1,0:T(8,128)S(1)} %get-tuple-element.52.refs_0_), channel_id=1, source_target_pairs={{0,3},{1,2},{2,1},{3,0},{4,7},{5,6},{6,5},{7,4},{8,11},{9,10},{10,... | collective-permute-start | bytes 184328 | tf_op jit(solution)/shard_map/ppermute | solution.py:429
  12.7 4.3 %collective-permute-start.4 = (f32[120,128]{1,0:T(8,128)S(1)}, f32[120,128]{1,0:T(8,128)S(1)}, u32[]{:S(2)}, u32[]{:S(2)}) collective-permute-start(f32[120,128]{1,0:T(8,128)S(1)} %get-tuple-element.52.refs_0_), channel_id=1, source_target_pairs={{0,2},{1,3},{2,0},{3,1},{4,6},{5,7},{6,4},{7,5},{8,10},{9,11},{10,... | collective-permute-start | bytes 184328 | tf_op jit(solution)/shard_map/ppermute | solution.py:429
  13.1 4.0 %collective-permute-start.3 = (f32[120,128]{1,0:T(8,128)S(1)}, f32[120,128]{1,0:T(8,128)S(1)}, u32[]{:S(2)}, u32[]{:S(2)}) collective-permute-start(f32[120,128]{1,0:T(8,128)S(1)} %get-tuple-element.52.refs_0_), channel_id=1, source_target_pairs={{0,1},{1,0},{2,3},{3,2},{4,5},{5,4},{6,7},{7,6},{8,9},{9,8},{10,11... | collective-permute-start | bytes 184328 | tf_op jit(solution)/shard_map/ppermute | solution.py:429
  20.1 10.0 %collective-permute-start.6 = (f32[160,128]{1,0:T(8,128)S(1)}, f32[160,128]{1,0:T(8,128)S(1)}, u32[]{:S(2)}, u32[]{:S(2)}) collective-permute-start(f32[160,128]{1,0:T(8,128)S(1)} %get-tuple-element.55), channel_id=1, source_target_pairs={{0,28},{4,24},{8,20},{12,16},{16,12},{20,8},{24,4},{28,0},{1,29},{... | collective-permute-start | bytes 245768 | tf_op jit(solution)/shard_map/ppermute | solution.py:498
  24.8 9.0 %collective-permute-start.7 = (f32[160,128]{1,0:T(8,128)S(1)}, f32[160,128]{1,0:T(8,128)S(1)}, u32[]{:S(2)}, u32[]{:S(2)}) collective-permute-start(f32[160,128]{1,0:T(8,128)S(1)} %get-tuple-element.56), channel_id=1, source_target_pairs={{0,24},{4,28},{8,16},{12,20},{16,8},{20,12},{24,0},{28,4},{1,25},{... | collective-permute-start | bytes 245768 | tf_op jit(solution)/shard_map/ppermute | solution.py:498
  25.0 12.7 %collective-permute-start.8 = (f32[160,128]{1,0:T(8,128)S(1)}, f32[160,128]{1,0:T(8,128)S(1)}, u32[]{:S(2)}, u32[]{:S(2)}) collective-permute-start(f32[160,128]{1,0:T(8,128)S(1)} %get-tuple-element.57), channel_id=1, source_target_pairs={{0,20},{4,16},{8,28},{12,24},{16,4},{20,0},{24,12},{28,8},{1,21},{... | collective-permute-start | bytes 245768 | tf_op jit(solution)/shard_map/ppermute | solution.py:498
  25.7 12.9 %collective-permute-start.9 = (f32[160,128]{1,0:T(8,128)S(1)}, f32[160,128]{1,0:T(8,128)S(1)}, u32[]{:S(2)}, u32[]{:S(2)}) collective-permute-start(f32[160,128]{1,0:T(8,128)S(1)} %get-tuple-element.58), channel_id=1, source_target_pairs={{0,16},{4,20},{8,24},{12,28},{16,0},{20,4},{24,8},{28,12},{1,17},{... | collective-permute-start | bytes 245768 | tf_op jit(solution)/shard_map/ppermute | solution.py:498
  27.8 10.8 %collective-permute-start.10 = (f32[160,128]{1,0:T(8,128)S(1)}, f32[160,128]{1,0:T(8,128)S(1)}, u32[]{:S(2)}, u32[]{:S(2)}) collective-permute-start(f32[160,128]{1,0:T(8,128)S(1)} %get-tuple-element.59), channel_id=1, source_target_pairs={{0,12},{4,8},{8,4},{12,0},{16,28},{20,24},{24,20},{28,16},{1,13},{... | collective-permute-start | bytes 245768 | tf_op jit(solution)/shard_map/ppermute | solution.py:498
  30.1 9.0 %collective-permute-start.11 = (f32[160,128]{1,0:T(8,128)S(1)}, f32[160,128]{1,0:T(8,128)S(1)}, u32[]{:S(2)}, u32[]{:S(2)}) collective-permute-start(f32[160,128]{1,0:T(8,128)S(1)} %get-tuple-element.60), channel_id=1, source_target_pairs={{0,8},{4,12},{8,0},{12,4},{16,24},{20,28},{24,16},{28,20},{1,9},{5... | collective-permute-start | bytes 245768 | tf_op jit(solution)/shard_map/ppermute | solution.py:498
  33.8 5.3 %collective-permute-start.12 = (f32[160,128]{1,0:T(8,128)S(1)}, f32[160,128]{1,0:T(8,128)S(1)}, u32[]{:S(2)}, u32[]{:S(2)}) collective-permute-start(f32[160,128]{1,0:T(8,128)S(1)} %get-tuple-element.61), channel_id=1, source_target_pairs={{0,4},{4,0},{8,12},{12,8},{16,20},{20,16},{24,28},{28,24},{1,5},{5... | collective-permute-start | bytes 245768 | tf_op jit(solution)/shard_map/ppermute | solution.py:498
  35.2 3.9 %copy-start = (f32[128,256]{1,0:T(8,128)S(1)}, f32[128,256]{1,0:T(8,128)}, u32[]{:S(2)}) copy-start(f32[128,256]{1,0:T(8,128)} %constant.5.clone.table_ref) | copy-start | bytes 393220

commit v3 on v2

--- a/solution.py
+++ b/solution.py
@@ -95,35 +95,31 @@
     return jnp.where(names == keys.astype(f32), 1.0, 0.0).astype(bf16)
 
 
-def face_tables(fields, extract):
+def face_table(fields, extract):
     elements = fields.shape[0] // FIELDS
-    parts = []
-    for part in split(fields):
-        faces = dot(part, extract).astype(bf16)
-        rows = [
-            jnp.concatenate(
-                [
-                    faces[c * elements : (c + 1) * elements, f * 128 : (f + 1) * 128]
-                    for c in range(FIELDS)
-                ],
-                axis=1,
-            )
-            for f in range(6)
-        ]
-        parts.append(jnp.concatenate(rows, axis=0))
-    return parts
-
-
-def share_rows(table_high, table_low, send_ref, out_ref):
-    elements = send_ref.shape[1]
-    picked = pick_rows(column(send_ref), local_key(elements))
-    rows = dot(picked, table_high) + dot(picked, table_low)
+    faces = dot(fields.astype(bf16), extract).astype(bf16)
+    rows = [
+        jnp.concatenate(
+            [
+                faces[c * elements : (c + 1) * elements, f * 128 : (f + 1) * 128]
+                for c in range(FIELDS)
+            ],
+            axis=1,
+        )
+        for f in range(6)
+    ]
+    return jnp.concatenate(rows, axis=0)
+
+
+def share_rows(table, picked, out_ref):
+    elements = picked.shape[0]
+    rows = dot(picked, table)
     field = [rows[:, c * 128 : (c + 1) * 128] for c in range(FIELDS)]
     half = low_half((elements, 128))
     out_ref[0:elements, :] = jnp.where(half, field[0], field[1])
     out_ref[elements : 2 * elements, :] = jnp.where(half, field[2], field[3])
     middle = elements // 2
-    out_ref[2 * elements :, :] = jnp.where(
+    out_ref[2 * elements : 2 * elements + middle, :] = jnp.where(
         half[:middle], field[4][:middle], field[4][middle:]
     )
 
@@ -137,7 +133,7 @@
         turned = pltpu.roll(both, 64, 1)
         fields.append(jnp.where(half, both, turned))
         fields.append(jnp.where(half, turned, both))
-    both = ref[2 * elements :, :]
+    both = ref[2 * elements : 2 * elements + middle, :]
     turned = pltpu.roll(both, 64, 1)
     fields.append(
         jnp.concatenate(
@@ -148,22 +144,35 @@
     return jnp.concatenate(fields, axis=1)
 
 
-def lift_rows(picked, tables, lift, elements):
+def share_names(names_ref, picked, out_ref):
+    elements = picked.shape[0]
+    lane = iota((1, 6 * elements), 1)
+    face = jnp.zeros_like(lane)
+    for f in range(1, 6):
+        face = face + (lane >= f * elements).astype(jnp.int32)
+    tile = (iota((elements, 6 * elements), 0) == lane - face * elements).astype(f32)
+    names = jnp.dot(
+        names_ref[...].astype(f32), tile, precision=highest, preferred_element_type=f32
+    )
+    rows = jnp.concatenate([names, face.astype(f32), jnp.zeros((1, 6 * elements), f32)], axis=0)
+    out_ref[-8:, :] = jnp.zeros((8, 128), f32)
+    out_ref[-8:, :elements] = lax.dot_general(
+        rows, picked.astype(f32), (((1,), (1,)), ((), ())),
+        precision=highest, preferred_element_type=f32,
+    )
+
+
+def facing_pairs(picked, table, elements):
     half = low_half((elements, 128))
-    total = None
-    for table in tables:
-        facing = dot(picked, table)
-        field_rows = []
-        for c in range(FIELDS):
-            blocks = [
-                facing[f * elements : (f + 1) * elements, c * 128 : (c + 1) * 128]
-                for f in range(6)
-            ]
-            pairs = [jnp.where(half, blocks[f], blocks[f + 1]) for f in range(0, 6, 2)]
-            field_rows.append(jnp.concatenate(pairs, axis=1))
-        part = dot(jnp.concatenate(field_rows, axis=0).astype(bf16), lift)
-        total = part if total is None else total + part
-    return total
+    facing = dot(picked, table)
+    field_rows = []
+    for c in range(FIELDS):
+        blocks = [
+            facing[f * elements : (f + 1) * elements, c * 128 : (c + 1) * 128] for f in range(6)
+        ]
+        pairs = [jnp.where(half, blocks[f], blocks[f + 1]) for f in range(0, 6, 2)]
+        field_rows.append(jnp.concatenate(pairs, axis=1))
+    return jnp.concatenate(field_rows, axis=0).astype(bf16)
 
 
 def x_derivative(fields):
@@ -183,7 +192,7 @@
     return out
 
 
-def local_rate(fields, velocity_ref, neigh_ref, tables, yz_high, yz_low, lift):
+def local_rate(fields, velocity_ref, neigh_ref, table, yz_high, yz_low, lift):
     elements = neigh_ref.shape[1]
     high, low = split(fields)
     speed = velocity_ref[...].T
@@ -208,23 +217,25 @@
                 for j in range(4)
             ]
             rows.append(jnp.concatenate(tiles, axis=1))
-    names = column(neigh_ref)
-    keys = local_key(elements)
-    picked = jnp.concatenate([pick_rows(names[:, f : f + 1], keys) for f in range(6)], axis=0)
-    lifted = lift_rows(picked, tables, lift, elements)
+    picked = pick_faces(column(neigh_ref), local_key(elements))
+    lifted = dot(facing_pairs(picked, table, elements), lift)
     return penalty * (lifted - face_counts() * fields) - jnp.concatenate(rows, axis=0)
 
 
-def remote_terms(me, neigh_ref, shared_refs, lift):
-    elements = neigh_ref.shape[1]
-    names = column(neigh_ref)
-    lane = lax.broadcasted_iota(jnp.int32, (1, elements), 1)
-    keys = jnp.concatenate(
-        [6 * elements + (me ^ m) * elements + lane for m in range(len(shared_refs))], axis=1
-    )
-    picked = jnp.concatenate([pick_rows(names[:, f : f + 1], keys) for f in range(6)], axis=0)
-    table = jnp.concatenate([unpack_rows(ref, elements) for ref in shared_refs], axis=0)
-    return lift_rows(picked, split(table), lift, elements)
+def pick_faces(names, keys):
+    return jnp.concatenate([pick_rows(names[:, f : f + 1], keys) for f in range(6)], axis=0)
+
+
+def remote_keys(elements):
+    me = lax.axis_index("ax")
+    lane = iota((1, elements), 1)
+    return jnp.concatenate(
+        [6 * elements + (me ^ m) * elements + lane for m in range(lax.axis_size("ax"))], axis=1
+    )
+
+
+def shared_table(refs, elements):
+    return jnp.concatenate([unpack_rows(ref, elements) for ref in refs], axis=0)
 
 
 def rows_of(ref):
@@ -235,7 +246,7 @@
 def load_kernel(*refs):
     count = 8
     sources, loaded = refs[:count], refs[count : 2 * count]
-    extract_ref, lift_ref, high_ref, low_ref, shared_ref, sems = refs[2 * count :]
+    extract_ref, lift_ref, cross_ref, table_ref, shared_ref, sems = refs[2 * count :]
     copies = [
         pltpu.make_async_copy(source, target, sems.at[i])
         for i, (source, target) in enumerate(zip(sources, loaded))
@@ -250,46 +261,59 @@
     for f in range(6):
         here = face_node(f, row) == lane
         lift_ref[f * 64 : (f + 1) * 64, :] = jnp.where(here, 1.0, 0.0).astype(bf16)
+    row, lane = iota((64, 128), 0), iota((64, 128), 1)
+    for f in range(6):
+        for g in range(6):
+            here = face_node(f, row) == face_node(g, lane & 63)
+            cross_ref[f * 64 : (f + 1) * 64, g * 128 : (g + 1) * 128] = jnp.where(
+                here, 1.0, 0.0
+            ).astype(bf16)
     for copy in copies:
         copy.wait()
-    high, low = face_tables(rows_of(loaded[0]), extract_ref[...])
-    high_ref[...] = high
-    low_ref[...] = low
-    share_rows(high, low, loaded[1], shared_ref)
+    table = face_table(rows_of(loaded[0]), extract_ref[...])
+    table_ref[...] = table
+    picked = pick_rows(column(loaded[1]), local_key(loaded[1].shape[1]))
+    share_rows(table, picked, shared_ref)
+    share_names(loaded[3], picked, shared_ref)
 
 
 def first_local_kernel(
-    state_ref, velocity_ref, neigh_ref, high_ref, low_ref, yz, lift, out_ref
+    state_ref, velocity_ref, neigh_ref, send_ref, table_ref, yz, lift, extract, out_ref, shared_ref
 ):
     fields = rows_of(state_ref)
     rate = local_rate(
-        fields, velocity_ref, neigh_ref, (high_ref[...], low_ref[...]),
-        *split(yz[...]), lift[...],
-    )
-    out_ref[...] = (fields + time_step * rate).reshape(out_ref.shape)
-
-
-def first_finish_kernel(base_ref, neigh_ref, send_ref, lift, extract, *refs):
-    shared_refs, (first_ref, high_ref, low_ref, shared_ref) = refs[:-4], refs[-4:]
-    me = lax.axis_index("ax")
-    terms = remote_terms(me, neigh_ref, shared_refs, lift[...])
+        fields, velocity_ref, neigh_ref, table_ref[...], *split(yz[...]), lift[...]
+    )
+    base = fields + time_step * rate
+    out_ref[...] = base.reshape(out_ref.shape)
+    picked = pick_rows(column(send_ref), local_key(send_ref.shape[1]))
+    share_rows(face_table(base, extract[...]), picked, shared_ref)
+
+
+def second_local_kernel(
+    state_ref, base_ref, velocity_ref, neigh_ref, yz, lift, extract, cross, *refs
+):
+    shared_refs, (out_ref, added_ref) = refs[:-2], refs[-2:]
+    elements = neigh_ref.shape[1]
+    table = shared_table(shared_refs, elements).astype(bf16)
+    keys = remote_keys(elements)
+    picked = pick_faces(column(neigh_ref), keys)
+    terms = dot(facing_pairs(picked, table, elements), lift[...])
     first = rows_of(base_ref) + (time_step * penalty) * terms
-    first_ref[...] = first.reshape(first_ref.shape)
-    high, low = face_tables(first, extract[...])
-    high_ref[...] = high
-    low_ref[...] = low
-    share_rows(high, low, send_ref, shared_ref)
-
-
-def second_local_kernel(
-    state_ref, first_ref, velocity_ref, neigh_ref, high_ref, low_ref, yz, lift, out_ref
-):
-    fields = rows_of(first_ref)
     rate = local_rate(
-        fields, velocity_ref, neigh_ref, (high_ref[...], low_ref[...]),
-        *split(yz[...]), lift[...],
-    )
-    out_ref[...] = (0.5 * (rows_of(state_ref) + fields + time_step * rate)).reshape(out_ref.shape)
+        first, velocity_ref, neigh_ref, face_table(first, extract[...]), *split(yz[...]), lift[...]
+    )
+    second = 0.5 * (rows_of(state_ref) + first + time_step * rate)
+    out_ref[...] = second.reshape(out_ref.shape)
+    names = jnp.concatenate([ref[-8:, :].T[:elements] for ref in shared_refs], axis=0)
+    pairs = facing_pairs(pick_faces(names, keys), table, names.shape[0])
+    for c in range(FIELDS):
+        rows = slice(c * names.shape[0], (c + 1) * names.shape[0])
+        faces = dot(pairs[rows], cross[...])
+        added = faces[:, :128]
+        for f in range(1, 6):
+            added = jnp.where(names[:, 6:7] == f, faces[:, f * 128 : (f + 1) * 128], added)
+        added_ref[:, c * 128 : (c + 1) * 128] = (time_step * penalty) * added
 
 
 def maps_kernel(maps_ref, device_ref, block_ref, radial_ref, axial_ref, high_ref, low_ref):
@@ -330,15 +354,24 @@
                 low_ref[rows, lanes] = jnp.where(mine, value_low.astype(f32), 0.0).astype(bf16)
 
 
-def sample_kernel(base_ref, neigh_ref, lift, radial_ref, axial_ref, high_ref, low_ref, *refs):
+def exchange_plan(size):
+    straight = [m for m in range(size // 2, 3 * size // 4) if m & 1]
+    relayed = [m for m in range(size - 1, 0, -2) if m not in straight]
+    return relayed, [m for m in range(size) if m not in relayed]
+
+
+def sample_kernel(
+    base_ref, neigh_ref, added_ref, lift, radial_ref, axial_ref, high_ref, low_ref, *refs
+):
     sectors = high_ref.shape[1] // (PB * TB * 8)
     shares = lax.axis_size("ax")
     shared_refs = refs[:shares]
-    new_ref, out_refs = refs[shares], refs[shares + 1 : shares + 1 + sectors]
-    turned_ref, mapped_ref, parts_ref = refs[shares + 1 + sectors :]
+    new_ref, out_refs = refs[shares], refs[shares + 1 : -3]
+    turned_ref, mapped_ref, parts_ref = refs[-3:]
     elements = neigh_ref.shape[1]
-    me = lax.axis_index("ax")
-    terms = remote_terms(me, neigh_ref, shared_refs, lift[...])
+    table = (shared_table(shared_refs, elements) + added_ref[...]).astype(bf16)
+    picked = pick_faces(column(neigh_ref), remote_keys(elements))
+    terms = dot(facing_pairs(picked, table, elements), lift[...])
     new_state = rows_of(base_ref) + (0.5 * time_step * penalty) * terms
     new_ref[...] = new_state.reshape(new_ref.shape)
     gap = jnp.zeros((64 - elements, 128), f32)
@@ -381,14 +414,17 @@
                 start = c * 64 + g * rows
                 parts_ref[pb * groups + g, c * rows : (c + 1) * rows, :] = total[start : start + rows]
     owner = lax.axis_index("az")
-    for m in range(sectors):
-        out_refs[m][...] = parts_ref[owner ^ m]
-
-
-def fourier_kernel(table_ref, *refs):
+    relayed, kept = exchange_plan(sectors)
+    for i, m in enumerate(relayed):
+        out_refs[0][i] = parts_ref[owner ^ m]
+    for i, m in enumerate(kept):
+        out_refs[1 + i][...] = parts_ref[owner ^ m]
+
+
+def fourier_kernel(table_ref, bundle_ref, *refs):
     out_ref = refs[-1]
-    total = refs[0][...]
-    for ref in refs[1:-1]:
+    total = bundle_ref[bundle_ref.shape[0] - 1]
+    for ref in refs[:-1]:
         total = total + ref[...]
     high, low = split(total)
     weight, weight_low = split(table_ref[...])
@@ -400,6 +436,12 @@
             out_ref[k, c] = coeffs[c * rows : (c + 1) * rows, k * width : (k + 1) * width]
 
 
+def join_kernel(got_ref, *refs):
+    count = len(refs) // 2
+    for i in range(count):
+        refs[count + i][...] = refs[i][...] + got_ref[i]
+
+
 def store_kernel(new_ref, out_ref, sem):
     copy = pltpu.make_async_copy(new_ref, out_ref, sem)
     copy.start()
@@ -410,7 +452,7 @@
     return jax.ShapeDtypeStruct(dims, dtype)
 
 
-def call(kernel, outs, *args, scratch=(), flops=0, in_space=pltpu.VMEM, out_space=pltpu.VMEM):
+def call(kernel, outs, *args, scratch=(), flops=0, in_space=pltpu.VMEM, out_space=pltpu.VMEM, aliases={}):
     size = sum(math.prod(a.shape) * a.dtype.itemsize for a in list(args) + list(outs))
     return pl.pallas_call(
         kernel,
@@ -418,6 +460,7 @@
         in_specs=[pl.BlockSpec(memory_space=in_space)] * len(args),
         out_specs=tuple([pl.BlockSpec(memory_space=out_space)] * len(outs)),
         scratch_shapes=list(scratch),
+        input_output_aliases=aliases,
         cost_estimate=pl.CostEstimate(flops=flops, bytes_accessed=size, transcendentals=0),
         compiler_params=pltpu.CompilerParams(vmem_limit_bytes=48 * 1024 * 1024),
     )(*args)
@@ -444,45 +487,45 @@
     )
     yz_table = jnp.asarray(tile_tables(), f32)
     face_rows = shape((6 * elements, FIELDS * 128), bf16)
-    travel = shape((FIELDS * elements // 2, 128))
+    travel = FIELDS * elements // 2
     sources = inputs + (yz_table,)
     sources = tuple(pltpu.with_memory_space_constraint(a, pltpu.HBM) for a in sources)
     loaded = call(
         load_kernel,
         tuple(shape(a.shape, a.dtype) for a in sources)
-        + (shape((512, 768), bf16), shape((384, 512), bf16), face_rows, face_rows, travel),
+        + (shape((512, 768), bf16), shape((384, 512), bf16), shape((384, 768), bf16))
+        + (face_rows, shape((travel + 8, 128))),
         *sources,
         scratch=(pltpu.SemaphoreType.DMA((len(sources),)),),
         flops=400_000_000,
         in_space=pltpu.HBM,
     )
-    fields, sends, speed, names, maps, places, blocks, yz, extract, lift, high, low, shared = loaded
+    fields, sends, speed, names, maps, places, blocks, yz, extract, lift, cross, table, shared = loaded
     cube = shape(fields.shape)
     others = exchange(shared, "ax")
-    base = call(
-        first_local_kernel, (cube,), fields, speed, names, high, low, yz, lift,
+    base, shared = call(
+        first_local_kernel, (cube, shape((travel, 128))),
+        fields, speed, names, sends, table, yz, lift, extract,
         flops=1_000_000_000,
-    )[0]
+    )
+    firsts = exchange(shared, "ax")
     lanes = sectors * TB * 8
     weights = shape((512, PB * lanes), bf16)
     radial, axial, weight_high, weight_low = call(
         maps_kernel, (shape((64, 128)), shape((64, 128)), weights, weights), maps, places, blocks,
         flops=100_000_000,
     )
-    first, high, low, shared = call(
-        first_finish_kernel, (cube, face_rows, face_rows, travel),
-        base, names, sends, lift, extract, *others,
-        flops=600_000_000,
-    )
-    others = exchange(shared, "ax")
-    base = call(
-        second_local_kernel, (cube,), fields, first, speed, names, high, low, yz, lift,
-        flops=1_000_000_000,
-    )[0]
+    base, added = call(
+        second_local_kernel, (cube, shape((lax.axis_size("ax") * elements, FIELDS * 128))),
+        fields, base, speed, names, yz, lift, extract, cross, *others,
+        flops=1_500_000_000,
+    )
     rows = FIELDS * 64 * PB // sectors
-    pieces = call(
-        sample_kernel, (cube,) + (shape((rows, lanes)),) * sectors,
-        base, names, lift, radial, axial, weight_high, weight_low, *others,
+    piece = shape((rows, lanes))
+    relayed, kept = exchange_plan(sectors)
+    sampled = call(
+        sample_kernel, (cube, shape((len(relayed), rows, lanes))) + (piece,) * len(kept),
+        base, names, added, lift, radial, axial, weight_high, weight_low, *firsts,
         scratch=(
             pltpu.VMEM((FIELDS, 4, 128, 128), f32),
             pltpu.VMEM((FIELDS * 64, 512), f32),
@@ -490,19 +533,27 @@
         ),
         flops=800_000_000,
     )
-    new_state, pieces = pieces[0], pieces[1:]
+    new_state, bundle, pieces = sampled[0], sampled[1], dict(zip(kept, sampled[2:]))
     stored = call(
         store_kernel, (cube,), new_state, scratch=(pltpu.SemaphoreType.DMA,), out_space=pltpu.HBM
     )[0]
-    arrived = [pieces[0]] + [
-        lax.ppermute(pieces[m], "az", [(i, i ^ m) for i in range(sectors)])
-        for m in range(sectors - 1, 0, -1)
-    ]
+
+    def swap(value, mask):
+        return lax.ppermute(value, "az", [(i, i ^ mask) for i in range(sectors)])
+
+    bundle = swap(bundle, 1)
+    joined = [m - 1 for m in relayed if m > 1]
+    arrived = [swap(pieces[m], m) for m in kept if m and m not in joined]
+    sums = call(
+        join_kernel, (piece,) * len(joined), bundle, *[pieces[m] for m in joined]
+    )
+    arrived += [swap(value, m) for m, value in zip(joined, sums)]
+    arrived.append(pieces[0])
     angle = 2.0 * np.pi / lanes * (np.outer(np.arange(lanes), np.arange(lanes)) % lanes)
     table = np.concatenate([np.cos(angle), -np.sin(angle)], axis=1) * lanes**-0.5
     spectrum = call(
         fourier_kernel, (shape((2, FIELDS, rows // FIELDS, lanes)),),
-        jnp.asarray(table, f32), *arrived,
+        jnp.asarray(table, f32), bundle, *arrived,
         flops=100_000_000,
     )[0]
     return stored.transpose(1, 0, 2), spectrum

time: 40.1 us -> 34.3 us (0.86)
  starting transfers between devices: 20.2 us -> 14.8 us
  waiting for transfers between devices: 7.05 us -> 6.28 us
    ppermute x7 -> x5, starting transfers between devices: 15.1 us -> 9.43 us  [swap(): return lax.ppermute(value, 'az', [(i, i ^ mask) for i in range(sectors)])]
    ppermute x6, waiting for transfers between devices: 3.96 us -> 0.02 us  [exchange(): lax.ppermute(value, axis, [(i, i ^ m) for i in range(size)])]
    ppermute x7 -> x5, waiting for transfers between devices: 3.09 us -> 6.26 us  [swap(): return lax.ppermute(value, 'az', [(i, i ^ mask) for i in range(sectors)])]
  transfers between devices with their start and end apart: 13 -> 11, of which waited for: 6 -> 3; matrix products, arithmetic and copies ran while one was open for 0% -> 0% of each run, Pallas kernels for 11% -> 19%
where the time goes in v3:
time: 34.3 us; the launch traced here: 34.1 us
  starting transfers between devices  14.8 us (43%)
  Pallas kernels  12.3 us (36%)
  waiting for transfers between devices  6.28 us (18%)
  between operations  0.76 us (2%)
    pallas_call x8, Pallas kernels, call(): pl.pallas_call(kernel, out_shape=outs, in_specs=[pl.BlockSpec(memory_spac...  12.3 us
    ppermute x5, starting transfers between devices, swap(): return lax.ppermute(value, 'az', [(i, i ^ mask) for i in range(sectors)])  9.43 us
    ppermute x5, waiting for transfers between devices, swap(): return lax.ppermute(value, 'az', [(i, i ^ mask) for i in range(sectors)])  6.26 us
    ppermute x6, starting transfers between devices, exchange(): lax.ppermute(value, axis, [(i, i ^ m) for i in range(size)])  5.38 us
  transfers between devices with their start and end apart: 11, of which 3 were waited for; matrix products, arithmetic and copies ran while one was open for 0% of the time, Pallas kernels for 19%

profile of v3, /device:TPU:0, one launch (start us, length us, event | category | flops | bytes accessed | tf_op | source)
XLA Modules:
  0.0 34.1 jit_solution(9867417963526030790)
XLA Ops:
  0.6 2.2 %shard_map.104 = (f32[5,48,512]{2,1,0:T(8,128)S(1)}, s32[1,48]{1,0:T(1,128)S(1)}, f32[3,48]{1,0:T(4,128)S(1)}, s32[6,48]{1,0:T(8,128)S(1)}, f32[3,64,48]{2,1,0:T...) custom-call(f32[5,48,512]{2,1,0:T(8,128)} %bitcast.11, ...), custom_call_target="tpu_custom_call" | custom-call | flops 400000000 | bytes 3527168 | tf_op jit(solution)/shard_map/pallas_call | solution.py:457
  2.9 2.5 %collective-permute-start.2 = (f32[128,128]{1,0:T(8,128)S(1)}, f32[128,128]{1,0:T(8,128)S(1)}, u32[]{:S(2)}, u32[]{:S(2)}) collective-permute-start(f32[128,128]{1,0:T(8,128)S(1)} %get-tuple-element.42.refs_0_), channel_id=1, source_target_pairs={{0,3},{1,2},{2,1},{3,0},{4,7},{5,6},{6,5},{7,4},{8,11},{9,10},{10,... | collective-permute-start | bytes 196616 | tf_op jit(solution)/shard_map/ppermute | solution.py:472
  5.3 0.6 %collective-permute-start.1 = (f32[128,128]{1,0:T(8,128)S(1)}, f32[128,128]{1,0:T(8,128)S(1)}, u32[]{:S(2)}, u32[]{:S(2)}) collective-permute-start(f32[128,128]{1,0:T(8,128)S(1)} %get-tuple-element.42.refs_0_), channel_id=1, source_target_pairs={{0,2},{1,3},{2,0},{3,1},{4,6},{5,7},{6,4},{7,5},{8,10},{9,11},{10,... | collective-permute-start | bytes 196616 | tf_op jit(solution)/shard_map/ppermute | solution.py:472
  6.0 0.0 collective-permute-start
  6.0 1.8 %shard_map.105 = (f32[5,48,512]{2,1,0:T(8,128)S(1)}, f32[120,128]{1,0:T(8,128)S(1)}) custom-call(f32[5,48,512]{2,1,0:T(8,128)S(1)} %get-tuple-element.32.state_ref, f32[3,48]{1,0:T(4,128)S(1)} %get-tuple-element.33.velocity_ref, s32[6,48]{1,0:T(8,128)S(1)} %get-tuple-element.34.neigh_ref, s32[1,48]{1,0:T(1,128)S(1)} %get-tuple-element.35.send_ref, ...), custom_call_target="tpu_custom_call" | custom-call | flops 1000000000 | bytes 2725760 | tf_op jit(solution)/shard_map/pallas_call | solution.py:457
  7.8 1.5 %collective-permute-start.5 = (f32[120,128]{1,0:T(8,128)S(1)}, f32[120,128]{1,0:T(8,128)S(1)}, u32[]{:S(2)}, u32[]{:S(2)}) collective-permute-start(f32[120,128]{1,0:T(8,128)S(1)} %get-tuple-element.52.refs_0_), channel_id=1, source_target_pairs={{0,3},{1,2},{2,1},{3,0},{4,7},{5,6},{6,5},{7,4},{8,11},{9,10},{10,... | collective-permute-start | bytes 184328 | tf_op jit(solution)/shard_map/ppermute | solution.py:472
  9.3 0.6 %collective-permute-start.4 = (f32[120,128]{1,0:T(8,128)S(1)}, f32[120,128]{1,0:T(8,128)S(1)}, u32[]{:S(2)}, u32[]{:S(2)}) collective-permute-start(f32[120,128]{1,0:T(8,128)S(1)} %get-tuple-element.52.refs_0_), channel_id=1, source_target_pairs={{0,2},{1,3},{2,0},{3,1},{4,6},{5,7},{6,4},{7,5},{8,10},{9,11},{10,... | collective-permute-start | bytes 184328 | tf_op jit(solution)/shard_map/ppermute | solution.py:472
  9.9 0.6 %shard_map.107 = (f32[64,128]{1,0:T(8,128)S(1)}, f32[64,128]{1,0:T(8,128)S(1)}, bf16[512,512]{1,0:T(8,128)(2,1)S(1)}, bf16[512,512]{1,0:T(8,128)(2,1)S(1)}) custom-call(f32[3,64,48]{2,1,0:T(8,128)S(1)} %get-tuple-element.45.maps_ref, s32[1,48]{1,0:T(1,128)S(1)} %get-tuple-element.46.device_ref, s32[1,48]{1,0:T(1,128)S(1)} %get-tuple-element.47.block_ref), custom_call_target="tpu_custom_call" | custom-call | flops 100000000 | bytes 1151360 | tf_op jit(solution)/shard_map/pallas_call | solution.py:457
  10.6 0.0 collective-permute-done.2.refs_3_
  10.6 0.1 collective-permute-start.3
  10.6 0.0 collective-permute-done.1.refs_2_
  10.7 0.0 collective-permute-done.refs_1_
  10.7 3.2 %shard_map.106 = (f32[5,48,512]{2,1,0:T(8,128)S(1)}, f32[192,640]{1,0:T(8,128)S(1)}) custom-call(f32[5,48,512]{2,1,0:T(8,128)S(1)} %get-tuple-element.32.state_ref, f32[5,48,512]{2,1,0:T(8,128)S(1)} %get-tuple-element.40.base_ref, f32[3,48]{1,0:T(4,128)S(1)} %get-tuple-element.33.velocity_ref, s32[6,48]{1,0:T(8,128)S(1)} %get-tuple-element.34.neigh_ref, ...), custom_call_target="tpu_custom_call" | custom-call | flops 1500000000 | bytes 4130496 | tf_op jit(solution)/shard_map/pallas_call | solution.py:457
  13.9 0.0 collective-permute-done.5.refs_3_
  13.9 0.0 collective-permute-done.4.refs_2_
  13.9 0.0 collective-permute-done.3.refs_1_
  13.9 2.8 %shard_map.108 = (f32[5,48,512]{2,1,0:T(8,128)S(1)}, f32[3,160,128]{2,1,0:T(8,128)S(1)}, f32[160,128]{1,0:T(8,128)S(1)}, f32[160,128]{1,0:T(8,128)S(1)}, f32[160...) custom-call(f32[5,48,512]{2,1,0:T(8,128)S(1)} %get-tuple-element.43.base_ref, ...), custom_call_target="tpu_custom_call" | custom-call | flops 800000000 | bytes 3884160 | tf_op jit(solution)/shard_map/pallas_call | solution.py:457
  16.7 1.6 %collective-permute-start.6 = (f32[3,160,128]{2,1,0:T(8,128)S(1)}, f32[3,160,128]{2,1,0:T(8,128)S(1)}, u32[]{:S(2)}, u32[]{:S(2)}) collective-permute-start(f32[3,160,128]{2,1,0:T(8,128)S(1)} %get-tuple-element.54), channel_id=1, source_target_pairs={{0,4},{4,0},{8,12},{12,8},{16,20},{20,16},{24,28},{28,24},{1,5},{5... | collective-permute-start | bytes 737288 | tf_op jit(solution)/shard_map/ppermute | solution.py:542
  18.3 2.6 %collective-permute-start.7 = (f32[160,128]{1,0:T(8,128)S(1)}, f32[160,128]{1,0:T(8,128)S(1)}, u32[]{:S(2)}, u32[]{:S(2)}) collective-permute-start(f32[160,128]{1,0:T(8,128)S(1)} %get-tuple-element.55), channel_id=1, source_target_pairs={{0,16},{4,20},{8,24},{12,28},{16,0},{20,4},{24,8},{28,12},{1,17},{... | collective-permute-start | bytes 245768 | tf_op jit(solution)/shard_map/ppermute | solution.py:542
  20.9 0.3 collective-permute-start.8
  21.2 3.9 %collective-permute-done.6.got_ref.bundle_ref = f32[3,160,128]{2,1,0:T(8,128)S(1)} collective-permute-done((f32[3,160,128]{2,1,0:T(8,128)S(1)}, f32[3,160,128]{2,1,0:T(8,128)S(1)}, u32[]{:S(2)}, u32[]{:S(2)}) %collective-permute-start.6) | collective-permute-done | bytes 245792 | tf_op jit(solution)/shard_map/ppermute | solution.py:542
  25.1 3.7 %collective-permute-start.9 = (f32[160,128]{1,0:T(8,128)S(1)}, f32[160,128]{1,0:T(8,128)S(1)}, u32[]{:S(2)}, u32[]{:S(2)}) collective-permute-start(f32[160,128]{1,0:T(8,128)S(1)} %get-tuple-element.59), channel_id=1, source_target_pairs={{0,24},{4,28},{8,16},{12,20},{16,8},{20,12},{24,0},{28,4},{1,25},{... | collective-permute-start | bytes 245768 | tf_op jit(solution)/shard_map/ppermute | solution.py:542
  28.8 1.3 %collective-permute-start.10 = (f32[160,128]{1,0:T(8,128)S(1)}, f32[160,128]{1,0:T(8,128)S(1)}, u32[]{:S(2)}, u32[]{:S(2)}) collective-permute-start(f32[160,128]{1,0:T(8,128)S(1)} %get-tuple-element.60), channel_id=1, source_target_pairs={{0,8},{4,12},{8,0},{12,4},{16,24},{20,28},{24,16},{28,20},{1,9},{5... | collective-permute-start | bytes 245768 | tf_op jit(solution)/shard_map/ppermute | solution.py:542
  30.1 0.0 copy-start
  30.1 0.8 %shard_map.109 = f32[5,48,512]{2,1,0:T(8,128)} custom-call(f32[5,48,512]{2,1,0:T(8,128)S(1)} %get-tuple-element.53.new_ref), custom_call_target="tpu_custom_call" | custom-call | bytes 983040 | tf_op jit(solution)/shard_map/pallas_call | solution.py:457
  30.9 0.0 collective-permute-done.7.refs_0_
  30.9 0.0 collective-permute-done.8.refs_1_
  30.9 0.6 %collective-permute-done.9.refs_2_ = f32[160,128]{1,0:T(8,128)S(1)} collective-permute-done((f32[160,128]{1,0:T(8,128)S(1)}, f32[160,128]{1,0:T(8,128)S(1)}, u32[]{:S(2)}, u32[]{:S(2)}) %collective-permute-start.9) | collective-permute-done | bytes 81952 | tf_op jit(solution)/shard_map/ppermute | solution.py:542
  31.6 1.7 %collective-permute-done.10.refs_3_ = f32[160,128]{1,0:T(8,128)S(1)} collective-permute-done((f32[160,128]{1,0:T(8,128)S(1)}, f32[160,128]{1,0:T(8,128)S(1)}, u32[]{:S(2)}, u32[]{:S(2)}) %collective-permute-start.10) | collective-permute-done | bytes 81952 | tf_op jit(solution)/shard_map/ppermute | solution.py:542
  33.2 0.0 copy-done
  33.3 0.9 %shard_map.111 = f32[2,5,32,128]{3,2,1,0:T(8,128)} custom-call(f32[128,256]{1,0:T(8,128)S(1)} %copy-done, f32[3,160,128]{2,1,0:T(8,128)S(1)} %collective-permute-done.6.got_ref.bundle_ref, f32[160,128]{1,0:T(8,128)S(1)} %collective-permute-done.7.refs_0_, f32[160,128]{1,0:T(8,128)S(1)} %collective-permute-done.8.refs_1_, ...), custom_call_target="tpu_custom_call" | custom-call | flops 100000000 | bytes 950272 | tf_op jit(solution)/shard_map/pallas_call | solution.py:457
  (1 shorter events, 0.0 us)
Async XLA Ops:
  2.9 7.7 %collective-permute-start.2 = (f32[128,128]{1,0:T(8,128)S(1)}, f32[128,128]{1,0:T(8,128)S(1)}, u32[]{:S(2)}, u32[]{:S(2)}) collective-permute-start(f32[128,128]{1,0:T(8,128)S(1)} %get-tuple-element.42.refs_0_), channel_id=1, source_target_pairs={{0,3},{1,2},{2,1},{3,0},{4,7},{5,6},{6,5},{7,4},{8,11},{9,10},{10,... | collective-permute-start | bytes 196616 | tf_op jit(solution)/shard_map/ppermute | solution.py:472
  5.3 5.3 %collective-permute-start.1 = (f32[128,128]{1,0:T(8,128)S(1)}, f32[128,128]{1,0:T(8,128)S(1)}, u32[]{:S(2)}, u32[]{:S(2)}) collective-permute-start(f32[128,128]{1,0:T(8,128)S(1)} %get-tuple-element.42.refs_0_), channel_id=1, source_target_pairs={{0,2},{1,3},{2,0},{3,1},{4,6},{5,7},{6,4},{7,5},{8,10},{9,11},{10,... | collective-permute-start | bytes 196616 | tf_op jit(solution)/shard_map/ppermute | solution.py:472
  6.0 4.7 %collective-permute-start = (f32[128,128]{1,0:T(8,128)S(1)}, f32[128,128]{1,0:T(8,128)S(1)}, u32[]{:S(2)}, u32[]{:S(2)}) collective-permute-start(f32[128,128]{1,0:T(8,128)S(1)} %get-tuple-element.42.refs_0_), channel_id=1, source_target_pairs={{0,1},{1,0},{2,3},{3,2},{4,5},{5,4},{6,7},{7,6},{8,9},{9,8},{10,11... | collective-permute-start | bytes 196616 | tf_op jit(solution)/shard_map/ppermute | solution.py:472
  7.8 6.1 %collective-permute-start.5 = (f32[120,128]{1,0:T(8,128)S(1)}, f32[120,128]{1,0:T(8,128)S(1)}, u32[]{:S(2)}, u32[]{:S(2)}) collective-permute-start(f32[120,128]{1,0:T(8,128)S(1)} %get-tuple-element.52.refs_0_), channel_id=1, source_target_pairs={{0,3},{1,2},{2,1},{3,0},{4,7},{5,6},{6,5},{7,4},{8,11},{9,10},{10,... | collective-permute-start | bytes 184328 | tf_op jit(solution)/shard_map/ppermute | solution.py:472
  9.3 4.6 %collective-permute-start.4 = (f32[120,128]{1,0:T(8,128)S(1)}, f32[120,128]{1,0:T(8,128)S(1)}, u32[]{:S(2)}, u32[]{:S(2)}) collective-permute-start(f32[120,128]{1,0:T(8,128)S(1)} %get-tuple-element.52.refs_0_), channel_id=1, source_target_pairs={{0,2},{1,3},{2,0},{3,1},{4,6},{5,7},{6,4},{7,5},{8,10},{9,11},{10,... | collective-permute-start | bytes 184328 | tf_op jit(solution)/shard_map/ppermute | solution.py:472
  10.6 3.4 %collective-permute-start.3 = (f32[120,128]{1,0:T(8,128)S(1)}, f32[120,128]{1,0:T(8,128)S(1)}, u32[]{:S(2)}, u32[]{:S(2)}) collective-permute-start(f32[120,128]{1,0:T(8,128)S(1)} %get-tuple-element.52.refs_0_), channel_id=1, source_target_pairs={{0,1},{1,0},{2,3},{3,2},{4,5},{5,4},{6,7},{7,6},{8,9},{9,8},{10,11... | collective-permute-start | bytes 184328 | tf_op jit(solution)/shard_map/ppermute | solution.py:472
  16.7 8.4 %collective-permute-start.6 = (f32[3,160,128]{2,1,0:T(8,128)S(1)}, f32[3,160,128]{2,1,0:T(8,128)S(1)}, u32[]{:S(2)}, u32[]{:S(2)}) collective-permute-start(f32[3,160,128]{2,1,0:T(8,128)S(1)} %get-tuple-element.54), channel_id=1, source_target_pairs={{0,4},{4,0},{8,12},{12,8},{16,20},{20,16},{24,28},{28,24},{1,5},{5... | collective-permute-start | bytes 737288 | tf_op jit(solution)/shard_map/ppermute | solution.py:542
  18.3 12.6 %collective-permute-start.7 = (f32[160,128]{1,0:T(8,128)S(1)}, f32[160,128]{1,0:T(8,128)S(1)}, u32[]{:S(2)}, u32[]{:S(2)}) collective-permute-start(f32[160,128]{1,0:T(8,128)S(1)} %get-tuple-element.55), channel_id=1, source_target_pairs={{0,16},{4,20},{8,24},{12,28},{16,0},{20,4},{24,8},{28,12},{1,17},{... | collective-permute-start | bytes 245768 | tf_op jit(solution)/shard_map/ppermute | solution.py:542
  20.9 10.1 %collective-permute-start.8 = (f32[160,128]{1,0:T(8,128)S(1)}, f32[160,128]{1,0:T(8,128)S(1)}, u32[]{:S(2)}, u32[]{:S(2)}) collective-permute-start(f32[160,128]{1,0:T(8,128)S(1)} %get-tuple-element.56), channel_id=1, source_target_pairs={{0,20},{4,16},{8,28},{12,24},{16,4},{20,0},{24,12},{28,8},{1,21},{... | collective-permute-start | bytes 245768 | tf_op jit(solution)/shard_map/ppermute | solution.py:542
  25.1 6.4 %collective-permute-start.9 = (f32[160,128]{1,0:T(8,128)S(1)}, f32[160,128]{1,0:T(8,128)S(1)}, u32[]{:S(2)}, u32[]{:S(2)}) collective-permute-start(f32[160,128]{1,0:T(8,128)S(1)} %get-tuple-element.59), channel_id=1, source_target_pairs={{0,24},{4,28},{8,16},{12,20},{16,8},{20,12},{24,0},{28,4},{1,25},{... | collective-permute-start | bytes 245768 | tf_op jit(solution)/shard_map/ppermute | solution.py:542
  28.8 4.4 %collective-permute-start.10 = (f32[160,128]{1,0:T(8,128)S(1)}, f32[160,128]{1,0:T(8,128)S(1)}, u32[]{:S(2)}, u32[]{:S(2)}) collective-permute-start(f32[160,128]{1,0:T(8,128)S(1)} %get-tuple-element.60), channel_id=1, source_target_pairs={{0,8},{4,12},{8,0},{12,4},{16,24},{20,28},{24,16},{28,20},{1,9},{5... | collective-permute-start | bytes 245768 | tf_op jit(solution)/shard_map/ppermute | solution.py:542
  30.1 3.1 %copy-start = (f32[128,256]{1,0:T(8,128)S(1)}, f32[128,256]{1,0:T(8,128)}, u32[]{:S(2)}) copy-start(f32[128,256]{1,0:T(8,128)} %constant.5.clone.table_ref) | copy-start | bytes 393220

commit v4 on v3

--- a/solution.py
+++ b/solution.py
@@ -247,9 +247,11 @@
     count = 8
     sources, loaded = refs[:count], refs[count : 2 * count]
     extract_ref, lift_ref, cross_ref, table_ref, shared_ref, sems = refs[2 * count :]
+    pairs = list(zip(sources, loaded))
+    fields = [(pairs[0][0].at[c], pairs[0][1].at[c]) for c in range(FIELDS)]
     copies = [
         pltpu.make_async_copy(source, target, sems.at[i])
-        for i, (source, target) in enumerate(zip(sources, loaded))
+        for i, (source, target) in enumerate(pairs[1:4] + fields + pairs[4:])
     ]
     for copy in copies:
         copy.start()
@@ -257,24 +259,26 @@
     for f in range(6):
         here = row == face_node(f, lane & 63)
         extract_ref[:, f * 128 : (f + 1) * 128] = jnp.where(here, 1.0, 0.0).astype(bf16)
+    for copy in copies[:3]:
+        copy.wait()
+    picked = pick_rows(column(loaded[1]), local_key(loaded[1].shape[1]))
+    share_names(loaded[3], picked, shared_ref)
     row, lane = iota((64, 512), 0), iota((64, 512), 1)
     for f in range(6):
         here = face_node(f, row) == lane
         lift_ref[f * 64 : (f + 1) * 64, :] = jnp.where(here, 1.0, 0.0).astype(bf16)
     row, lane = iota((64, 128), 0), iota((64, 128), 1)
     for f in range(6):
-        for g in range(6):
-            here = face_node(f, row) == face_node(g, lane & 63)
-            cross_ref[f * 64 : (f + 1) * 64, g * 128 : (g + 1) * 128] = jnp.where(
-                here, 1.0, 0.0
+        for g in range(0, 6, 2):
+            node = jnp.where(lane < 64, face_node(g, lane & 63), face_node(g + 1, lane & 63))
+            cross_ref[f * 64 : (f + 1) * 64, g * 64 : (g + 2) * 64] = jnp.where(
+                face_node(f, row) == node, 1.0, 0.0
             ).astype(bf16)
-    for copy in copies:
+    for copy in copies[3:]:
         copy.wait()
     table = face_table(rows_of(loaded[0]), extract_ref[...])
     table_ref[...] = table
-    picked = pick_rows(column(loaded[1]), local_key(loaded[1].shape[1]))
     share_rows(table, picked, shared_ref)
-    share_names(loaded[3], picked, shared_ref)
 
 
 def first_local_kernel(
@@ -290,73 +294,84 @@
     share_rows(face_table(base, extract[...]), picked, shared_ref)
 
 
+def fill_maps(
+    maps_ref, device_ref, block_ref, radial_ref, axial_ref, high_ref, low_ref
+):
+    elements = maps_ref.shape[2]
+    row, lane = iota((elements, 128), 0), iota((elements, 128), 1)
+    twice = ((lane & 63) == row).astype(f32).astype(bf16)
+    radial_ref[...] = exact_dot(maps_ref[1], twice)
+    swap = ((iota((64, 64), 0) >> 3) + 8 * (iota((64, 64), 0) & 7) == iota((64, 64), 1)).astype(f32)
+    axial = [dot(swap.astype(bf16), part).astype(bf16) for part in split(maps_ref[2])]
+    axial_ref[...] = dot(axial[0], twice) + dot(axial[1], twice)
+    tile_row, tile_lane = iota((64, 1024), 0), iota((64, 1024), 1)
+    tile = ((tile_row >> 3) == (tile_lane & 7)) & ((tile_row & 7) == (tile_lane >> 7))
+    tile = jnp.where(tile, 1.0, 0.0).astype(bf16)
+    values = [dot(part, tile) for part in split(maps_ref[0].T)]
+    places = device_ref[...].astype(f32).T
+    blocks = block_ref[...].astype(f32).T
+    theta_lanes = high_ref.shape[1] // PB
+    upper = (blocks >= PB).astype(f32)
+    sector_key = places * TB + upper
+    plane_key = blocks - PB * upper
+    gap = jnp.zeros((64 - elements, high_ref.shape[1]), bf16)
+    for y in range(8):
+        start = y * 64
+        high_ref[start + elements : start + 64, :] = gap
+        low_ref[start + elements : start + 64, :] = gap
+    for pb in range(PB):
+        for tile_at in range(theta_lanes // 128):
+            here = ((lane + tile_at * 128) >> 3).astype(f32)
+            mine = (sector_key == here) & (plane_key == pb)
+            begin = pb * theta_lanes + tile_at * 128
+            for ref, value in zip((high_ref, low_ref), values):
+                for y in range(8):
+                    ref[y * 64 : y * 64 + elements, begin : begin + 128] = jnp.where(
+                        mine, value[:, y * 128 : (y + 1) * 128], 0.0
+                    ).astype(bf16)
+
+
+def exact_dot(value, choice):
+    high, low = split(value)
+    return dot(high, choice) + dot(low, choice)
+
+
 def second_local_kernel(
-    state_ref, base_ref, velocity_ref, neigh_ref, yz, lift, extract, cross, *refs
+    state_ref, base_ref, velocity_ref, neigh_ref, send_ref, yz, lift, extract, cross, *refs
 ):
-    shared_refs, (out_ref, added_ref) = refs[:-2], refs[-2:]
+    shared_refs, map_refs, (out_ref, added_ref) = refs[:-9], refs[-9:-6] + refs[-4:], refs[-6:-4]
+    fill_maps(*map_refs)
     elements = neigh_ref.shape[1]
     table = shared_table(shared_refs, elements).astype(bf16)
     keys = remote_keys(elements)
     picked = pick_faces(column(neigh_ref), keys)
     terms = dot(facing_pairs(picked, table, elements), lift[...])
     first = rows_of(base_ref) + (time_step * penalty) * terms
+    first_table = face_table(first, extract[...])
     rate = local_rate(
-        first, velocity_ref, neigh_ref, face_table(first, extract[...]), *split(yz[...]), lift[...]
+        first, velocity_ref, neigh_ref, first_table, *split(yz[...]), lift[...]
     )
     second = 0.5 * (rows_of(state_ref) + first + time_step * rate)
     out_ref[...] = second.reshape(out_ref.shape)
-    names = jnp.concatenate([ref[-8:, :].T[:elements] for ref in shared_refs], axis=0)
-    pairs = facing_pairs(pick_faces(names, keys), table, names.shape[0])
+    own = pick_rows(column(send_ref), local_key(elements))
+    added_ref[:elements, :] = dot(own, first_table)
+    names = jnp.concatenate([ref[-8:, :].T[:elements] for ref in shared_refs[1:]], axis=0)
+    count = names.shape[0]
+    pairs = facing_pairs(pick_faces(names, keys), table, count)
+    face = names[:, 6:7]
+    half = low_half((count, 128))
+    same = half != ((face == 1) | (face == 3) | (face == 5))
     for c in range(FIELDS):
-        rows = slice(c * names.shape[0], (c + 1) * names.shape[0])
-        faces = dot(pairs[rows], cross[...])
-        added = faces[:, :128]
-        for f in range(1, 6):
-            added = jnp.where(names[:, 6:7] == f, faces[:, f * 128 : (f + 1) * 128], added)
-        added_ref[:, c * 128 : (c + 1) * 128] = (time_step * penalty) * added
-
-
-def maps_kernel(maps_ref, device_ref, block_ref, radial_ref, axial_ref, high_ref, low_ref):
-    elements = maps_ref.shape[2]
-    row = lax.broadcasted_iota(jnp.int32, (elements, 128), 0)
-    lane = lax.broadcasted_iota(jnp.int32, (elements, 128), 1)
-    twice = ((lane & 63) == row).astype(f32)
-    radial_ref[...] = jnp.dot(maps_ref[1], twice, precision=highest, preferred_element_type=f32)
-    axial = jnp.dot(maps_ref[2], twice, precision=highest, preferred_element_type=f32)
-    row64 = lax.broadcasted_iota(jnp.int32, (64, 64), 0)
-    lane64 = lax.broadcasted_iota(jnp.int32, (64, 64), 1)
-    swap = ((row64 >> 3) + 8 * (row64 & 7) == lane64).astype(f32)
-    axial_ref[...] = jnp.dot(swap, axial, precision=highest, preferred_element_type=f32)
-    azimuthal = maps_ref[0].T
-    row_t = lax.broadcasted_iota(jnp.int32, (64, 128), 0)
-    lane_t = lax.broadcasted_iota(jnp.int32, (64, 128), 1)
-    places = device_ref[...].astype(f32).T
-    blocks = block_ref[...].astype(f32).T
-    theta_lanes = high_ref.shape[1] // PB
-    high_ref[...] = jnp.zeros_like(high_ref)
-    low_ref[...] = jnp.zeros_like(low_ref)
-    upper = (blocks >= PB).astype(f32)
-    sector_key = places * TB + upper
-    plane_key = blocks - PB * upper
-    for y in range(8):
-        tile_t = ((row_t >> 3) == (lane_t & 7)) & ((row_t & 7) == y)
-        values = jnp.dot(
-            azimuthal, tile_t.astype(f32), precision=highest, preferred_element_type=f32
-        )
-        value_high, value_low = split(values)
-        rows = pl.ds((y // 2) * 128 + (y % 2) * 64, elements)
-        for pb in range(PB):
-            for tile in range(theta_lanes // 128):
-                here = ((lane + tile * 128) >> 3).astype(f32)
-                mine = (sector_key == here) & (plane_key == pb)
-                lanes = pl.ds(pb * theta_lanes + tile * 128, 128)
-                high_ref[rows, lanes] = jnp.where(mine, value_high.astype(f32), 0.0).astype(bf16)
-                low_ref[rows, lanes] = jnp.where(mine, value_low.astype(f32), 0.0).astype(bf16)
+        faces = dot(pairs[c * count : (c + 1) * count], cross[...])
+        added = jnp.where(face >= 2, faces[:, 128:256], faces[:, :128])
+        added = jnp.where(face >= 4, faces[:, 256:], added)
+        added = jnp.where(same, added, pltpu.roll(added, 64, 1))
+        added_ref[elements:, c * 128 : (c + 1) * 128] = (time_step * penalty) * added
 
 
 def exchange_plan(size):
     straight = [m for m in range(size // 2, 3 * size // 4) if m & 1]
-    relayed = [m for m in range(size - 1, 0, -2) if m not in straight]
+    relayed = [m for m in range(size - 1, 1, -2) if m not in straight]
     return relayed, [m for m in range(size) if m not in relayed]
 
 
@@ -364,12 +379,13 @@
     base_ref, neigh_ref, added_ref, lift, radial_ref, axial_ref, high_ref, low_ref, *refs
 ):
     sectors = high_ref.shape[1] // (PB * TB * 8)
-    shares = lax.axis_size("ax")
+    shares = lax.axis_size("ax") - 1
     shared_refs = refs[:shares]
     new_ref, out_refs = refs[shares], refs[shares + 1 : -3]
     turned_ref, mapped_ref, parts_ref = refs[-3:]
     elements = neigh_ref.shape[1]
-    table = (shared_table(shared_refs, elements) + added_ref[...]).astype(bf16)
+    added = added_ref[elements:, :] + shared_table(shared_refs, elements)
+    table = jnp.concatenate([added_ref[:elements, :], added], axis=0).astype(bf16)
     picked = pick_faces(column(neigh_ref), remote_keys(elements))
     terms = dot(facing_pairs(picked, table, elements), lift[...])
     new_state = rows_of(base_ref) + (0.5 * time_step * penalty) * terms
@@ -421,10 +437,10 @@
         out_refs[1 + i][...] = parts_ref[owner ^ m]
 
 
-def fourier_kernel(table_ref, bundle_ref, *refs):
+def fourier_kernel(table_ref, *refs):
     out_ref = refs[-1]
-    total = bundle_ref[bundle_ref.shape[0] - 1]
-    for ref in refs[:-1]:
+    total = refs[0][...]
+    for ref in refs[1:-1]:
         total = total + ref[...]
     high, low = split(total)
     weight, weight_low = split(table_ref[...])
@@ -438,8 +454,9 @@
 
 def join_kernel(got_ref, *refs):
     count = len(refs) // 2
-    for i in range(count):
+    for i in range(count - 1):
         refs[count + i][...] = refs[i][...] + got_ref[i]
+    refs[-1][...] = refs[count - 1][...]
 
 
 def store_kernel(new_ref, out_ref, sem):
@@ -493,10 +510,10 @@
     loaded = call(
         load_kernel,
         tuple(shape(a.shape, a.dtype) for a in sources)
-        + (shape((512, 768), bf16), shape((384, 512), bf16), shape((384, 768), bf16))
+        + (shape((512, 768), bf16), shape((384, 512), bf16), shape((384, 384), bf16))
         + (face_rows, shape((travel + 8, 128))),
         *sources,
-        scratch=(pltpu.SemaphoreType.DMA((len(sources),)),),
+        scratch=(pltpu.SemaphoreType.DMA((len(sources) - 1 + FIELDS,)),),
         flops=400_000_000,
         in_space=pltpu.HBM,
     )
@@ -511,13 +528,11 @@
     firsts = exchange(shared, "ax")
     lanes = sectors * TB * 8
     weights = shape((512, PB * lanes), bf16)
-    radial, axial, weight_high, weight_low = call(
-        maps_kernel, (shape((64, 128)), shape((64, 128)), weights, weights), maps, places, blocks,
-        flops=100_000_000,
-    )
-    base, added = call(
-        second_local_kernel, (cube, shape((lax.axis_size("ax") * elements, FIELDS * 128))),
-        fields, base, speed, names, yz, lift, extract, cross, *others,
+    base, added, radial, axial, weight_high, weight_low = call(
+        second_local_kernel,
+        (cube, shape((lax.axis_size("ax") * elements, FIELDS * 128)))
+        + (shape((64, 128)), shape((64, 128)), weights, weights),
+        fields, base, speed, names, sends, yz, lift, extract, cross, *others, maps, places, blocks,
         flops=1_500_000_000,
     )
     rows = FIELDS * 64 * PB // sectors
@@ -525,7 +540,7 @@
     relayed, kept = exchange_plan(sectors)
     sampled = call(
         sample_kernel, (cube, shape((len(relayed), rows, lanes))) + (piece,) * len(kept),
-        base, names, added, lift, radial, axial, weight_high, weight_low, *firsts,
+        base, names, added, lift, radial, axial, weight_high, weight_low, *firsts[1:],
         scratch=(
             pltpu.VMEM((FIELDS, 4, 128, 128), f32),
             pltpu.VMEM((FIELDS * 64, 512), f32),
@@ -542,18 +557,16 @@
         return lax.ppermute(value, "az", [(i, i ^ mask) for i in range(sectors)])
 
     bundle = swap(bundle, 1)
-    joined = [m - 1 for m in relayed if m > 1]
+    joined = [m - 1 for m in relayed] + [1]
     arrived = [swap(pieces[m], m) for m in kept if m and m not in joined]
-    sums = call(
-        join_kernel, (piece,) * len(joined), bundle, *[pieces[m] for m in joined]
-    )
+    sums = call(join_kernel, (piece,) * len(joined), bundle, *[pieces[m] for m in joined])
     arrived += [swap(value, m) for m, value in zip(joined, sums)]
     arrived.append(pieces[0])
     angle = 2.0 * np.pi / lanes * (np.outer(np.arange(lanes), np.arange(lanes)) % lanes)
     table = np.concatenate([np.cos(angle), -np.sin(angle)], axis=1) * lanes**-0.5
     spectrum = call(
         fourier_kernel, (shape((2, FIELDS, rows // FIELDS, lanes)),),
-        jnp.asarray(table, f32), bundle, *arrived,
+        jnp.asarray(table, f32), *arrived,
         flops=100_000_000,
     )[0]
     return stored.transpose(1, 0, 2), spectrum

time: 34.3 us -> 32.2 us (0.939)
  waiting for transfers between devices: 6.28 us -> 4.88 us
  Pallas kernels: 12.3 us -> 11.2 us
  starting transfers between devices: 14.8 us -> 15.3 us
    ppermute x5 -> x6, waiting for transfers between devices: 6.26 us -> 4.25 us  [swap(): return lax.ppermute(value, 'az', [(i, i ^ mask) for i in range(sectors)])]
    pallas_call x8 -> x7, Pallas kernels: 12.3 us -> 11.2 us  [call(): pl.pallas_call(kernel, out_shape=outs, in_specs=[pl.BlockSpec(memory_spac...]
    ppermute x6, waiting for transfers between devices: 0.02 us -> 0.64 us  [exchange(): lax.ppermute(value, axis, [(i, i ^ m) for i in range(size)])]
    ppermute x5 -> x6, starting transfers between devices: 9.43 us -> 10 us  [swap(): return lax.ppermute(value, 'az', [(i, i ^ mask) for i in range(sectors)])]
  transfers between devices with their start and end apart: 11 -> 12, of which waited for: 3 -> 5; matrix products, arithmetic and copies ran while one was open for 0% -> 0% of each run, Pallas kernels for 19% -> 17%
where the time goes in v4:
time: 32.2 us; the launch traced here: 32.1 us
  starting transfers between devices  15.3 us (48%)
  Pallas kernels  11.2 us (35%)
  waiting for transfers between devices  4.88 us (15%)
  between operations  0.7 us (2%)
    pallas_call x7, Pallas kernels, call(): pl.pallas_call(kernel, out_shape=outs, in_specs=[pl.BlockSpec(memory_spac...  11.2 us
    ppermute x6, starting transfers between devices, swap(): return lax.ppermute(value, 'az', [(i, i ^ mask) for i in range(sectors)])  10 us
    ppermute x6, starting transfers between devices, exchange(): lax.ppermute(value, axis, [(i, i ^ m) for i in range(size)])  5.31 us
    ppermute x6, waiting for transfers between devices, swap(): return lax.ppermute(value, 'az', [(i, i ^ mask) for i in range(sectors)])  4.25 us
  transfers between devices with their start and end apart: 12, of which 5 were waited for; matrix products, arithmetic and copies ran while one was open for 0% of the time, Pallas kernels for 17%

profile of v4, /device:TPU:0, one launch (start us, length us, event | category | flops | bytes accessed | tf_op | source)
XLA Modules:
  0.0 32.1 jit_solution(4082504446735627212)
XLA Ops:
  0.6 1.9 %shard_map.104 = (f32[5,48,512]{2,1,0:T(8,128)S(1)}, s32[1,48]{1,0:T(1,128)S(1)}, f32[3,48]{1,0:T(4,128)S(1)}, s32[6,48]{1,0:T(8,128)S(1)}, f32[3,64,48]{2,1,0:T...) custom-call(f32[5,48,512]{2,1,0:T(8,128)} %bitcast.11, ...), custom_call_target="tpu_custom_call" | custom-call | flops 400000000 | bytes 3232256 | tf_op jit(solution)/shard_map/pallas_call | solution.py:474
  2.6 2.5 %collective-permute-start.2 = (f32[128,128]{1,0:T(8,128)S(1)}, f32[128,128]{1,0:T(8,128)S(1)}, u32[]{:S(2)}, u32[]{:S(2)}) collective-permute-start(f32[128,128]{1,0:T(8,128)S(1)} %get-tuple-element.44.refs_0_), channel_id=1, source_target_pairs={{0,3},{1,2},{2,1},{3,0},{4,7},{5,6},{6,5},{7,4},{8,11},{9,10},{10,... | collective-permute-start | bytes 196616 | tf_op jit(solution)/shard_map/ppermute | solution.py:489
  5.1 0.6 %collective-permute-start.1 = (f32[128,128]{1,0:T(8,128)S(1)}, f32[128,128]{1,0:T(8,128)S(1)}, u32[]{:S(2)}, u32[]{:S(2)}) collective-permute-start(f32[128,128]{1,0:T(8,128)S(1)} %get-tuple-element.44.refs_0_), channel_id=1, source_target_pairs={{0,2},{1,3},{2,0},{3,1},{4,6},{5,7},{6,4},{7,5},{8,10},{9,11},{10,... | collective-permute-start | bytes 196616 | tf_op jit(solution)/shard_map/ppermute | solution.py:489
  5.7 0.0 collective-permute-start
  5.7 1.7 %shard_map.105 = (f32[5,48,512]{2,1,0:T(8,128)S(1)}, f32[120,128]{1,0:T(8,128)S(1)}) custom-call(f32[5,48,512]{2,1,0:T(8,128)S(1)} %get-tuple-element.34.state_ref, f32[3,48]{1,0:T(4,128)S(1)} %get-tuple-element.35.velocity_ref, s32[6,48]{1,0:T(8,128)S(1)} %get-tuple-element.36.neigh_ref, s32[1,48]{1,0:T(1,128)S(1)} %get-tuple-element.37.send_ref, ...), custom_call_target="tpu_custom_call" | custom-call | flops 1000000000 | bytes 2725760 | tf_op jit(solution)/shard_map/pallas_call | solution.py:474
  7.5 1.5 %collective-permute-start.5 = (f32[120,128]{1,0:T(8,128)S(1)}, f32[120,128]{1,0:T(8,128)S(1)}, u32[]{:S(2)}, u32[]{:S(2)}) collective-permute-start(f32[120,128]{1,0:T(8,128)S(1)} %get-tuple-element.54), channel_id=1, source_target_pairs={{0,3},{1,2},{2,1},{3,0},{4,7},{5,6},{6,5},{7,4},{8,11},{9,10},{10,... | collective-permute-start | bytes 184328 | tf_op jit(solution)/shard_map/ppermute | solution.py:489
  9.0 0.6 %collective-permute-start.4 = (f32[120,128]{1,0:T(8,128)S(1)}, f32[120,128]{1,0:T(8,128)S(1)}, u32[]{:S(2)}, u32[]{:S(2)}) collective-permute-start(f32[120,128]{1,0:T(8,128)S(1)} %get-tuple-element.54), channel_id=1, source_target_pairs={{0,2},{1,3},{2,0},{3,1},{4,6},{5,7},{6,4},{7,5},{8,10},{9,11},{10,... | collective-permute-start | bytes 184328 | tf_op jit(solution)/shard_map/ppermute | solution.py:489
  9.6 0.0 collective-permute-done.2.refs_3_
  9.6 0.0 collective-permute-start.3
  9.6 0.1 collective-permute-done.1.refs_2_
  9.7 0.0 collective-permute-done.refs_1_
  9.7 3.0 %shard_map.106 = (f32[5,48,512]{2,1,0:T(8,128)S(1)}, f32[192,640]{1,0:T(8,128)S(1)}, f32[64,128]{1,0:T(8,128)S(1)}, f32[64,128]{1,0:T(8,128)S(1)}, bf16[512,512]...) custom-call(f32[5,48,512]{2,1,0:T(8,128)S(1)} %get-tuple-element.34.state_ref, ...), custom_call_target="tpu_custom_call" | custom-call | flops 1500000000 | bytes 4987136 | tf_op jit(solution)/shard_map/pallas_call | solution.py:474
  12.8 0.0 collective-permute-done.5.refs_2_
  12.8 0.5 %collective-permute-done.4.refs_1_ = f32[120,128]{1,0:T(8,128)S(1)} collective-permute-done((f32[120,128]{1,0:T(8,128)S(1)}, f32[120,128]{1,0:T(8,128)S(1)}, u32[]{:S(2)}, u32[]{:S(2)}) %collective-permute-start.4) | collective-permute-done | bytes 61472 | tf_op jit(solution)/shard_map/ppermute | solution.py:489
  13.3 0.0 collective-permute-done.3.refs_0_
  13.3 2.8 %shard_map.107 = (f32[5,48,512]{2,1,0:T(8,128)S(1)}, f32[2,160,128]{2,1,0:T(8,128)S(1)}, f32[160,128]{1,0:T(8,128)S(1)}, f32[160,128]{1,0:T(8,128)S(1)}, f32[160...) custom-call(f32[5,48,512]{2,1,0:T(8,128)S(1)} %get-tuple-element.48.base_ref, ...), custom_call_target="tpu_custom_call" | custom-call | flops 800000000 | bytes 3822720 | tf_op jit(solution)/shard_map/pallas_call | solution.py:474
  16.1 1.6 %collective-permute-start.8 = (f32[2,160,128]{2,1,0:T(8,128)S(1)}, f32[2,160,128]{2,1,0:T(8,128)S(1)}, u32[]{:S(2)}, u32[]{:S(2)}) collective-permute-start(f32[2,160,128]{2,1,0:T(8,128)S(1)} %get-tuple-element.58), channel_id=1, source_target_pairs={{0,4},{4,0},{8,12},{12,8},{16,20},{20,16},{24,28},{28,24},{1,5},{5... | collective-permute-start | bytes 491528 | tf_op jit(solution)/shard_map/ppermute | solution.py:557
  17.7 2.6 %collective-permute-start.6 = (f32[160,128]{1,0:T(8,128)S(1)}, f32[160,128]{1,0:T(8,128)S(1)}, u32[]{:S(2)}, u32[]{:S(2)}) collective-permute-start(f32[160,128]{1,0:T(8,128)S(1)} %get-tuple-element.56), channel_id=1, source_target_pairs={{0,16},{4,20},{8,24},{12,28},{16,0},{20,4},{24,8},{28,12},{1,17},{... | collective-permute-start | bytes 245768 | tf_op jit(solution)/shard_map/ppermute | solution.py:557
  20.3 0.2 collective-permute-start.7
  20.5 1.6 %collective-permute-done.8.got_ref = f32[2,160,128]{2,1,0:T(8,128)S(1)} collective-permute-done((f32[2,160,128]{2,1,0:T(8,128)S(1)}, f32[2,160,128]{2,1,0:T(8,128)S(1)}, u32[]{:S(2)}, u32[]{:S(2)}) %collective-permute-start.8) | collective-permute-done | bytes 163872 | tf_op jit(solution)/shard_map/ppermute | solution.py:557
  22.2 3.7 %collective-permute-start.9 = (f32[160,128]{1,0:T(8,128)S(1)}, f32[160,128]{1,0:T(8,128)S(1)}, u32[]{:S(2)}, u32[]{:S(2)}) collective-permute-start(f32[160,128]{1,0:T(8,128)S(1)} %get-tuple-element.62), channel_id=1, source_target_pairs={{0,24},{4,28},{8,16},{12,20},{16,8},{20,12},{24,0},{28,4},{1,25},{... | collective-permute-start | bytes 245768 | tf_op jit(solution)/shard_map/ppermute | solution.py:557
  25.9 0.3 collective-permute-start.10
  26.2 1.6 %collective-permute-start.11 = (f32[160,128]{1,0:T(8,128)S(1)}, f32[160,128]{1,0:T(8,128)S(1)}, u32[]{:S(2)}, u32[]{:S(2)}) collective-permute-start(f32[160,128]{1,0:T(8,128)S(1)} %get-tuple-element.64), channel_id=1, source_target_pairs={{0,4},{4,0},{8,12},{12,8},{16,20},{20,16},{24,28},{28,24},{1,5},{5... | collective-permute-start | bytes 245768 | tf_op jit(solution)/shard_map/ppermute | solution.py:557
  27.8 0.0 copy-start
  27.8 0.8 %shard_map.108 = f32[5,48,512]{2,1,0:T(8,128)} custom-call(f32[5,48,512]{2,1,0:T(8,128)S(1)} %get-tuple-element.55.new_ref), custom_call_target="tpu_custom_call" | custom-call | bytes 983040 | tf_op jit(solution)/shard_map/pallas_call | solution.py:474
  28.6 0.0 collective-permute-done.6.refs_0_
  28.6 1.8 %collective-permute-done.7.refs_1_ = f32[160,128]{1,0:T(8,128)S(1)} collective-permute-done((f32[160,128]{1,0:T(8,128)S(1)}, f32[160,128]{1,0:T(8,128)S(1)}, u32[]{:S(2)}, u32[]{:S(2)}) %collective-permute-start.7) | collective-permute-done | bytes 81952 | tf_op jit(solution)/shard_map/ppermute | solution.py:557
  30.4 0.0 collective-permute-done.9.refs_2_
  30.4 0.8 %collective-permute-done.10.refs_3_ = f32[160,128]{1,0:T(8,128)S(1)} collective-permute-done((f32[160,128]{1,0:T(8,128)S(1)}, f32[160,128]{1,0:T(8,128)S(1)}, u32[]{:S(2)}, u32[]{:S(2)}) %collective-permute-start.10) | collective-permute-done | bytes 81952 | tf_op jit(solution)/shard_map/ppermute | solution.py:557
  31.2 0.0 collective-permute-done.11.refs_4_
  31.2 0.0 copy-done
  31.2 0.9 %shard_map.110 = f32[2,5,32,128]{3,2,1,0:T(8,128)} custom-call(f32[128,256]{1,0:T(8,128)S(1)} %copy-done, f32[160,128]{1,0:T(8,128)S(1)} %collective-permute-done.6.refs_0_, f32[160,128]{1,0:T(8,128)S(1)} %collective-permute-done.7.refs_1_, f32[160,128]{1,0:T(8,128)S(1)} %collective-permute-done.9.refs_2_, f32[160,128]{1,0:T(8,128)S(1)} %collective-permute-done.10.refs_3_, ...), custom_call_target="tpu_custom_call" | custom-call | flops 100000000 | bytes 786432 | tf_op jit(solution)/shard_map/pallas_call | solution.py:474
  (1 shorter events, 0.0 us)
Async XLA Ops:
  2.6 7.1 %collective-permute-start.2 = (f32[128,128]{1,0:T(8,128)S(1)}, f32[128,128]{1,0:T(8,128)S(1)}, u32[]{:S(2)}, u32[]{:S(2)}) collective-permute-start(f32[128,128]{1,0:T(8,128)S(1)} %get-tuple-element.44.refs_0_), channel_id=1, source_target_pairs={{0,3},{1,2},{2,1},{3,0},{4,7},{5,6},{6,5},{7,4},{8,11},{9,10},{10,... | collective-permute-start | bytes 196616 | tf_op jit(solution)/shard_map/ppermute | solution.py:489
  5.1 4.7 %collective-permute-start.1 = (f32[128,128]{1,0:T(8,128)S(1)}, f32[128,128]{1,0:T(8,128)S(1)}, u32[]{:S(2)}, u32[]{:S(2)}) collective-permute-start(f32[128,128]{1,0:T(8,128)S(1)} %get-tuple-element.44.refs_0_), channel_id=1, source_target_pairs={{0,2},{1,3},{2,0},{3,1},{4,6},{5,7},{6,4},{7,5},{8,10},{9,11},{10,... | collective-permute-start | bytes 196616 | tf_op jit(solution)/shard_map/ppermute | solution.py:489
  5.7 4.0 %collective-permute-start = (f32[128,128]{1,0:T(8,128)S(1)}, f32[128,128]{1,0:T(8,128)S(1)}, u32[]{:S(2)}, u32[]{:S(2)}) collective-permute-start(f32[128,128]{1,0:T(8,128)S(1)} %get-tuple-element.44.refs_0_), channel_id=1, source_target_pairs={{0,1},{1,0},{2,3},{3,2},{4,5},{5,4},{6,7},{7,6},{8,9},{9,8},{10,11... | collective-permute-start | bytes 196616 | tf_op jit(solution)/shard_map/ppermute | solution.py:489
  7.5 5.3 %collective-permute-start.5 = (f32[120,128]{1,0:T(8,128)S(1)}, f32[120,128]{1,0:T(8,128)S(1)}, u32[]{:S(2)}, u32[]{:S(2)}) collective-permute-start(f32[120,128]{1,0:T(8,128)S(1)} %get-tuple-element.54), channel_id=1, source_target_pairs={{0,3},{1,2},{2,1},{3,0},{4,7},{5,6},{6,5},{7,4},{8,11},{9,10},{10,... | collective-permute-start | bytes 184328 | tf_op jit(solution)/shard_map/ppermute | solution.py:489
  9.0 4.3 %collective-permute-start.4 = (f32[120,128]{1,0:T(8,128)S(1)}, f32[120,128]{1,0:T(8,128)S(1)}, u32[]{:S(2)}, u32[]{:S(2)}) collective-permute-start(f32[120,128]{1,0:T(8,128)S(1)} %get-tuple-element.54), channel_id=1, source_target_pairs={{0,2},{1,3},{2,0},{3,1},{4,6},{5,7},{6,4},{7,5},{8,10},{9,11},{10,... | collective-permute-start | bytes 184328 | tf_op jit(solution)/shard_map/ppermute | solution.py:489
  9.6 3.7 %collective-permute-start.3 = (f32[120,128]{1,0:T(8,128)S(1)}, f32[120,128]{1,0:T(8,128)S(1)}, u32[]{:S(2)}, u32[]{:S(2)}) collective-permute-start(f32[120,128]{1,0:T(8,128)S(1)} %get-tuple-element.54), channel_id=1, source_target_pairs={{0,1},{1,0},{2,3},{3,2},{4,5},{5,4},{6,7},{7,6},{8,9},{9,8},{10,11... | collective-permute-start | bytes 184328 | tf_op jit(solution)/shard_map/ppermute | solution.py:489
  16.1 6.1 %collective-permute-start.8 = (f32[2,160,128]{2,1,0:T(8,128)S(1)}, f32[2,160,128]{2,1,0:T(8,128)S(1)}, u32[]{:S(2)}, u32[]{:S(2)}) collective-permute-start(f32[2,160,128]{2,1,0:T(8,128)S(1)} %get-tuple-element.58), channel_id=1, source_target_pairs={{0,4},{4,0},{8,12},{12,8},{16,20},{20,16},{24,28},{28,24},{1,5},{5... | collective-permute-start | bytes 491528 | tf_op jit(solution)/shard_map/ppermute | solution.py:557
  17.7 10.9 %collective-permute-start.6 = (f32[160,128]{1,0:T(8,128)S(1)}, f32[160,128]{1,0:T(8,128)S(1)}, u32[]{:S(2)}, u32[]{:S(2)}) collective-permute-start(f32[160,128]{1,0:T(8,128)S(1)} %get-tuple-element.56), channel_id=1, source_target_pairs={{0,16},{4,20},{8,24},{12,28},{16,0},{20,4},{24,8},{28,12},{1,17},{... | collective-permute-start | bytes 245768 | tf_op jit(solution)/shard_map/ppermute | solution.py:557
  20.3 10.1 %collective-permute-start.7 = (f32[160,128]{1,0:T(8,128)S(1)}, f32[160,128]{1,0:T(8,128)S(1)}, u32[]{:S(2)}, u32[]{:S(2)}) collective-permute-start(f32[160,128]{1,0:T(8,128)S(1)} %get-tuple-element.57), channel_id=1, source_target_pairs={{0,20},{4,16},{8,28},{12,24},{16,4},{20,0},{24,12},{28,8},{1,21},{... | collective-permute-start | bytes 245768 | tf_op jit(solution)/shard_map/ppermute | solution.py:557
  22.2 8.2 %collective-permute-start.9 = (f32[160,128]{1,0:T(8,128)S(1)}, f32[160,128]{1,0:T(8,128)S(1)}, u32[]{:S(2)}, u32[]{:S(2)}) collective-permute-start(f32[160,128]{1,0:T(8,128)S(1)} %get-tuple-element.62), channel_id=1, source_target_pairs={{0,24},{4,28},{8,16},{12,20},{16,8},{20,12},{24,0},{28,4},{1,25},{... | collective-permute-start | bytes 245768 | tf_op jit(solution)/shard_map/ppermute | solution.py:557
  25.9 5.3 %collective-permute-start.10 = (f32[160,128]{1,0:T(8,128)S(1)}, f32[160,128]{1,0:T(8,128)S(1)}, u32[]{:S(2)}, u32[]{:S(2)}) collective-permute-start(f32[160,128]{1,0:T(8,128)S(1)} %get-tuple-element.63), channel_id=1, source_target_pairs={{0,8},{4,12},{8,0},{12,4},{16,24},{20,28},{24,16},{28,20},{1,9},{5... | collective-permute-start | bytes 245768 | tf_op jit(solution)/shard_map/ppermute | solution.py:557
  26.2 5.0 %collective-permute-start.11 = (f32[160,128]{1,0:T(8,128)S(1)}, f32[160,128]{1,0:T(8,128)S(1)}, u32[]{:S(2)}, u32[]{:S(2)}) collective-permute-start(f32[160,128]{1,0:T(8,128)S(1)} %get-tuple-element.64), channel_id=1, source_target_pairs={{0,4},{4,0},{8,12},{12,8},{16,20},{20,16},{24,28},{28,24},{1,5},{5... | collective-permute-start | bytes 245768 | tf_op jit(solution)/shard_map/ppermute | solution.py:557
  27.8 3.4 %copy-start = (f32[128,256]{1,0:T(8,128)S(1)}, f32[128,256]{1,0:T(8,128)}, u32[]{:S(2)}) copy-start(f32[128,256]{1,0:T(8,128)} %constant.5.clone.table_ref) | copy-start | bytes 393220

commit v5 on v4

--- a/solution.py
+++ b/solution.py
@@ -98,15 +98,18 @@
 def face_table(fields, extract):
     elements = fields.shape[0] // FIELDS
     faces = dot(fields.astype(bf16), extract).astype(bf16)
+    half = low_half((fields.shape[0], 128))
+    ends = [fields[:, :128], fields[:, 384:]]
+    turned = [pltpu.roll(end, 64, 1) for end in ends]
+    ends = [jnp.where(half, ends[0], turned[0]), jnp.where(half, turned[1], ends[1])]
+    blocks = [end.astype(bf16) for end in ends] + [
+        faces[:, f * 128 : (f + 1) * 128] for f in range(4)
+    ]
     rows = [
         jnp.concatenate(
-            [
-                faces[c * elements : (c + 1) * elements, f * 128 : (f + 1) * 128]
-                for c in range(FIELDS)
-            ],
-            axis=1,
+            [block[c * elements : (c + 1) * elements] for c in range(FIELDS)], axis=1
         )
-        for f in range(6)
+        for block in blocks
     ]
     return jnp.concatenate(rows, axis=0)
 
@@ -175,6 +178,29 @@
     return jnp.concatenate(field_rows, axis=0).astype(bf16)
 
 
+def lift_rows(picked, table, lift, elements):
+    half = low_half((elements, 128))
+    facing = dot(picked, table)
+    ends, inner = [], []
+    for c in range(FIELDS):
+        blocks = [
+            facing[f * elements : (f + 1) * elements, c * 128 : (c + 1) * 128] for f in range(6)
+        ]
+        ends.append((jnp.where(half, blocks[0], 0.0), jnp.where(half, 0.0, blocks[1])))
+        pairs = [jnp.where(half, blocks[f], blocks[f + 1]) for f in (2, 4)]
+        inner.append(jnp.concatenate(pairs, axis=1))
+    lifted = dot(jnp.concatenate(inner, axis=0).astype(bf16), lift)
+    rows = []
+    for c in range(FIELDS):
+        part = lifted[c * elements : (c + 1) * elements]
+        rows.append(
+            jnp.concatenate(
+                [part[:, :128] + ends[c][0], part[:, 128:384], part[:, 384:] + ends[c][1]], axis=1
+            )
+        )
+    return jnp.concatenate(rows, axis=0)
+
+
 def x_derivative(fields):
     deriv = spectral_derivative()
     half = low_half((1, 128))
@@ -197,12 +223,12 @@
     high, low = split(fields)
     speed = velocity_ref[...].T
     speeds = [jnp.broadcast_to(speed[:, d : d + 1], (elements, 128)) for d in range(3)]
+    yz_twice = jnp.concatenate([yz_high, yz_high], axis=0)
     both = []
     for j in range(4):
         lanes = slice(j * 128, (j + 1) * 128)
-        both.append(
-            dot(high[:, lanes], yz_high) + dot(low[:, lanes], yz_high) + dot(high[:, lanes], yz_low)
-        )
+        parts = jnp.concatenate([high[:, lanes], low[:, lanes]], axis=1)
+        both.append(dot(parts, yz_twice) + dot(high[:, lanes], yz_low))
     chunk = elements // 2
     rows = []
     for c in range(FIELDS):
@@ -218,7 +244,7 @@
             ]
             rows.append(jnp.concatenate(tiles, axis=1))
     picked = pick_faces(column(neigh_ref), local_key(elements))
-    lifted = dot(facing_pairs(picked, table, elements), lift)
+    lifted = lift_rows(picked, table, lift, elements)
     return penalty * (lifted - face_counts() * fields) - jnp.concatenate(rows, axis=0)
 
 
@@ -256,16 +282,16 @@
     for copy in copies:
         copy.start()
     row, lane = iota((512, 128), 0), iota((512, 128), 1)
-    for f in range(6):
-        here = row == face_node(f, lane & 63)
+    for f in range(4):
+        here = row == face_node(f + 2, lane & 63)
         extract_ref[:, f * 128 : (f + 1) * 128] = jnp.where(here, 1.0, 0.0).astype(bf16)
     for copy in copies[:3]:
         copy.wait()
     picked = pick_rows(column(loaded[1]), local_key(loaded[1].shape[1]))
     share_names(loaded[3], picked, shared_ref)
     row, lane = iota((64, 512), 0), iota((64, 512), 1)
-    for f in range(6):
-        here = face_node(f, row) == lane
+    for f in range(4):
+        here = face_node(f + 2, row) == lane
         lift_ref[f * 64 : (f + 1) * 64, :] = jnp.where(here, 1.0, 0.0).astype(bf16)
     row, lane = iota((64, 128), 0), iota((64, 128), 1)
     for f in range(6):
@@ -345,7 +371,7 @@
     table = shared_table(shared_refs, elements).astype(bf16)
     keys = remote_keys(elements)
     picked = pick_faces(column(neigh_ref), keys)
-    terms = dot(facing_pairs(picked, table, elements), lift[...])
+    terms = lift_rows(picked, table, lift[...], elements)
     first = rows_of(base_ref) + (time_step * penalty) * terms
     first_table = face_table(first, extract[...])
     rate = local_rate(
@@ -381,13 +407,13 @@
     sectors = high_ref.shape[1] // (PB * TB * 8)
     shares = lax.axis_size("ax") - 1
     shared_refs = refs[:shares]
-    new_ref, out_refs = refs[shares], refs[shares + 1 : -3]
-    turned_ref, mapped_ref, parts_ref = refs[-3:]
+    new_ref, out_refs = refs[shares], refs[shares + 1 : -2]
+    turned_ref, parts_ref = refs[-2:]
     elements = neigh_ref.shape[1]
     added = added_ref[elements:, :] + shared_table(shared_refs, elements)
     table = jnp.concatenate([added_ref[:elements, :], added], axis=0).astype(bf16)
     picked = pick_faces(column(neigh_ref), remote_keys(elements))
-    terms = dot(facing_pairs(picked, table, elements), lift[...])
+    terms = lift_rows(picked, table, lift[...], elements)
     new_state = rows_of(base_ref) + (0.5 * time_step * penalty) * terms
     new_ref[...] = new_state.reshape(new_ref.shape)
     gap = jnp.zeros((64 - elements, 128), f32)
@@ -398,37 +424,43 @@
             turned_ref[c, j] = jnp.concatenate([part, gap, after, gap], axis=0).T
     radial = radial_ref[...]
     axial = axial_ref[...]
-    for c in range(FIELDS):
-        for yy in range(4):
-            inputs = []
-            for x in range(8):
-                start = (x % 2) * 64 + 16 * yy
-                inputs.append(turned_ref[c, x // 2, start : start + 8, :])
-            for r in range(8):
-                mixed = radial[8 * r : 8 * r + 1, :] * inputs[0]
-                for x in range(1, 8):
-                    mixed = mixed + radial[8 * r + x : 8 * r + x + 1, :] * inputs[x]
-                value = axial[0:8, :] * mixed[0:1, :]
-                for z in range(1, 8):
-                    value = value + axial[8 * z : 8 * z + 8, :] * mixed[z : z + 1, :]
-                row = (c * 8 + r) * 8
-                mapped_ref[row : row + 8, yy * 128 : (yy + 1) * 128] = value
-    mapped_high, mapped_low = split(mapped_ref[...])
     theta_lanes = high_ref.shape[1] // PB
     groups = sectors // PB
     rows = 64 // groups
-    for pb in range(PB):
-        lanes = pl.ds(pb * theta_lanes, theta_lanes)
-        weight_high = high_ref[:, lanes]
-        total = (
+    for pair in range(2):
+        tiles = []
+        for yy in (2 * pair, 2 * pair + 1):
+            values = []
+            for c in range(FIELDS):
+                inputs = []
+                for x in range(8):
+                    start = (x % 2) * 64 + 16 * yy
+                    inputs.append(turned_ref[c, x // 2, start : start + 8, :])
+                for r in range(8):
+                    mixed = radial[8 * r : 8 * r + 1, :] * inputs[0]
+                    for x in range(1, 8):
+                        mixed = mixed + radial[8 * r + x : 8 * r + x + 1, :] * inputs[x]
+                    value = axial[0:8, :] * mixed[0:1, :]
+                    for z in range(1, 8):
+                        value = value + axial[8 * z : 8 * z + 8, :] * mixed[z : z + 1, :]
+                    values.append(value)
+            tiles.append(jnp.concatenate(values, axis=0))
+        mapped_high, mapped_low = split(jnp.concatenate(tiles, axis=1))
+        depth = slice(256 * pair, 256 * pair + 256)
+        weight_high = high_ref[depth, :]
+        part = (
             dot(mapped_high, weight_high)
             + dot(mapped_low, weight_high)
-            + dot(mapped_high, low_ref[:, lanes])
+            + dot(mapped_high, low_ref[depth, :])
         )
+        total = part if pair == 0 else total + part
+    for pb in range(PB):
         for g in range(groups):
             for c in range(FIELDS):
                 start = c * 64 + g * rows
-                parts_ref[pb * groups + g, c * rows : (c + 1) * rows, :] = total[start : start + rows]
+                parts_ref[pb * groups + g, c * rows : (c + 1) * rows, :] = total[
+                    start : start + rows, pb * theta_lanes : (pb + 1) * theta_lanes
+                ]
     owner = lax.axis_index("az")
     relayed, kept = exchange_plan(sectors)
     for i, m in enumerate(relayed):
@@ -510,7 +542,7 @@
     loaded = call(
         load_kernel,
         tuple(shape(a.shape, a.dtype) for a in sources)
-        + (shape((512, 768), bf16), shape((384, 512), bf16), shape((384, 384), bf16))
+        + (shape((512, 512), bf16), shape((256, 512), bf16), shape((384, 384), bf16))
         + (face_rows, shape((travel + 8, 128))),
         *sources,
         scratch=(pltpu.SemaphoreType.DMA((len(sources) - 1 + FIELDS,)),),
@@ -543,7 +575,6 @@
         base, names, added, lift, radial, axial, weight_high, weight_low, *firsts[1:],
         scratch=(
             pltpu.VMEM((FIELDS, 4, 128, 128), f32),
-            pltpu.VMEM((FIELDS * 64, 512), f32),
             pltpu.VMEM((sectors, rows, lanes), f32),
         ),
         flops=800_000_000,

time: 32.2 us -> 31.1 us (0.966)
  Pallas kernels: 11.2 us -> 10.1 us
    pallas_call x7, Pallas kernels: 11.2 us -> 10.1 us  [call(): pl.pallas_call(kernel, out_shape=outs, in_specs=[pl.BlockSpec(memory_spac...]
where the time goes in v5:
time: 31.1 us; the launch traced here: 30.9 us
  starting transfers between devices  15.4 us (50%)
  Pallas kernels  10.1 us (32%)
  waiting for transfers between devices  4.79 us (15%)
  between operations  0.7 us (2%)
    pallas_call x7, Pallas kernels, call(): pl.pallas_call(kernel, out_shape=outs, in_specs=[pl.BlockSpec(memory_spac...  10.1 us
    ppermute x6, starting transfers between devices, swap(): return lax.ppermute(value, 'az', [(i, i ^ mask) for i in range(sectors)])  10 us
    ppermute x6, starting transfers between devices, exchange(): lax.ppermute(value, axis, [(i, i ^ m) for i in range(size)])  5.32 us
    ppermute x6, waiting for transfers between devices, swap(): return lax.ppermute(value, 'az', [(i, i ^ mask) for i in range(sectors)])  4.02 us
    ppermute x6, waiting for transfers between devices, exchange(): lax.ppermute(value, axis, [(i, i ^ m) for i in range(size)])  0.77 us
  transfers between devices with their start and end apart: 12, of which 5 were waited for; matrix products, arithmetic and copies ran while one was open for 0% of the time, Pallas kernels for 17%

profile of v5, /device:TPU:0, one launch (start us, length us, event | category | flops | bytes accessed | tf_op | source)
XLA Modules:
  0.0 30.9 jit_solution(17107268340241147058)
XLA Ops:
  0.6 1.9 %shard_map.104 = (f32[5,48,512]{2,1,0:T(8,128)S(1)}, s32[1,48]{1,0:T(1,128)S(1)}, f32[3,48]{1,0:T(4,128)S(1)}, s32[6,48]{1,0:T(8,128)S(1)}, f32[3,64,48]{2,1,0:T...) custom-call(f32[5,48,512]{2,1,0:T(8,128)} %bitcast.11, ...), custom_call_target="tpu_custom_call" | custom-call | flops 400000000 | bytes 2839040 | tf_op jit(solution)/shard_map/pallas_call | solution.py:506
  2.6 2.5 %collective-permute-start.2 = (f32[128,128]{1,0:T(8,128)S(1)}, f32[128,128]{1,0:T(8,128)S(1)}, u32[]{:S(2)}, u32[]{:S(2)}) collective-permute-start(f32[128,128]{1,0:T(8,128)S(1)} %get-tuple-element.44.refs_0_), channel_id=1, source_target_pairs={{0,3},{1,2},{2,1},{3,0},{4,7},{5,6},{6,5},{7,4},{8,11},{9,10},{10,... | collective-permute-start | bytes 196616 | tf_op jit(solution)/shard_map/ppermute | solution.py:521
  5.1 0.6 %collective-permute-start.1 = (f32[128,128]{1,0:T(8,128)S(1)}, f32[128,128]{1,0:T(8,128)S(1)}, u32[]{:S(2)}, u32[]{:S(2)}) collective-permute-start(f32[128,128]{1,0:T(8,128)S(1)} %get-tuple-element.44.refs_0_), channel_id=1, source_target_pairs={{0,2},{1,3},{2,0},{3,1},{4,6},{5,7},{6,4},{7,5},{8,10},{9,11},{10,... | collective-permute-start | bytes 196616 | tf_op jit(solution)/shard_map/ppermute | solution.py:521
  5.7 0.0 collective-permute-start
  5.7 1.4 %shard_map.105 = (f32[5,48,512]{2,1,0:T(8,128)S(1)}, f32[120,128]{1,0:T(8,128)S(1)}) custom-call(f32[5,48,512]{2,1,0:T(8,128)S(1)} %get-tuple-element.34.state_ref, f32[3,48]{1,0:T(4,128)S(1)} %get-tuple-element.35.velocity_ref, s32[6,48]{1,0:T(8,128)S(1)} %get-tuple-element.36.neigh_ref, s32[1,48]{1,0:T(1,128)S(1)} %get-tuple-element.37.send_ref, ...), custom_call_target="tpu_custom_call" | custom-call | flops 1000000000 | bytes 2332544 | tf_op jit(solution)/shard_map/pallas_call | solution.py:506
  7.2 1.5 %collective-permute-start.5 = (f32[120,128]{1,0:T(8,128)S(1)}, f32[120,128]{1,0:T(8,128)S(1)}, u32[]{:S(2)}, u32[]{:S(2)}) collective-permute-start(f32[120,128]{1,0:T(8,128)S(1)} %get-tuple-element.54), channel_id=1, source_target_pairs={{0,3},{1,2},{2,1},{3,0},{4,7},{5,6},{6,5},{7,4},{8,11},{9,10},{10,... | collective-permute-start | bytes 184328 | tf_op jit(solution)/shard_map/ppermute | solution.py:521
  8.7 0.6 %collective-permute-start.4 = (f32[120,128]{1,0:T(8,128)S(1)}, f32[120,128]{1,0:T(8,128)S(1)}, u32[]{:S(2)}, u32[]{:S(2)}) collective-permute-start(f32[120,128]{1,0:T(8,128)S(1)} %get-tuple-element.54), channel_id=1, source_target_pairs={{0,2},{1,3},{2,0},{3,1},{4,6},{5,7},{6,4},{7,5},{8,10},{9,11},{10,... | collective-permute-start | bytes 184328 | tf_op jit(solution)/shard_map/ppermute | solution.py:521
  9.3 0.0 collective-permute-done.2.refs_3_
  9.3 0.0 collective-permute-start.3
  9.3 0.4 %collective-permute-done.1.refs_2_ = f32[128,128]{1,0:T(8,128)S(1)} collective-permute-done((f32[128,128]{1,0:T(8,128)S(1)}, f32[128,128]{1,0:T(8,128)S(1)}, u32[]{:S(2)}, u32[]{:S(2)}) %collective-permute-start.1) | collective-permute-done | bytes 65568 | tf_op jit(solution)/shard_map/ppermute | solution.py:521
  9.7 0.0 collective-permute-done.refs_1_
  9.7 2.9 %shard_map.106 = (f32[5,48,512]{2,1,0:T(8,128)S(1)}, f32[192,640]{1,0:T(8,128)S(1)}, f32[64,128]{1,0:T(8,128)S(1)}, f32[64,128]{1,0:T(8,128)S(1)}, bf16[512,512]...) custom-call(f32[5,48,512]{2,1,0:T(8,128)S(1)} %get-tuple-element.34.state_ref, ...), custom_call_target="tpu_custom_call" | custom-call | flops 1500000000 | bytes 4593920 | tf_op jit(solution)/shard_map/pallas_call | solution.py:506
  12.7 0.0 collective-permute-done.5.refs_2_
  12.7 0.4 %collective-permute-done.4.refs_1_ = f32[120,128]{1,0:T(8,128)S(1)} collective-permute-done((f32[120,128]{1,0:T(8,128)S(1)}, f32[120,128]{1,0:T(8,128)S(1)}, u32[]{:S(2)}, u32[]{:S(2)}) %collective-permute-start.4) | collective-permute-done | bytes 61472 | tf_op jit(solution)/shard_map/ppermute | solution.py:521
  13.0 0.0 collective-permute-done.3.refs_0_
  13.0 2.1 %shard_map.107 = (f32[5,48,512]{2,1,0:T(8,128)S(1)}, f32[2,160,128]{2,1,0:T(8,128)S(1)}, f32[160,128]{1,0:T(8,128)S(1)}, f32[160,128]{1,0:T(8,128)S(1)}, f32[160...) custom-call(f32[5,48,512]{2,1,0:T(8,128)S(1)} %get-tuple-element.48.base_ref, ...), custom_call_target="tpu_custom_call" | custom-call | flops 800000000 | bytes 3691648 | tf_op jit(solution)/shard_map/pallas_call | solution.py:506
  15.2 1.6 %collective-permute-start.8 = (f32[2,160,128]{2,1,0:T(8,128)S(1)}, f32[2,160,128]{2,1,0:T(8,128)S(1)}, u32[]{:S(2)}, u32[]{:S(2)}) collective-permute-start(f32[2,160,128]{2,1,0:T(8,128)S(1)} %get-tuple-element.58), channel_id=1, source_target_pairs={{0,4},{4,0},{8,12},{12,8},{16,20},{20,16},{24,28},{28,24},{1,5},{5... | collective-permute-start | bytes 491528 | tf_op jit(solution)/shard_map/ppermute | solution.py:588
  16.8 2.6 %collective-permute-start.6 = (f32[160,128]{1,0:T(8,128)S(1)}, f32[160,128]{1,0:T(8,128)S(1)}, u32[]{:S(2)}, u32[]{:S(2)}) collective-permute-start(f32[160,128]{1,0:T(8,128)S(1)} %get-tuple-element.56), channel_id=1, source_target_pairs={{0,16},{4,20},{8,24},{12,28},{16,0},{20,4},{24,8},{28,12},{1,17},{... | collective-permute-start | bytes 245768 | tf_op jit(solution)/shard_map/ppermute | solution.py:588
  19.3 0.3 collective-permute-start.7
  19.6 1.5 %collective-permute-done.8.got_ref = f32[2,160,128]{2,1,0:T(8,128)S(1)} collective-permute-done((f32[2,160,128]{2,1,0:T(8,128)S(1)}, f32[2,160,128]{2,1,0:T(8,128)S(1)}, u32[]{:S(2)}, u32[]{:S(2)}) %collective-permute-start.8) | collective-permute-done | bytes 163872 | tf_op jit(solution)/shard_map/ppermute | solution.py:588
  21.1 3.7 %collective-permute-start.9 = (f32[160,128]{1,0:T(8,128)S(1)}, f32[160,128]{1,0:T(8,128)S(1)}, u32[]{:S(2)}, u32[]{:S(2)}) collective-permute-start(f32[160,128]{1,0:T(8,128)S(1)} %get-tuple-element.62), channel_id=1, source_target_pairs={{0,24},{4,28},{8,16},{12,20},{16,8},{20,12},{24,0},{28,4},{1,25},{... | collective-permute-start | bytes 245768 | tf_op jit(solution)/shard_map/ppermute | solution.py:588
  24.8 0.4 %collective-permute-start.10 = (f32[160,128]{1,0:T(8,128)S(1)}, f32[160,128]{1,0:T(8,128)S(1)}, u32[]{:S(2)}, u32[]{:S(2)}) collective-permute-start(f32[160,128]{1,0:T(8,128)S(1)} %get-tuple-element.63), channel_id=1, source_target_pairs={{0,8},{4,12},{8,0},{12,4},{16,24},{20,28},{24,16},{28,20},{1,9},{5... | collective-permute-start | bytes 245768 | tf_op jit(solution)/shard_map/ppermute | solution.py:588
  25.2 1.5 %collective-permute-start.11 = (f32[160,128]{1,0:T(8,128)S(1)}, f32[160,128]{1,0:T(8,128)S(1)}, u32[]{:S(2)}, u32[]{:S(2)}) collective-permute-start(f32[160,128]{1,0:T(8,128)S(1)} %get-tuple-element.64), channel_id=1, source_target_pairs={{0,4},{4,0},{8,12},{12,8},{16,20},{20,16},{24,28},{28,24},{1,5},{5... | collective-permute-start | bytes 245768 | tf_op jit(solution)/shard_map/ppermute | solution.py:588
  26.7 0.0 copy-start
  26.7 0.8 %shard_map.108 = f32[5,48,512]{2,1,0:T(8,128)} custom-call(f32[5,48,512]{2,1,0:T(8,128)S(1)} %get-tuple-element.55.new_ref), custom_call_target="tpu_custom_call" | custom-call | bytes 983040 | tf_op jit(solution)/shard_map/pallas_call | solution.py:506
  27.5 0.0 collective-permute-done.6.refs_0_
  27.5 1.8 %collective-permute-done.7.refs_1_ = f32[160,128]{1,0:T(8,128)S(1)} collective-permute-done((f32[160,128]{1,0:T(8,128)S(1)}, f32[160,128]{1,0:T(8,128)S(1)}, u32[]{:S(2)}, u32[]{:S(2)}) %collective-permute-start.7) | collective-permute-done | bytes 81952 | tf_op jit(solution)/shard_map/ppermute | solution.py:588
  29.4 0.0 collective-permute-done.9.refs_2_
  29.4 0.7 %collective-permute-done.10.refs_3_ = f32[160,128]{1,0:T(8,128)S(1)} collective-permute-done((f32[160,128]{1,0:T(8,128)S(1)}, f32[160,128]{1,0:T(8,128)S(1)}, u32[]{:S(2)}, u32[]{:S(2)}) %collective-permute-start.10) | collective-permute-done | bytes 81952 | tf_op jit(solution)/shard_map/ppermute | solution.py:588
  30.0 0.0 collective-permute-done.11.refs_4_
  30.1 0.0 copy-done
  30.1 0.9 %shard_map.110 = f32[2,5,32,128]{3,2,1,0:T(8,128)} custom-call(f32[128,256]{1,0:T(8,128)S(1)} %copy-done, f32[160,128]{1,0:T(8,128)S(1)} %collective-permute-done.6.refs_0_, f32[160,128]{1,0:T(8,128)S(1)} %collective-permute-done.7.refs_1_, f32[160,128]{1,0:T(8,128)S(1)} %collective-permute-done.9.refs_2_, f32[160,128]{1,0:T(8,128)S(1)} %collective-permute-done.10.refs_3_, ...), custom_call_target="tpu_custom_call" | custom-call | flops 100000000 | bytes 786432 | tf_op jit(solution)/shard_map/pallas_call | solution.py:506
  (1 shorter events, 0.0 us)
Async XLA Ops:
  2.6 6.7 %collective-permute-start.2 = (f32[128,128]{1,0:T(8,128)S(1)}, f32[128,128]{1,0:T(8,128)S(1)}, u32[]{:S(2)}, u32[]{:S(2)}) collective-permute-start(f32[128,128]{1,0:T(8,128)S(1)} %get-tuple-element.44.refs_0_), channel_id=1, source_target_pairs={{0,3},{1,2},{2,1},{3,0},{4,7},{5,6},{6,5},{7,4},{8,11},{9,10},{10,... | collective-permute-start | bytes 196616 | tf_op jit(solution)/shard_map/ppermute | solution.py:521
  5.1 4.7 %collective-permute-start.1 = (f32[128,128]{1,0:T(8,128)S(1)}, f32[128,128]{1,0:T(8,128)S(1)}, u32[]{:S(2)}, u32[]{:S(2)}) collective-permute-start(f32[128,128]{1,0:T(8,128)S(1)} %get-tuple-element.44.refs_0_), channel_id=1, source_target_pairs={{0,2},{1,3},{2,0},{3,1},{4,6},{5,7},{6,4},{7,5},{8,10},{9,11},{10,... | collective-permute-start | bytes 196616 | tf_op jit(solution)/shard_map/ppermute | solution.py:521
  5.7 4.0 %collective-permute-start = (f32[128,128]{1,0:T(8,128)S(1)}, f32[128,128]{1,0:T(8,128)S(1)}, u32[]{:S(2)}, u32[]{:S(2)}) collective-permute-start(f32[128,128]{1,0:T(8,128)S(1)} %get-tuple-element.44.refs_0_), channel_id=1, source_target_pairs={{0,1},{1,0},{2,3},{3,2},{4,5},{5,4},{6,7},{7,6},{8,9},{9,8},{10,11... | collective-permute-start | bytes 196616 | tf_op jit(solution)/shard_map/ppermute | solution.py:521
  7.2 5.5 %collective-permute-start.5 = (f32[120,128]{1,0:T(8,128)S(1)}, f32[120,128]{1,0:T(8,128)S(1)}, u32[]{:S(2)}, u32[]{:S(2)}) collective-permute-start(f32[120,128]{1,0:T(8,128)S(1)} %get-tuple-element.54), channel_id=1, source_target_pairs={{0,3},{1,2},{2,1},{3,0},{4,7},{5,6},{6,5},{7,4},{8,11},{9,10},{10,... | collective-permute-start | bytes 184328 | tf_op jit(solution)/shard_map/ppermute | solution.py:521
  8.7 4.3 %collective-permute-start.4 = (f32[120,128]{1,0:T(8,128)S(1)}, f32[120,128]{1,0:T(8,128)S(1)}, u32[]{:S(2)}, u32[]{:S(2)}) collective-permute-start(f32[120,128]{1,0:T(8,128)S(1)} %get-tuple-element.54), channel_id=1, source_target_pairs={{0,2},{1,3},{2,0},{3,1},{4,6},{5,7},{6,4},{7,5},{8,10},{9,11},{10,... | collective-permute-start | bytes 184328 | tf_op jit(solution)/shard_map/ppermute | solution.py:521
  9.3 3.7 %collective-permute-start.3 = (f32[120,128]{1,0:T(8,128)S(1)}, f32[120,128]{1,0:T(8,128)S(1)}, u32[]{:S(2)}, u32[]{:S(2)}) collective-permute-start(f32[120,128]{1,0:T(8,128)S(1)} %get-tuple-element.54), channel_id=1, source_target_pairs={{0,1},{1,0},{2,3},{3,2},{4,5},{5,4},{6,7},{7,6},{8,9},{9,8},{10,11... | collective-permute-start | bytes 184328 | tf_op jit(solution)/shard_map/ppermute | solution.py:521
  15.2 5.9 %collective-permute-start.8 = (f32[2,160,128]{2,1,0:T(8,128)S(1)}, f32[2,160,128]{2,1,0:T(8,128)S(1)}, u32[]{:S(2)}, u32[]{:S(2)}) collective-permute-start(f32[2,160,128]{2,1,0:T(8,128)S(1)} %get-tuple-element.58), channel_id=1, source_target_pairs={{0,4},{4,0},{8,12},{12,8},{16,20},{20,16},{24,28},{28,24},{1,5},{5... | collective-permute-start | bytes 491528 | tf_op jit(solution)/shard_map/ppermute | solution.py:588
  16.8 10.8 %collective-permute-start.6 = (f32[160,128]{1,0:T(8,128)S(1)}, f32[160,128]{1,0:T(8,128)S(1)}, u32[]{:S(2)}, u32[]{:S(2)}) collective-permute-start(f32[160,128]{1,0:T(8,128)S(1)} %get-tuple-element.56), channel_id=1, source_target_pairs={{0,16},{4,20},{8,24},{12,28},{16,0},{20,4},{24,8},{28,12},{1,17},{... | collective-permute-start | bytes 245768 | tf_op jit(solution)/shard_map/ppermute | solution.py:588
  19.3 10.0 %collective-permute-start.7 = (f32[160,128]{1,0:T(8,128)S(1)}, f32[160,128]{1,0:T(8,128)S(1)}, u32[]{:S(2)}, u32[]{:S(2)}) collective-permute-start(f32[160,128]{1,0:T(8,128)S(1)} %get-tuple-element.57), channel_id=1, source_target_pairs={{0,20},{4,16},{8,28},{12,24},{16,4},{20,0},{24,12},{28,8},{1,21},{... | collective-permute-start | bytes 245768 | tf_op jit(solution)/shard_map/ppermute | solution.py:588
  21.1 8.2 %collective-permute-start.9 = (f32[160,128]{1,0:T(8,128)S(1)}, f32[160,128]{1,0:T(8,128)S(1)}, u32[]{:S(2)}, u32[]{:S(2)}) collective-permute-start(f32[160,128]{1,0:T(8,128)S(1)} %get-tuple-element.62), channel_id=1, source_target_pairs={{0,24},{4,28},{8,16},{12,20},{16,8},{20,12},{24,0},{28,4},{1,25},{... | collective-permute-start | bytes 245768 | tf_op jit(solution)/shard_map/ppermute | solution.py:588
  24.8 5.3 %collective-permute-start.10 = (f32[160,128]{1,0:T(8,128)S(1)}, f32[160,128]{1,0:T(8,128)S(1)}, u32[]{:S(2)}, u32[]{:S(2)}) collective-permute-start(f32[160,128]{1,0:T(8,128)S(1)} %get-tuple-element.63), channel_id=1, source_target_pairs={{0,8},{4,12},{8,0},{12,4},{16,24},{20,28},{24,16},{28,20},{1,9},{5... | collective-permute-start | bytes 245768 | tf_op jit(solution)/shard_map/ppermute | solution.py:588
  25.2 4.8 %collective-permute-start.11 = (f32[160,128]{1,0:T(8,128)S(1)}, f32[160,128]{1,0:T(8,128)S(1)}, u32[]{:S(2)}, u32[]{:S(2)}) collective-permute-start(f32[160,128]{1,0:T(8,128)S(1)} %get-tuple-element.64), channel_id=1, source_target_pairs={{0,4},{4,0},{8,12},{12,8},{16,20},{20,16},{24,28},{28,24},{1,5},{5... | collective-permute-start | bytes 245768 | tf_op jit(solution)/shard_map/ppermute | solution.py:588
  26.7 3.3 %copy-start = (f32[128,256]{1,0:T(8,128)S(1)}, f32[128,256]{1,0:T(8,128)}, u32[]{:S(2)}) copy-start(f32[128,256]{1,0:T(8,128)} %constant.5.clone.table_ref) | copy-start | bytes 393220

commit v6 on v5

--- a/solution.py
+++ b/solution.py
@@ -69,6 +69,10 @@
 def split(value):
     high = value.astype(bf16)
     return high, (value - high.astype(f32)).astype(bf16)
+
+
+def remainder(value):
+    return value - value.astype(bf16).astype(f32)
 
 
 def dot(a, b):
@@ -317,7 +321,7 @@
     base = fields + time_step * rate
     out_ref[...] = base.reshape(out_ref.shape)
     picked = pick_rows(column(send_ref), local_key(send_ref.shape[1]))
-    share_rows(face_table(base, extract[...]), picked, shared_ref)
+    share_rows(face_table(base + remainder(fields), extract[...]), picked, shared_ref)
 
 
 def fill_maps(
@@ -373,7 +377,7 @@
     picked = pick_faces(column(neigh_ref), keys)
     terms = lift_rows(picked, table, lift[...], elements)
     first = rows_of(base_ref) + (time_step * penalty) * terms
-    first_table = face_table(first, extract[...])
+    first_table = face_table(first + remainder(rows_of(state_ref)), extract[...])
     rate = local_rate(
         first, velocity_ref, neigh_ref, first_table, *split(yz[...]), lift[...]
     )
@@ -435,14 +439,15 @@
                 inputs = []
                 for x in range(8):
                     start = (x % 2) * 64 + 16 * yy
-                    inputs.append(turned_ref[c, x // 2, start : start + 8, :])
+                    value = axial[0:8, :] * turned_ref[c, x // 2, start : start + 1, :]
+                    for z in range(1, 8):
+                        row = turned_ref[c, x // 2, start + z : start + z + 1, :]
+                        value = value + axial[8 * z : 8 * z + 8, :] * row
+                    inputs.append(value)
                 for r in range(8):
-                    mixed = radial[8 * r : 8 * r + 1, :] * inputs[0]
+                    value = radial_ref[8 * r : 8 * r + 1, :] * inputs[0]
                     for x in range(1, 8):
-                        mixed = mixed + radial[8 * r + x : 8 * r + x + 1, :] * inputs[x]
-                    value = axial[0:8, :] * mixed[0:1, :]
-                    for z in range(1, 8):
-                        value = value + axial[8 * z : 8 * z + 8, :] * mixed[z : z + 1, :]
+                        value = value + radial_ref[8 * r + x : 8 * r + x + 1, :] * inputs[x]
                     values.append(value)
             tiles.append(jnp.concatenate(values, axis=0))
         mapped_high, mapped_low = split(jnp.concatenate(tiles, axis=1))

time: 31.1 us -> 31.1 us (level)
  no operation moved by 1% of the time
where the time goes in v6:
time: 31.1 us; the launch traced here: 30.9 us
  starting transfers between devices  15.4 us (50%)
  Pallas kernels  10.1 us (32%)
  waiting for transfers between devices  4.82 us (15%)
  between operations  0.7 us (2%)
    pallas_call x7, Pallas kernels, call(): pl.pallas_call(kernel, out_shape=outs, in_specs=[pl.BlockSpec(memory_spac...  10.1 us
    ppermute x6, starting transfers between devices, swap(): return lax.ppermute(value, 'az', [(i, i ^ mask) for i in range(sectors)])  10 us
    ppermute x6, starting transfers between devices, exchange(): lax.ppermute(value, axis, [(i, i ^ m) for i in range(size)])  5.32 us
    ppermute x6, waiting for transfers between devices, swap(): return lax.ppermute(value, 'az', [(i, i ^ mask) for i in range(sectors)])  4.11 us
    ppermute x6, waiting for transfers between devices, exchange(): lax.ppermute(value, axis, [(i, i ^ m) for i in range(size)])  0.71 us
  transfers between devices with their start and end apart: 12, of which 5 were waited for; matrix products, arithmetic and copies ran while one was open for 0% of the time, Pallas kernels for 17%

profile of v6, /device:TPU:0, one launch (start us, length us, event | category | flops | bytes accessed | tf_op | source)
XLA Modules:
  0.0 30.9 jit_solution(10352572941765729071)
XLA Ops:
  0.6 1.9 %shard_map.104 = (f32[5,48,512]{2,1,0:T(8,128)S(1)}, s32[1,48]{1,0:T(1,128)S(1)}, f32[3,48]{1,0:T(4,128)S(1)}, s32[6,48]{1,0:T(8,128)S(1)}, f32[3,64,48]{2,1,0:T...) custom-call(f32[5,48,512]{2,1,0:T(8,128)} %bitcast.11, ...), custom_call_target="tpu_custom_call" | custom-call | flops 400000000 | bytes 2839040 | tf_op jit(solution)/shard_map/pallas_call | solution.py:511
  2.6 2.5 %collective-permute-start.2 = (f32[128,128]{1,0:T(8,128)S(1)}, f32[128,128]{1,0:T(8,128)S(1)}, u32[]{:S(2)}, u32[]{:S(2)}) collective-permute-start(f32[128,128]{1,0:T(8,128)S(1)} %get-tuple-element.44.refs_0_), channel_id=1, source_target_pairs={{0,3},{1,2},{2,1},{3,0},{4,7},{5,6},{6,5},{7,4},{8,11},{9,10},{10,... | collective-permute-start | bytes 196616 | tf_op jit(solution)/shard_map/ppermute | solution.py:526
  5.1 0.6 %collective-permute-start.1 = (f32[128,128]{1,0:T(8,128)S(1)}, f32[128,128]{1,0:T(8,128)S(1)}, u32[]{:S(2)}, u32[]{:S(2)}) collective-permute-start(f32[128,128]{1,0:T(8,128)S(1)} %get-tuple-element.44.refs_0_), channel_id=1, source_target_pairs={{0,2},{1,3},{2,0},{3,1},{4,6},{5,7},{6,4},{7,5},{8,10},{9,11},{10,... | collective-permute-start | bytes 196616 | tf_op jit(solution)/shard_map/ppermute | solution.py:526
  5.7 0.0 collective-permute-start
  5.7 1.4 %shard_map.105 = (f32[5,48,512]{2,1,0:T(8,128)S(1)}, f32[120,128]{1,0:T(8,128)S(1)}) custom-call(f32[5,48,512]{2,1,0:T(8,128)S(1)} %get-tuple-element.34.state_ref, f32[3,48]{1,0:T(4,128)S(1)} %get-tuple-element.35.velocity_ref, s32[6,48]{1,0:T(8,128)S(1)} %get-tuple-element.36.neigh_ref, s32[1,48]{1,0:T(1,128)S(1)} %get-tuple-element.37.send_ref, ...), custom_call_target="tpu_custom_call" | custom-call | flops 1000000000 | bytes 2332544 | tf_op jit(solution)/shard_map/pallas_call | solution.py:511
  7.2 1.5 %collective-permute-start.5 = (f32[120,128]{1,0:T(8,128)S(1)}, f32[120,128]{1,0:T(8,128)S(1)}, u32[]{:S(2)}, u32[]{:S(2)}) collective-permute-start(f32[120,128]{1,0:T(8,128)S(1)} %get-tuple-element.54), channel_id=1, source_target_pairs={{0,3},{1,2},{2,1},{3,0},{4,7},{5,6},{6,5},{7,4},{8,11},{9,10},{10,... | collective-permute-start | bytes 184328 | tf_op jit(solution)/shard_map/ppermute | solution.py:526
  8.7 0.6 %collective-permute-start.4 = (f32[120,128]{1,0:T(8,128)S(1)}, f32[120,128]{1,0:T(8,128)S(1)}, u32[]{:S(2)}, u32[]{:S(2)}) collective-permute-start(f32[120,128]{1,0:T(8,128)S(1)} %get-tuple-element.54), channel_id=1, source_target_pairs={{0,2},{1,3},{2,0},{3,1},{4,6},{5,7},{6,4},{7,5},{8,10},{9,11},{10,... | collective-permute-start | bytes 184328 | tf_op jit(solution)/shard_map/ppermute | solution.py:526
  9.4 0.0 collective-permute-done.2.refs_3_
  9.4 0.0 collective-permute-start.3
  9.4 0.4 %collective-permute-done.1.refs_2_ = f32[128,128]{1,0:T(8,128)S(1)} collective-permute-done((f32[128,128]{1,0:T(8,128)S(1)}, f32[128,128]{1,0:T(8,128)S(1)}, u32[]{:S(2)}, u32[]{:S(2)}) %collective-permute-start.1) | collective-permute-done | bytes 65568 | tf_op jit(solution)/shard_map/ppermute | solution.py:526
  9.7 0.0 collective-permute-done.refs_1_
  9.7 3.0 %shard_map.106 = (f32[5,48,512]{2,1,0:T(8,128)S(1)}, f32[192,640]{1,0:T(8,128)S(1)}, f32[64,128]{1,0:T(8,128)S(1)}, f32[64,128]{1,0:T(8,128)S(1)}, bf16[512,512]...) custom-call(f32[5,48,512]{2,1,0:T(8,128)S(1)} %get-tuple-element.34.state_ref, ...), custom_call_target="tpu_custom_call" | custom-call | flops 1500000000 | bytes 4593920 | tf_op jit(solution)/shard_map/pallas_call | solution.py:511
  12.7 0.0 collective-permute-done.5.refs_2_
  12.7 0.3 %collective-permute-done.4.refs_1_ = f32[120,128]{1,0:T(8,128)S(1)} collective-permute-done((f32[120,128]{1,0:T(8,128)S(1)}, f32[120,128]{1,0:T(8,128)S(1)}, u32[]{:S(2)}, u32[]{:S(2)}) %collective-permute-start.4) | collective-permute-done | bytes 61472 | tf_op jit(solution)/shard_map/ppermute | solution.py:526
  13.1 0.0 collective-permute-done.3.refs_0_
  13.1 2.0 %shard_map.107 = (f32[5,48,512]{2,1,0:T(8,128)S(1)}, f32[2,160,128]{2,1,0:T(8,128)S(1)}, f32[160,128]{1,0:T(8,128)S(1)}, f32[160,128]{1,0:T(8,128)S(1)}, f32[160...) custom-call(f32[5,48,512]{2,1,0:T(8,128)S(1)} %get-tuple-element.48.base_ref, ...), custom_call_target="tpu_custom_call" | custom-call | flops 800000000 | bytes 3691648 | tf_op jit(solution)/shard_map/pallas_call | solution.py:511
  15.1 1.6 %collective-permute-start.8 = (f32[2,160,128]{2,1,0:T(8,128)S(1)}, f32[2,160,128]{2,1,0:T(8,128)S(1)}, u32[]{:S(2)}, u32[]{:S(2)}) collective-permute-start(f32[2,160,128]{2,1,0:T(8,128)S(1)} %get-tuple-element.58), channel_id=1, source_target_pairs={{0,4},{4,0},{8,12},{12,8},{16,20},{20,16},{24,28},{28,24},{1,5},{5... | collective-permute-start | bytes 491528 | tf_op jit(solution)/shard_map/ppermute | solution.py:593
  16.7 2.6 %collective-permute-start.6 = (f32[160,128]{1,0:T(8,128)S(1)}, f32[160,128]{1,0:T(8,128)S(1)}, u32[]{:S(2)}, u32[]{:S(2)}) collective-permute-start(f32[160,128]{1,0:T(8,128)S(1)} %get-tuple-element.56), channel_id=1, source_target_pairs={{0,16},{4,20},{8,24},{12,28},{16,0},{20,4},{24,8},{28,12},{1,17},{... | collective-permute-start | bytes 245768 | tf_op jit(solution)/shard_map/ppermute | solution.py:593
  19.3 0.3 collective-permute-start.7
  19.5 1.6 %collective-permute-done.8.got_ref = f32[2,160,128]{2,1,0:T(8,128)S(1)} collective-permute-done((f32[2,160,128]{2,1,0:T(8,128)S(1)}, f32[2,160,128]{2,1,0:T(8,128)S(1)}, u32[]{:S(2)}, u32[]{:S(2)}) %collective-permute-start.8) | collective-permute-done | bytes 163872 | tf_op jit(solution)/shard_map/ppermute | solution.py:593
  21.1 3.6 %collective-permute-start.9 = (f32[160,128]{1,0:T(8,128)S(1)}, f32[160,128]{1,0:T(8,128)S(1)}, u32[]{:S(2)}, u32[]{:S(2)}) collective-permute-start(f32[160,128]{1,0:T(8,128)S(1)} %get-tuple-element.62), channel_id=1, source_target_pairs={{0,24},{4,28},{8,16},{12,20},{16,8},{20,12},{24,0},{28,4},{1,25},{... | collective-permute-start | bytes 245768 | tf_op jit(solution)/shard_map/ppermute | solution.py:593
  24.8 0.4 %collective-permute-start.10 = (f32[160,128]{1,0:T(8,128)S(1)}, f32[160,128]{1,0:T(8,128)S(1)}, u32[]{:S(2)}, u32[]{:S(2)}) collective-permute-start(f32[160,128]{1,0:T(8,128)S(1)} %get-tuple-element.63), channel_id=1, source_target_pairs={{0,8},{4,12},{8,0},{12,4},{16,24},{20,28},{24,16},{28,20},{1,9},{5... | collective-permute-start | bytes 245768 | tf_op jit(solution)/shard_map/ppermute | solution.py:593
  25.1 1.5 %collective-permute-start.11 = (f32[160,128]{1,0:T(8,128)S(1)}, f32[160,128]{1,0:T(8,128)S(1)}, u32[]{:S(2)}, u32[]{:S(2)}) collective-permute-start(f32[160,128]{1,0:T(8,128)S(1)} %get-tuple-element.64), channel_id=1, source_target_pairs={{0,4},{4,0},{8,12},{12,8},{16,20},{20,16},{24,28},{28,24},{1,5},{5... | collective-permute-start | bytes 245768 | tf_op jit(solution)/shard_map/ppermute | solution.py:593
  26.7 0.0 copy-start
  26.7 0.8 %shard_map.108 = f32[5,48,512]{2,1,0:T(8,128)} custom-call(f32[5,48,512]{2,1,0:T(8,128)S(1)} %get-tuple-element.55.new_ref), custom_call_target="tpu_custom_call" | custom-call | bytes 983040 | tf_op jit(solution)/shard_map/pallas_call | solution.py:511
  27.5 0.0 collective-permute-done.6.refs_0_
  27.5 1.8 %collective-permute-done.7.refs_1_ = f32[160,128]{1,0:T(8,128)S(1)} collective-permute-done((f32[160,128]{1,0:T(8,128)S(1)}, f32[160,128]{1,0:T(8,128)S(1)}, u32[]{:S(2)}, u32[]{:S(2)}) %collective-permute-start.7) | collective-permute-done | bytes 81952 | tf_op jit(solution)/shard_map/ppermute | solution.py:593
  29.3 0.0 collective-permute-done.9.refs_2_
  29.3 0.7 %collective-permute-done.10.refs_3_ = f32[160,128]{1,0:T(8,128)S(1)} collective-permute-done((f32[160,128]{1,0:T(8,128)S(1)}, f32[160,128]{1,0:T(8,128)S(1)}, u32[]{:S(2)}, u32[]{:S(2)}) %collective-permute-start.10) | collective-permute-done | bytes 81952 | tf_op jit(solution)/shard_map/ppermute | solution.py:593
  30.0 0.0 collective-permute-done.11.refs_4_
  30.1 0.0 copy-done
  30.1 0.9 %shard_map.110 = f32[2,5,32,128]{3,2,1,0:T(8,128)} custom-call(f32[128,256]{1,0:T(8,128)S(1)} %copy-done, f32[160,128]{1,0:T(8,128)S(1)} %collective-permute-done.6.refs_0_, f32[160,128]{1,0:T(8,128)S(1)} %collective-permute-done.7.refs_1_, f32[160,128]{1,0:T(8,128)S(1)} %collective-permute-done.9.refs_2_, f32[160,128]{1,0:T(8,128)S(1)} %collective-permute-done.10.refs_3_, ...), custom_call_target="tpu_custom_call" | custom-call | flops 100000000 | bytes 786432 | tf_op jit(solution)/shard_map/pallas_call | solution.py:511
  (1 shorter events, 0.0 us)
Async XLA Ops:
  2.6 6.8 %collective-permute-start.2 = (f32[128,128]{1,0:T(8,128)S(1)}, f32[128,128]{1,0:T(8,128)S(1)}, u32[]{:S(2)}, u32[]{:S(2)}) collective-permute-start(f32[128,128]{1,0:T(8,128)S(1)} %get-tuple-element.44.refs_0_), channel_id=1, source_target_pairs={{0,3},{1,2},{2,1},{3,0},{4,7},{5,6},{6,5},{7,4},{8,11},{9,10},{10,... | collective-permute-start | bytes 196616 | tf_op jit(solution)/shard_map/ppermute | solution.py:526
  5.1 4.7 %collective-permute-start.1 = (f32[128,128]{1,0:T(8,128)S(1)}, f32[128,128]{1,0:T(8,128)S(1)}, u32[]{:S(2)}, u32[]{:S(2)}) collective-permute-start(f32[128,128]{1,0:T(8,128)S(1)} %get-tuple-element.44.refs_0_), channel_id=1, source_target_pairs={{0,2},{1,3},{2,0},{3,1},{4,6},{5,7},{6,4},{7,5},{8,10},{9,11},{10,... | collective-permute-start | bytes 196616 | tf_op jit(solution)/shard_map/ppermute | solution.py:526
  5.7 4.0 %collective-permute-start = (f32[128,128]{1,0:T(8,128)S(1)}, f32[128,128]{1,0:T(8,128)S(1)}, u32[]{:S(2)}, u32[]{:S(2)}) collective-permute-start(f32[128,128]{1,0:T(8,128)S(1)} %get-tuple-element.44.refs_0_), channel_id=1, source_target_pairs={{0,1},{1,0},{2,3},{3,2},{4,5},{5,4},{6,7},{7,6},{8,9},{9,8},{10,11... | collective-permute-start | bytes 196616 | tf_op jit(solution)/shard_map/ppermute | solution.py:526
  7.2 5.5 %collective-permute-start.5 = (f32[120,128]{1,0:T(8,128)S(1)}, f32[120,128]{1,0:T(8,128)S(1)}, u32[]{:S(2)}, u32[]{:S(2)}) collective-permute-start(f32[120,128]{1,0:T(8,128)S(1)} %get-tuple-element.54), channel_id=1, source_target_pairs={{0,3},{1,2},{2,1},{3,0},{4,7},{5,6},{6,5},{7,4},{8,11},{9,10},{10,... | collective-permute-start | bytes 184328 | tf_op jit(solution)/shard_map/ppermute | solution.py:526
  8.7 4.3 %collective-permute-start.4 = (f32[120,128]{1,0:T(8,128)S(1)}, f32[120,128]{1,0:T(8,128)S(1)}, u32[]{:S(2)}, u32[]{:S(2)}) collective-permute-start(f32[120,128]{1,0:T(8,128)S(1)} %get-tuple-element.54), channel_id=1, source_target_pairs={{0,2},{1,3},{2,0},{3,1},{4,6},{5,7},{6,4},{7,5},{8,10},{9,11},{10,... | collective-permute-start | bytes 184328 | tf_op jit(solution)/shard_map/ppermute | solution.py:526
  9.4 3.7 %collective-permute-start.3 = (f32[120,128]{1,0:T(8,128)S(1)}, f32[120,128]{1,0:T(8,128)S(1)}, u32[]{:S(2)}, u32[]{:S(2)}) collective-permute-start(f32[120,128]{1,0:T(8,128)S(1)} %get-tuple-element.54), channel_id=1, source_target_pairs={{0,1},{1,0},{2,3},{3,2},{4,5},{5,4},{6,7},{7,6},{8,9},{9,8},{10,11... | collective-permute-start | bytes 184328 | tf_op jit(solution)/shard_map/ppermute | solution.py:526
  15.1 6.0 %collective-permute-start.8 = (f32[2,160,128]{2,1,0:T(8,128)S(1)}, f32[2,160,128]{2,1,0:T(8,128)S(1)}, u32[]{:S(2)}, u32[]{:S(2)}) collective-permute-start(f32[2,160,128]{2,1,0:T(8,128)S(1)} %get-tuple-element.58), channel_id=1, source_target_pairs={{0,4},{4,0},{8,12},{12,8},{16,20},{20,16},{24,28},{28,24},{1,5},{5... | collective-permute-start | bytes 491528 | tf_op jit(solution)/shard_map/ppermute | solution.py:593
  16.7 10.8 %collective-permute-start.6 = (f32[160,128]{1,0:T(8,128)S(1)}, f32[160,128]{1,0:T(8,128)S(1)}, u32[]{:S(2)}, u32[]{:S(2)}) collective-permute-start(f32[160,128]{1,0:T(8,128)S(1)} %get-tuple-element.56), channel_id=1, source_target_pairs={{0,16},{4,20},{8,24},{12,28},{16,0},{20,4},{24,8},{28,12},{1,17},{... | collective-permute-start | bytes 245768 | tf_op jit(solution)/shard_map/ppermute | solution.py:593
  19.3 10.1 %collective-permute-start.7 = (f32[160,128]{1,0:T(8,128)S(1)}, f32[160,128]{1,0:T(8,128)S(1)}, u32[]{:S(2)}, u32[]{:S(2)}) collective-permute-start(f32[160,128]{1,0:T(8,128)S(1)} %get-tuple-element.57), channel_id=1, source_target_pairs={{0,20},{4,16},{8,28},{12,24},{16,4},{20,0},{24,12},{28,8},{1,21},{... | collective-permute-start | bytes 245768 | tf_op jit(solution)/shard_map/ppermute | solution.py:593
  21.1 8.2 %collective-permute-start.9 = (f32[160,128]{1,0:T(8,128)S(1)}, f32[160,128]{1,0:T(8,128)S(1)}, u32[]{:S(2)}, u32[]{:S(2)}) collective-permute-start(f32[160,128]{1,0:T(8,128)S(1)} %get-tuple-element.62), channel_id=1, source_target_pairs={{0,24},{4,28},{8,16},{12,20},{16,8},{20,12},{24,0},{28,4},{1,25},{... | collective-permute-start | bytes 245768 | tf_op jit(solution)/shard_map/ppermute | solution.py:593
  24.8 5.3 %collective-permute-start.10 = (f32[160,128]{1,0:T(8,128)S(1)}, f32[160,128]{1,0:T(8,128)S(1)}, u32[]{:S(2)}, u32[]{:S(2)}) collective-permute-start(f32[160,128]{1,0:T(8,128)S(1)} %get-tuple-element.63), channel_id=1, source_target_pairs={{0,8},{4,12},{8,0},{12,4},{16,24},{20,28},{24,16},{28,20},{1,9},{5... | collective-permute-start | bytes 245768 | tf_op jit(solution)/shard_map/ppermute | solution.py:593
  25.1 4.9 %collective-permute-start.11 = (f32[160,128]{1,0:T(8,128)S(1)}, f32[160,128]{1,0:T(8,128)S(1)}, u32[]{:S(2)}, u32[]{:S(2)}) collective-permute-start(f32[160,128]{1,0:T(8,128)S(1)} %get-tuple-element.64), channel_id=1, source_target_pairs={{0,4},{4,0},{8,12},{12,8},{16,20},{20,16},{24,28},{28,24},{1,5},{5... | collective-permute-start | bytes 245768 | tf_op jit(solution)/shard_map/ppermute | solution.py:593
  26.7 3.4 %copy-start = (f32[128,256]{1,0:T(8,128)S(1)}, f32[128,256]{1,0:T(8,128)}, u32[]{:S(2)}) copy-start(f32[128,256]{1,0:T(8,128)} %constant.5.clone.table_ref) | copy-start | bytes 393220

commit v7 on v6

--- a/solution.py
+++ b/solution.py
@@ -151,22 +151,15 @@
     return jnp.concatenate(fields, axis=1)
 
 
-def share_names(names_ref, picked, out_ref):
-    elements = picked.shape[0]
-    lane = iota((1, 6 * elements), 1)
-    face = jnp.zeros_like(lane)
-    for f in range(1, 6):
-        face = face + (lane >= f * elements).astype(jnp.int32)
-    tile = (iota((elements, 6 * elements), 0) == lane - face * elements).astype(f32)
-    names = jnp.dot(
-        names_ref[...].astype(f32), tile, precision=highest, preferred_element_type=f32
-    )
-    rows = jnp.concatenate([names, face.astype(f32), jnp.zeros((1, 6 * elements), f32)], axis=0)
+def share_names(names_ref, send_ref, out_ref):
+    elements = send_ref.shape[1]
+    sends = send_ref[...].astype(f32)
+    element = jnp.floor((sends + 0.5) * (1.0 / 6.0))
+    chosen = (iota((elements, elements), 0).astype(f32) == element).astype(f32).astype(bf16)
+    names = jnp.concatenate([names_ref[...].astype(f32), jnp.zeros((2, elements), f32)], axis=0)
     out_ref[-8:, :] = jnp.zeros((8, 128), f32)
-    out_ref[-8:, :elements] = lax.dot_general(
-        rows, picked.astype(f32), (((1,), (1,)), ((), ())),
-        precision=highest, preferred_element_type=f32,
-    )
+    out_ref[-8:, :elements] = exact_dot(names, chosen)
+    out_ref[-2:-1, :elements] = sends - 6.0 * element
 
 
 def facing_pairs(picked, table, elements):
@@ -281,7 +274,7 @@
     fields = [(pairs[0][0].at[c], pairs[0][1].at[c]) for c in range(FIELDS)]
     copies = [
         pltpu.make_async_copy(source, target, sems.at[i])
-        for i, (source, target) in enumerate(pairs[1:4] + fields + pairs[4:])
+        for i, (source, target) in enumerate(pairs[1:2] + pairs[3:4] + fields + pairs[2:3] + pairs[4:])
     ]
     for copy in copies:
         copy.start()
@@ -289,10 +282,10 @@
     for f in range(4):
         here = row == face_node(f + 2, lane & 63)
         extract_ref[:, f * 128 : (f + 1) * 128] = jnp.where(here, 1.0, 0.0).astype(bf16)
-    for copy in copies[:3]:
+    for copy in copies[:2]:
         copy.wait()
     picked = pick_rows(column(loaded[1]), local_key(loaded[1].shape[1]))
-    share_names(loaded[3], picked, shared_ref)
+    share_names(loaded[3], loaded[1], shared_ref)
     row, lane = iota((64, 512), 0), iota((64, 512), 1)
     for f in range(4):
         here = face_node(f + 2, row) == lane
@@ -304,11 +297,13 @@
             cross_ref[f * 64 : (f + 1) * 64, g * 64 : (g + 2) * 64] = jnp.where(
                 face_node(f, row) == node, 1.0, 0.0
             ).astype(bf16)
-    for copy in copies[3:]:
+    for copy in copies[2 : 2 + FIELDS]:
         copy.wait()
     table = face_table(rows_of(loaded[0]), extract_ref[...])
     table_ref[...] = table
     share_rows(table, picked, shared_ref)
+    for copy in copies[2 + FIELDS :]:
+        copy.wait()
 
 
 def first_local_kernel(
@@ -369,12 +364,14 @@
 def second_local_kernel(
     state_ref, base_ref, velocity_ref, neigh_ref, send_ref, yz, lift, extract, cross, *refs
 ):
-    shared_refs, map_refs, (out_ref, added_ref) = refs[:-9], refs[-9:-6] + refs[-4:], refs[-6:-4]
+    shared_refs, map_refs = refs[:-10], refs[-10:-7] + refs[-4:]
+    out_ref, added_ref, picked_ref = refs[-7:-4]
     fill_maps(*map_refs)
     elements = neigh_ref.shape[1]
     table = shared_table(shared_refs, elements).astype(bf16)
     keys = remote_keys(elements)
     picked = pick_faces(column(neigh_ref), keys)
+    picked_ref[...] = picked
     terms = lift_rows(picked, table, lift[...], elements)
     first = rows_of(base_ref) + (time_step * penalty) * terms
     first_table = face_table(first + remainder(rows_of(state_ref)), extract[...])
@@ -406,18 +403,17 @@
 
 
 def sample_kernel(
-    base_ref, neigh_ref, added_ref, lift, radial_ref, axial_ref, high_ref, low_ref, *refs
+    base_ref, picked_ref, added_ref, lift, radial_ref, axial_ref, high_ref, low_ref, *refs
 ):
     sectors = high_ref.shape[1] // (PB * TB * 8)
     shares = lax.axis_size("ax") - 1
     shared_refs = refs[:shares]
     new_ref, out_refs = refs[shares], refs[shares + 1 : -2]
     turned_ref, parts_ref = refs[-2:]
-    elements = neigh_ref.shape[1]
+    elements = base_ref.shape[1]
     added = added_ref[elements:, :] + shared_table(shared_refs, elements)
     table = jnp.concatenate([added_ref[:elements, :], added], axis=0).astype(bf16)
-    picked = pick_faces(column(neigh_ref), remote_keys(elements))
-    terms = lift_rows(picked, table, lift[...], elements)
+    terms = lift_rows(picked_ref[...], table, lift[...], elements)
     new_state = rows_of(base_ref) + (0.5 * time_step * penalty) * terms
     new_ref[...] = new_state.reshape(new_ref.shape)
     gap = jnp.zeros((64 - elements, 128), f32)
@@ -565,10 +561,10 @@
     firsts = exchange(shared, "ax")
     lanes = sectors * TB * 8
     weights = shape((512, PB * lanes), bf16)
-    base, added, radial, axial, weight_high, weight_low = call(
+    base, added, picked, radial, axial, weight_high, weight_low = call(
         second_local_kernel,
         (cube, shape((lax.axis_size("ax") * elements, FIELDS * 128)))
-        + (shape((64, 128)), shape((64, 128)), weights, weights),
+        + (shape((6 * elements, lax.axis_size("ax") * elements), bf16), shape((64, 128)), shape((64, 128)), weights, weights),
         fields, base, speed, names, sends, yz, lift, extract, cross, *others, maps, places, blocks,
         flops=1_500_000_000,
     )
@@ -577,7 +573,7 @@
     relayed, kept = exchange_plan(sectors)
     sampled = call(
         sample_kernel, (cube, shape((len(relayed), rows, lanes))) + (piece,) * len(kept),
-        base, names, added, lift, radial, axial, weight_high, weight_low, *firsts[1:],
+        base, picked, added, lift, radial, axial, weight_high, weight_low, *firsts[1:],
         scratch=(
             pltpu.VMEM((FIELDS, 4, 128, 128), f32),
             pltpu.VMEM((sectors, rows, lanes), f32),

time: 31.1 us -> 30.9 us (level)
  Pallas kernels: 10.1 us -> 9.77 us
where the time goes in v7:
time: 30.9 us; the launch traced here: 30.7 us
  starting transfers between devices  15.4 us (50%)
  Pallas kernels  9.77 us (32%)
  waiting for transfers between devices  4.89 us (16%)
  between operations  0.7 us (2%)
    ppermute x6, starting transfers between devices, swap(): return lax.ppermute(value, 'az', [(i, i ^ mask) for i in range(sectors)])  10 us
    pallas_call x7, Pallas kernels, call(): pl.pallas_call(kernel, out_shape=outs, in_specs=[pl.BlockSpec(memory_spac...  9.77 us
    ppermute x6, starting transfers between devices, exchange(): lax.ppermute(value, axis, [(i, i ^ m) for i in range(size)])  5.32 us
    ppermute x6, waiting for transfers between devices, swap(): return lax.ppermute(value, 'az', [(i, i ^ mask) for i in range(sectors)])  4.24 us
    ppermute x6, waiting for transfers between devices, exchange(): lax.ppermute(value, axis, [(i, i ^ m) for i in range(size)])  0.65 us
  transfers between devices with their start and end apart: 12, of which 5 were waited for; matrix products, arithmetic and copies ran while one was open for 0% of the time, Pallas kernels for 17%

profile of v7, /device:TPU:0, one launch (start us, length us, event | category | flops | bytes accessed | tf_op | source)
XLA Modules:
  0.0 30.7 jit_solution(10740876319200615541)
XLA Ops:
  0.6 1.7 %shard_map.104 = (f32[5,48,512]{2,1,0:T(8,128)S(1)}, s32[1,48]{1,0:T(1,128)S(1)}, f32[3,48]{1,0:T(4,128)S(1)}, s32[6,48]{1,0:T(8,128)S(1)}, f32[3,64,48]{2,1,0:T...) custom-call(f32[5,48,512]{2,1,0:T(8,128)} %bitcast.11, ...), custom_call_target="tpu_custom_call" | custom-call | flops 400000000 | bytes 2839040 | tf_op jit(solution)/shard_map/pallas_call | solution.py:507
  2.3 2.5 %collective-permute-start.2 = (f32[128,128]{1,0:T(8,128)S(1)}, f32[128,128]{1,0:T(8,128)S(1)}, u32[]{:S(2)}, u32[]{:S(2)}) collective-permute-start(f32[128,128]{1,0:T(8,128)S(1)} %get-tuple-element.45.refs_0_), channel_id=1, source_target_pairs={{0,3},{1,2},{2,1},{3,0},{4,7},{5,6},{6,5},{7,4},{8,11},{9,10},{10,... | collective-permute-start | bytes 196616 | tf_op jit(solution)/shard_map/ppermute | solution.py:522
  4.8 0.6 %collective-permute-start.1 = (f32[128,128]{1,0:T(8,128)S(1)}, f32[128,128]{1,0:T(8,128)S(1)}, u32[]{:S(2)}, u32[]{:S(2)}) collective-permute-start(f32[128,128]{1,0:T(8,128)S(1)} %get-tuple-element.45.refs_0_), channel_id=1, source_target_pairs={{0,2},{1,3},{2,0},{3,1},{4,6},{5,7},{6,4},{7,5},{8,10},{9,11},{10,... | collective-permute-start | bytes 196616 | tf_op jit(solution)/shard_map/ppermute | solution.py:522
  5.4 0.0 collective-permute-start
  5.5 1.5 %shard_map.105 = (f32[5,48,512]{2,1,0:T(8,128)S(1)}, f32[120,128]{1,0:T(8,128)S(1)}) custom-call(f32[5,48,512]{2,1,0:T(8,128)S(1)} %get-tuple-element.35.state_ref, f32[3,48]{1,0:T(4,128)S(1)} %get-tuple-element.36.velocity_ref, s32[6,48]{1,0:T(8,128)S(1)} %get-tuple-element.37.neigh_ref, s32[1,48]{1,0:T(1,128)S(1)} %get-tuple-element.38.send_ref, ...), custom_call_target="tpu_custom_call" | custom-call | flops 1000000000 | bytes 2332544 | tf_op jit(solution)/shard_map/pallas_call | solution.py:507
  6.9 1.5 %collective-permute-start.5 = (f32[120,128]{1,0:T(8,128)S(1)}, f32[120,128]{1,0:T(8,128)S(1)}, u32[]{:S(2)}, u32[]{:S(2)}) collective-permute-start(f32[120,128]{1,0:T(8,128)S(1)} %get-tuple-element.56), channel_id=1, source_target_pairs={{0,3},{1,2},{2,1},{3,0},{4,7},{5,6},{6,5},{7,4},{8,11},{9,10},{10,... | collective-permute-start | bytes 184328 | tf_op jit(solution)/shard_map/ppermute | solution.py:522
  8.5 0.6 %collective-permute-start.4 = (f32[120,128]{1,0:T(8,128)S(1)}, f32[120,128]{1,0:T(8,128)S(1)}, u32[]{:S(2)}, u32[]{:S(2)}) collective-permute-start(f32[120,128]{1,0:T(8,128)S(1)} %get-tuple-element.56), channel_id=1, source_target_pairs={{0,2},{1,3},{2,0},{3,1},{4,6},{5,7},{6,4},{7,5},{8,10},{9,11},{10,... | collective-permute-start | bytes 184328 | tf_op jit(solution)/shard_map/ppermute | solution.py:522
  9.1 0.0 collective-permute-done.2.refs_3_
  9.1 0.0 collective-permute-start.3
  9.1 0.4 %collective-permute-done.1.refs_2_ = f32[128,128]{1,0:T(8,128)S(1)} collective-permute-done((f32[128,128]{1,0:T(8,128)S(1)}, f32[128,128]{1,0:T(8,128)S(1)}, u32[]{:S(2)}, u32[]{:S(2)}) %collective-permute-start.1) | collective-permute-done | bytes 65568 | tf_op jit(solution)/shard_map/ppermute | solution.py:522
  9.5 0.0 collective-permute-done.refs_1_
  9.5 3.0 %shard_map.106 = (f32[5,48,512]{2,1,0:T(8,128)S(1)}, f32[192,640]{1,0:T(8,128)S(1)}, bf16[288,192]{1,0:T(8,128)(2,1)S(1)}, f32[64,128]{1,0:T(8,128)S(1)}, f32[64...) custom-call(f32[5,48,512]{2,1,0:T(8,128)S(1)} %get-tuple-element.35.state_ref, ...), custom_call_target="tpu_custom_call" | custom-call | flops 1500000000 | bytes 4704512 | tf_op jit(solution)/shard_map/pallas_call | solution.py:507
  12.5 0.0 collective-permute-done.5.refs_2_
  12.5 0.3 collective-permute-done.4.refs_1_
  12.8 0.0 collective-permute-done.3.refs_0_
  12.8 1.9 %shard_map.107 = (f32[5,48,512]{2,1,0:T(8,128)S(1)}, f32[2,160,128]{2,1,0:T(8,128)S(1)}, f32[160,128]{1,0:T(8,128)S(1)}, f32[160,128]{1,0:T(8,128)S(1)}, f32[160...) custom-call(f32[5,48,512]{2,1,0:T(8,128)S(1)} %get-tuple-element.49.base_ref, ...), custom_call_target="tpu_custom_call" | custom-call | flops 800000000 | bytes 3801088 | tf_op jit(solution)/shard_map/pallas_call | solution.py:507
  14.7 1.6 %collective-permute-start.8 = (f32[2,160,128]{2,1,0:T(8,128)S(1)}, f32[2,160,128]{2,1,0:T(8,128)S(1)}, u32[]{:S(2)}, u32[]{:S(2)}) collective-permute-start(f32[2,160,128]{2,1,0:T(8,128)S(1)} %get-tuple-element.60), channel_id=1, source_target_pairs={{0,4},{4,0},{8,12},{12,8},{16,20},{20,16},{24,28},{28,24},{1,5},{5... | collective-permute-start | bytes 491528 | tf_op jit(solution)/shard_map/ppermute | solution.py:589
  16.3 2.6 %collective-permute-start.6 = (f32[160,128]{1,0:T(8,128)S(1)}, f32[160,128]{1,0:T(8,128)S(1)}, u32[]{:S(2)}, u32[]{:S(2)}) collective-permute-start(f32[160,128]{1,0:T(8,128)S(1)} %get-tuple-element.58), channel_id=1, source_target_pairs={{0,16},{4,20},{8,24},{12,28},{16,0},{20,4},{24,8},{28,12},{1,17},{... | collective-permute-start | bytes 245768 | tf_op jit(solution)/shard_map/ppermute | solution.py:589
  18.9 0.3 collective-permute-start.7
  19.2 1.6 %collective-permute-done.8.got_ref = f32[2,160,128]{2,1,0:T(8,128)S(1)} collective-permute-done((f32[2,160,128]{2,1,0:T(8,128)S(1)}, f32[2,160,128]{2,1,0:T(8,128)S(1)}, u32[]{:S(2)}, u32[]{:S(2)}) %collective-permute-start.8) | collective-permute-done | bytes 163872 | tf_op jit(solution)/shard_map/ppermute | solution.py:589
  20.8 3.7 %collective-permute-start.9 = (f32[160,128]{1,0:T(8,128)S(1)}, f32[160,128]{1,0:T(8,128)S(1)}, u32[]{:S(2)}, u32[]{:S(2)}) collective-permute-start(f32[160,128]{1,0:T(8,128)S(1)} %get-tuple-element.64), channel_id=1, source_target_pairs={{0,24},{4,28},{8,16},{12,20},{16,8},{20,12},{24,0},{28,4},{1,25},{... | collective-permute-start | bytes 245768 | tf_op jit(solution)/shard_map/ppermute | solution.py:589
  24.5 0.3 %collective-permute-start.10 = (f32[160,128]{1,0:T(8,128)S(1)}, f32[160,128]{1,0:T(8,128)S(1)}, u32[]{:S(2)}, u32[]{:S(2)}) collective-permute-start(f32[160,128]{1,0:T(8,128)S(1)} %get-tuple-element.65), channel_id=1, source_target_pairs={{0,8},{4,12},{8,0},{12,4},{16,24},{20,28},{24,16},{28,20},{1,9},{5... | collective-permute-start | bytes 245768 | tf_op jit(solution)/shard_map/ppermute | solution.py:589
  24.8 1.6 %collective-permute-start.11 = (f32[160,128]{1,0:T(8,128)S(1)}, f32[160,128]{1,0:T(8,128)S(1)}, u32[]{:S(2)}, u32[]{:S(2)}) collective-permute-start(f32[160,128]{1,0:T(8,128)S(1)} %get-tuple-element.66), channel_id=1, source_target_pairs={{0,4},{4,0},{8,12},{12,8},{16,20},{20,16},{24,28},{28,24},{1,5},{5... | collective-permute-start | bytes 245768 | tf_op jit(solution)/shard_map/ppermute | solution.py:589
  26.4 0.0 copy-start
  26.4 0.8 %shard_map.108 = f32[5,48,512]{2,1,0:T(8,128)} custom-call(f32[5,48,512]{2,1,0:T(8,128)S(1)} %get-tuple-element.57.new_ref), custom_call_target="tpu_custom_call" | custom-call | bytes 983040 | tf_op jit(solution)/shard_map/pallas_call | solution.py:507
  27.2 0.0 collective-permute-done.6.refs_0_
  27.2 1.8 %collective-permute-done.7.refs_1_ = f32[160,128]{1,0:T(8,128)S(1)} collective-permute-done((f32[160,128]{1,0:T(8,128)S(1)}, f32[160,128]{1,0:T(8,128)S(1)}, u32[]{:S(2)}, u32[]{:S(2)}) %collective-permute-start.7) | collective-permute-done | bytes 81952 | tf_op jit(solution)/shard_map/ppermute | solution.py:589
  29.0 0.0 collective-permute-done.9.refs_2_
  29.0 0.8 %collective-permute-done.10.refs_3_ = f32[160,128]{1,0:T(8,128)S(1)} collective-permute-done((f32[160,128]{1,0:T(8,128)S(1)}, f32[160,128]{1,0:T(8,128)S(1)}, u32[]{:S(2)}, u32[]{:S(2)}) %collective-permute-start.10) | collective-permute-done | bytes 81952 | tf_op jit(solution)/shard_map/ppermute | solution.py:589
  29.8 0.0 collective-permute-done.11.refs_4_
  29.8 0.0 copy-done
  29.8 0.9 %shard_map.110 = f32[2,5,32,128]{3,2,1,0:T(8,128)} custom-call(f32[128,256]{1,0:T(8,128)S(1)} %copy-done, f32[160,128]{1,0:T(8,128)S(1)} %collective-permute-done.6.refs_0_, f32[160,128]{1,0:T(8,128)S(1)} %collective-permute-done.7.refs_1_, f32[160,128]{1,0:T(8,128)S(1)} %collective-permute-done.9.refs_2_, f32[160,128]{1,0:T(8,128)S(1)} %collective-permute-done.10.refs_3_, ...), custom_call_target="tpu_custom_call" | custom-call | flops 100000000 | bytes 786432 | tf_op jit(solution)/shard_map/pallas_call | solution.py:507
  (1 shorter events, 0.0 us)
Async XLA Ops:
  2.3 6.8 %collective-permute-start.2 = (f32[128,128]{1,0:T(8,128)S(1)}, f32[128,128]{1,0:T(8,128)S(1)}, u32[]{:S(2)}, u32[]{:S(2)}) collective-permute-start(f32[128,128]{1,0:T(8,128)S(1)} %get-tuple-element.45.refs_0_), channel_id=1, source_target_pairs={{0,3},{1,2},{2,1},{3,0},{4,7},{5,6},{6,5},{7,4},{8,11},{9,10},{10,... | collective-permute-start | bytes 196616 | tf_op jit(solution)/shard_map/ppermute | solution.py:522
  4.8 4.7 %collective-permute-start.1 = (f32[128,128]{1,0:T(8,128)S(1)}, f32[128,128]{1,0:T(8,128)S(1)}, u32[]{:S(2)}, u32[]{:S(2)}) collective-permute-start(f32[128,128]{1,0:T(8,128)S(1)} %get-tuple-element.45.refs_0_), channel_id=1, source_target_pairs={{0,2},{1,3},{2,0},{3,1},{4,6},{5,7},{6,4},{7,5},{8,10},{9,11},{10,... | collective-permute-start | bytes 196616 | tf_op jit(solution)/shard_map/ppermute | solution.py:522
  5.4 4.0 %collective-permute-start = (f32[128,128]{1,0:T(8,128)S(1)}, f32[128,128]{1,0:T(8,128)S(1)}, u32[]{:S(2)}, u32[]{:S(2)}) collective-permute-start(f32[128,128]{1,0:T(8,128)S(1)} %get-tuple-element.45.refs_0_), channel_id=1, source_target_pairs={{0,1},{1,0},{2,3},{3,2},{4,5},{5,4},{6,7},{7,6},{8,9},{9,8},{10,11... | collective-permute-start | bytes 196616 | tf_op jit(solution)/shard_map/ppermute | solution.py:522
  6.9 5.6 %collective-permute-start.5 = (f32[120,128]{1,0:T(8,128)S(1)}, f32[120,128]{1,0:T(8,128)S(1)}, u32[]{:S(2)}, u32[]{:S(2)}) collective-permute-start(f32[120,128]{1,0:T(8,128)S(1)} %get-tuple-element.56), channel_id=1, source_target_pairs={{0,3},{1,2},{2,1},{3,0},{4,7},{5,6},{6,5},{7,4},{8,11},{9,10},{10,... | collective-permute-start | bytes 184328 | tf_op jit(solution)/shard_map/ppermute | solution.py:522
  8.5 4.3 %collective-permute-start.4 = (f32[120,128]{1,0:T(8,128)S(1)}, f32[120,128]{1,0:T(8,128)S(1)}, u32[]{:S(2)}, u32[]{:S(2)}) collective-permute-start(f32[120,128]{1,0:T(8,128)S(1)} %get-tuple-element.56), channel_id=1, source_target_pairs={{0,2},{1,3},{2,0},{3,1},{4,6},{5,7},{6,4},{7,5},{8,10},{9,11},{10,... | collective-permute-start | bytes 184328 | tf_op jit(solution)/shard_map/ppermute | solution.py:522
  9.1 3.7 %collective-permute-start.3 = (f32[120,128]{1,0:T(8,128)S(1)}, f32[120,128]{1,0:T(8,128)S(1)}, u32[]{:S(2)}, u32[]{:S(2)}) collective-permute-start(f32[120,128]{1,0:T(8,128)S(1)} %get-tuple-element.56), channel_id=1, source_target_pairs={{0,1},{1,0},{2,3},{3,2},{4,5},{5,4},{6,7},{7,6},{8,9},{9,8},{10,11... | collective-permute-start | bytes 184328 | tf_op jit(solution)/shard_map/ppermute | solution.py:522
  14.7 6.1 %collective-permute-start.8 = (f32[2,160,128]{2,1,0:T(8,128)S(1)}, f32[2,160,128]{2,1,0:T(8,128)S(1)}, u32[]{:S(2)}, u32[]{:S(2)}) collective-permute-start(f32[2,160,128]{2,1,0:T(8,128)S(1)} %get-tuple-element.60), channel_id=1, source_target_pairs={{0,4},{4,0},{8,12},{12,8},{16,20},{20,16},{24,28},{28,24},{1,5},{5... | collective-permute-start | bytes 491528 | tf_op jit(solution)/shard_map/ppermute | solution.py:589
  16.3 10.9 %collective-permute-start.6 = (f32[160,128]{1,0:T(8,128)S(1)}, f32[160,128]{1,0:T(8,128)S(1)}, u32[]{:S(2)}, u32[]{:S(2)}) collective-permute-start(f32[160,128]{1,0:T(8,128)S(1)} %get-tuple-element.58), channel_id=1, source_target_pairs={{0,16},{4,20},{8,24},{12,28},{16,0},{20,4},{24,8},{28,12},{1,17},{... | collective-permute-start | bytes 245768 | tf_op jit(solution)/shard_map/ppermute | solution.py:589
  18.9 10.1 %collective-permute-start.7 = (f32[160,128]{1,0:T(8,128)S(1)}, f32[160,128]{1,0:T(8,128)S(1)}, u32[]{:S(2)}, u32[]{:S(2)}) collective-permute-start(f32[160,128]{1,0:T(8,128)S(1)} %get-tuple-element.59), channel_id=1, source_target_pairs={{0,20},{4,16},{8,28},{12,24},{16,4},{20,0},{24,12},{28,8},{1,21},{... | collective-permute-start | bytes 245768 | tf_op jit(solution)/shard_map/ppermute | solution.py:589
  20.8 8.2 %collective-permute-start.9 = (f32[160,128]{1,0:T(8,128)S(1)}, f32[160,128]{1,0:T(8,128)S(1)}, u32[]{:S(2)}, u32[]{:S(2)}) collective-permute-start(f32[160,128]{1,0:T(8,128)S(1)} %get-tuple-element.64), channel_id=1, source_target_pairs={{0,24},{4,28},{8,16},{12,20},{16,8},{20,12},{24,0},{28,4},{1,25},{... | collective-permute-start | bytes 245768 | tf_op jit(solution)/shard_map/ppermute | solution.py:589
  24.5 5.3 %collective-permute-start.10 = (f32[160,128]{1,0:T(8,128)S(1)}, f32[160,128]{1,0:T(8,128)S(1)}, u32[]{:S(2)}, u32[]{:S(2)}) collective-permute-start(f32[160,128]{1,0:T(8,128)S(1)} %get-tuple-element.65), channel_id=1, source_target_pairs={{0,8},{4,12},{8,0},{12,4},{16,24},{20,28},{24,16},{28,20},{1,9},{5... | collective-permute-start | bytes 245768 | tf_op jit(solution)/shard_map/ppermute | solution.py:589
  24.8 5.0 %collective-permute-start.11 = (f32[160,128]{1,0:T(8,128)S(1)}, f32[160,128]{1,0:T(8,128)S(1)}, u32[]{:S(2)}, u32[]{:S(2)}) collective-permute-start(f32[160,128]{1,0:T(8,128)S(1)} %get-tuple-element.66), channel_id=1, source_target_pairs={{0,4},{4,0},{8,12},{12,8},{16,20},{20,16},{24,28},{28,24},{1,5},{5... | collective-permute-start | bytes 245768 | tf_op jit(solution)/shard_map/ppermute | solution.py:589
  26.4 3.4 %copy-start = (f32[128,256]{1,0:T(8,128)S(1)}, f32[128,256]{1,0:T(8,128)}, u32[]{:S(2)}) copy-start(f32[128,256]{1,0:T(8,128)} %constant.5.clone.table_ref) | copy-start | bytes 393220

commit v8 on v7

--- a/solution.py
+++ b/solution.py
@@ -307,7 +307,8 @@
 
 
 def first_local_kernel(
-    state_ref, velocity_ref, neigh_ref, send_ref, table_ref, yz, lift, extract, out_ref, shared_ref
+    state_ref, velocity_ref, neigh_ref, send_ref, table_ref, yz, lift, extract,
+    maps_ref, device_ref, block_ref, out_ref, shared_ref, *map_refs
 ):
     fields = rows_of(state_ref)
     rate = local_rate(
@@ -317,6 +318,7 @@
     out_ref[...] = base.reshape(out_ref.shape)
     picked = pick_rows(column(send_ref), local_key(send_ref.shape[1]))
     share_rows(face_table(base + remainder(fields), extract[...]), picked, shared_ref)
+    fill_maps(maps_ref, device_ref, block_ref, *map_refs)
 
 
 def fill_maps(
@@ -364,9 +366,7 @@
 def second_local_kernel(
     state_ref, base_ref, velocity_ref, neigh_ref, send_ref, yz, lift, extract, cross, *refs
 ):
-    shared_refs, map_refs = refs[:-10], refs[-10:-7] + refs[-4:]
-    out_ref, added_ref, picked_ref = refs[-7:-4]
-    fill_maps(*map_refs)
+    shared_refs, (out_ref, added_ref, picked_ref) = refs[:-3], refs[-3:]
     elements = neigh_ref.shape[1]
     table = shared_table(shared_refs, elements).astype(bf16)
     keys = remote_keys(elements)
@@ -477,7 +477,9 @@
         total = total + ref[...]
     high, low = split(total)
     weight, weight_low = split(table_ref[...])
-    coeffs = dot(high, weight) + dot(low, weight) + dot(high, weight_low)
+    coeffs = dot(
+        jnp.concatenate([high, low], axis=1), jnp.concatenate([weight, weight], axis=0)
+    ) + dot(high, weight_low)
     width = total.shape[1]
     rows = total.shape[0] // FIELDS
     for k in range(2):
@@ -553,19 +555,20 @@
     fields, sends, speed, names, maps, places, blocks, yz, extract, lift, cross, table, shared = loaded
     cube = shape(fields.shape)
     others = exchange(shared, "ax")
-    base, shared = call(
-        first_local_kernel, (cube, shape((travel, 128))),
-        fields, speed, names, sends, table, yz, lift, extract,
-        flops=1_000_000_000,
-    )
-    firsts = exchange(shared, "ax")
     lanes = sectors * TB * 8
     weights = shape((512, PB * lanes), bf16)
-    base, added, picked, radial, axial, weight_high, weight_low = call(
+    base, shared, radial, axial, weight_high, weight_low = call(
+        first_local_kernel,
+        (cube, shape((travel, 128)), shape((64, 128)), shape((64, 128)), weights, weights),
+        fields, speed, names, sends, table, yz, lift, extract, maps, places, blocks,
+        flops=1_000_000_000,
+    )
+    firsts = exchange(shared, "ax")
+    shares = lax.axis_size("ax") * elements
+    base, added, picked = call(
         second_local_kernel,
-        (cube, shape((lax.axis_size("ax") * elements, FIELDS * 128)))
-        + (shape((6 * elements, lax.axis_size("ax") * elements), bf16), shape((64, 128)), shape((64, 128)), weights, weights),
-        fields, base, speed, names, sends, yz, lift, extract, cross, *others, maps, places, blocks,
+        (cube, shape((shares, FIELDS * 128)), shape((6 * elements, shares), bf16)),
+        fields, base, speed, names, sends, yz, lift, extract, cross, *others,
         flops=1_500_000_000,
     )
     rows = FIELDS * 64 * PB // sectors

time: 30.9 us -> 30.8 us (level)
    ppermute x6, waiting for transfers between devices: 4.24 us -> 3.89 us  [swap(): return lax.ppermute(value, 'az', [(i, i ^ mask) for i in range(sectors)])]
where the time goes in v8:
time: 30.8 us; the launch traced here: 30.6 us
  starting transfers between devices  15.4 us (50%)
  Pallas kernels  9.72 us (32%)
  waiting for transfers between devices  4.79 us (16%)
  between operations  0.7 us (2%)
    ppermute x6, starting transfers between devices, swap(): return lax.ppermute(value, 'az', [(i, i ^ mask) for i in range(sectors)])  10.1 us
    pallas_call x7, Pallas kernels, call(): pl.pallas_call(kernel, out_shape=outs, in_specs=[pl.BlockSpec(memory_spac...  9.72 us
    ppermute x6, starting transfers between devices, exchange(): lax.ppermute(value, axis, [(i, i ^ m) for i in range(size)])  5.32 us
    ppermute x6, waiting for transfers between devices, swap(): return lax.ppermute(value, 'az', [(i, i ^ mask) for i in range(sectors)])  3.89 us
    ppermute x6, waiting for transfers between devices, exchange(): lax.ppermute(value, axis, [(i, i ^ m) for i in range(size)])  0.9 us
  transfers between devices with their start and end apart: 12, of which 5 were waited for; matrix products, arithmetic and copies ran while one was open for 0% of the time, Pallas kernels for 17%

profile of v8, /device:TPU:0, one launch (start us, length us, event | category | flops | bytes accessed | tf_op | source)
XLA Modules:
  0.0 30.6 jit_solution(8949529294374958544)
XLA Ops:
  0.6 1.7 %shard_map.104 = (f32[5,48,512]{2,1,0:T(8,128)S(1)}, s32[1,48]{1,0:T(1,128)S(1)}, f32[3,48]{1,0:T(4,128)S(1)}, s32[6,48]{1,0:T(8,128)S(1)}, f32[3,64,48]{2,1,0:T...) custom-call(f32[5,48,512]{2,1,0:T(8,128)} %bitcast.11, ...), custom_call_target="tpu_custom_call" | custom-call | flops 400000000 | bytes 2839040 | tf_op jit(solution)/shard_map/pallas_call | solution.py:509
  2.3 2.5 %collective-permute-start.2 = (f32[128,128]{1,0:T(8,128)S(1)}, f32[128,128]{1,0:T(8,128)S(1)}, u32[]{:S(2)}, u32[]{:S(2)}) collective-permute-start(f32[128,128]{1,0:T(8,128)S(1)} %get-tuple-element.48.refs_0_), channel_id=1, source_target_pairs={{0,3},{1,2},{2,1},{3,0},{4,7},{5,6},{6,5},{7,4},{8,11},{9,10},{10,... | collective-permute-start | bytes 196616 | tf_op jit(solution)/shard_map/ppermute | solution.py:524
  4.8 0.6 %collective-permute-start.1 = (f32[128,128]{1,0:T(8,128)S(1)}, f32[128,128]{1,0:T(8,128)S(1)}, u32[]{:S(2)}, u32[]{:S(2)}) collective-permute-start(f32[128,128]{1,0:T(8,128)S(1)} %get-tuple-element.48.refs_0_), channel_id=1, source_target_pairs={{0,2},{1,3},{2,0},{3,1},{4,6},{5,7},{6,4},{7,5},{8,10},{9,11},{10,... | collective-permute-start | bytes 196616 | tf_op jit(solution)/shard_map/ppermute | solution.py:524
  5.4 0.0 collective-permute-start
  5.5 1.6 %shard_map.105 = (f32[5,48,512]{2,1,0:T(8,128)S(1)}, f32[120,128]{1,0:T(8,128)S(1)}, f32[64,128]{1,0:T(8,128)S(1)}, f32[64,128]{1,0:T(8,128)S(1)}, bf16[512,512]...) custom-call(f32[5,48,512]{2,1,0:T(8,128)S(1)} %get-tuple-element.35.state_ref, f32[3,48]{1,0:T(4,128)S(1)} %get-tuple-element.36.velocity_ref, ...), custom_call_target="tpu_custom_call" | custom-call | flops 1000000000 | bytes 3483904 | tf_op jit(solution)/shard_map/pallas_call | solution.py:509
  7.1 1.5 %collective-permute-start.5 = (f32[120,128]{1,0:T(8,128)S(1)}, f32[120,128]{1,0:T(8,128)S(1)}, u32[]{:S(2)}, u32[]{:S(2)}) collective-permute-start(f32[120,128]{1,0:T(8,128)S(1)} %get-tuple-element.56), channel_id=1, source_target_pairs={{0,3},{1,2},{2,1},{3,0},{4,7},{5,6},{6,5},{7,4},{8,11},{9,10},{10,... | collective-permute-start | bytes 184328 | tf_op jit(solution)/shard_map/ppermute | solution.py:524
  8.7 0.6 %collective-permute-start.4 = (f32[120,128]{1,0:T(8,128)S(1)}, f32[120,128]{1,0:T(8,128)S(1)}, u32[]{:S(2)}, u32[]{:S(2)}) collective-permute-start(f32[120,128]{1,0:T(8,128)S(1)} %get-tuple-element.56), channel_id=1, source_target_pairs={{0,2},{1,3},{2,0},{3,1},{4,6},{5,7},{6,4},{7,5},{8,10},{9,11},{10,... | collective-permute-start | bytes 184328 | tf_op jit(solution)/shard_map/ppermute | solution.py:524
  9.3 0.0 collective-permute-done.2.refs_3_
  9.3 0.0 collective-permute-start.3
  9.3 0.2 collective-permute-done.1.refs_2_
  9.5 0.0 collective-permute-done.refs_1_
  9.5 2.8 %shard_map.106 = (f32[5,48,512]{2,1,0:T(8,128)S(1)}, f32[192,640]{1,0:T(8,128)S(1)}, bf16[288,192]{1,0:T(8,128)(2,1)S(1)}) custom-call(f32[5,48,512]{2,1,0:T(8,128)S(1)} %get-tuple-element.35.state_ref, f32[5,48,512]{2,1,0:T(8,128)S(1)} %get-tuple-element.46.base_ref, f32[3,48]{1,0:T(4,128)S(1)} %get-tuple-element.36.velocity_ref, ...), custom_call_target="tpu_custom_call" | custom-call | flops 1500000000 | bytes 3553152 | tf_op jit(solution)/shard_map/pallas_call | solution.py:509
  12.3 0.0 collective-permute-done.5.refs_2_
  12.3 0.7 %collective-permute-done.4.refs_1_ = f32[120,128]{1,0:T(8,128)S(1)} collective-permute-done((f32[120,128]{1,0:T(8,128)S(1)}, f32[120,128]{1,0:T(8,128)S(1)}, u32[]{:S(2)}, u32[]{:S(2)}) %collective-permute-start.4) | collective-permute-done | bytes 61472 | tf_op jit(solution)/shard_map/ppermute | solution.py:524
  13.0 0.0 collective-permute-done.3.refs_0_
  13.0 1.9 %shard_map.107 = (f32[5,48,512]{2,1,0:T(8,128)S(1)}, f32[2,160,128]{2,1,0:T(8,128)S(1)}, f32[160,128]{1,0:T(8,128)S(1)}, f32[160,128]{1,0:T(8,128)S(1)}, f32[160...) custom-call(f32[5,48,512]{2,1,0:T(8,128)S(1)} %get-tuple-element.49.base_ref, ...), custom_call_target="tpu_custom_call" | custom-call | flops 800000000 | bytes 3801088 | tf_op jit(solution)/shard_map/pallas_call | solution.py:509
  14.9 1.6 %collective-permute-start.8 = (f32[2,160,128]{2,1,0:T(8,128)S(1)}, f32[2,160,128]{2,1,0:T(8,128)S(1)}, u32[]{:S(2)}, u32[]{:S(2)}) collective-permute-start(f32[2,160,128]{2,1,0:T(8,128)S(1)} %get-tuple-element.60), channel_id=1, source_target_pairs={{0,4},{4,0},{8,12},{12,8},{16,20},{20,16},{24,28},{28,24},{1,5},{5... | collective-permute-start | bytes 491528 | tf_op jit(solution)/shard_map/ppermute | solution.py:592
  16.5 2.6 %collective-permute-start.6 = (f32[160,128]{1,0:T(8,128)S(1)}, f32[160,128]{1,0:T(8,128)S(1)}, u32[]{:S(2)}, u32[]{:S(2)}) collective-permute-start(f32[160,128]{1,0:T(8,128)S(1)} %get-tuple-element.58), channel_id=1, source_target_pairs={{0,16},{4,20},{8,24},{12,28},{16,0},{20,4},{24,8},{28,12},{1,17},{... | collective-permute-start | bytes 245768 | tf_op jit(solution)/shard_map/ppermute | solution.py:592
  19.1 0.3 collective-permute-start.7
  19.4 1.4 %collective-permute-done.8.got_ref = f32[2,160,128]{2,1,0:T(8,128)S(1)} collective-permute-done((f32[2,160,128]{2,1,0:T(8,128)S(1)}, f32[2,160,128]{2,1,0:T(8,128)S(1)}, u32[]{:S(2)}, u32[]{:S(2)}) %collective-permute-start.8) | collective-permute-done | bytes 163872 | tf_op jit(solution)/shard_map/ppermute | solution.py:592
  20.8 3.7 %collective-permute-start.9 = (f32[160,128]{1,0:T(8,128)S(1)}, f32[160,128]{1,0:T(8,128)S(1)}, u32[]{:S(2)}, u32[]{:S(2)}) collective-permute-start(f32[160,128]{1,0:T(8,128)S(1)} %get-tuple-element.64), channel_id=1, source_target_pairs={{0,24},{4,28},{8,16},{12,20},{16,8},{20,12},{24,0},{28,4},{1,25},{... | collective-permute-start | bytes 245768 | tf_op jit(solution)/shard_map/ppermute | solution.py:592
  24.5 0.4 %collective-permute-start.10 = (f32[160,128]{1,0:T(8,128)S(1)}, f32[160,128]{1,0:T(8,128)S(1)}, u32[]{:S(2)}, u32[]{:S(2)}) collective-permute-start(f32[160,128]{1,0:T(8,128)S(1)} %get-tuple-element.65), channel_id=1, source_target_pairs={{0,8},{4,12},{8,0},{12,4},{16,24},{20,28},{24,16},{28,20},{1,9},{5... | collective-permute-start | bytes 245768 | tf_op jit(solution)/shard_map/ppermute | solution.py:592
  25.0 1.5 %collective-permute-start.11 = (f32[160,128]{1,0:T(8,128)S(1)}, f32[160,128]{1,0:T(8,128)S(1)}, u32[]{:S(2)}, u32[]{:S(2)}) collective-permute-start(f32[160,128]{1,0:T(8,128)S(1)} %get-tuple-element.66), channel_id=1, source_target_pairs={{0,4},{4,0},{8,12},{12,8},{16,20},{20,16},{24,28},{28,24},{1,5},{5... | collective-permute-start | bytes 245768 | tf_op jit(solution)/shard_map/ppermute | solution.py:592
  26.4 0.0 copy-start
  26.4 0.8 %shard_map.108 = f32[5,48,512]{2,1,0:T(8,128)} custom-call(f32[5,48,512]{2,1,0:T(8,128)S(1)} %get-tuple-element.57.new_ref), custom_call_target="tpu_custom_call" | custom-call | bytes 983040 | tf_op jit(solution)/shard_map/pallas_call | solution.py:509
  27.2 0.0 collective-permute-done.6.refs_0_
  27.2 1.8 %collective-permute-done.7.refs_1_ = f32[160,128]{1,0:T(8,128)S(1)} collective-permute-done((f32[160,128]{1,0:T(8,128)S(1)}, f32[160,128]{1,0:T(8,128)S(1)}, u32[]{:S(2)}, u32[]{:S(2)}) %collective-permute-start.7) | collective-permute-done | bytes 81952 | tf_op jit(solution)/shard_map/ppermute | solution.py:592
  29.1 0.0 collective-permute-done.9.refs_2_
  29.1 0.7 %collective-permute-done.10.refs_3_ = f32[160,128]{1,0:T(8,128)S(1)} collective-permute-done((f32[160,128]{1,0:T(8,128)S(1)}, f32[160,128]{1,0:T(8,128)S(1)}, u32[]{:S(2)}, u32[]{:S(2)}) %collective-permute-start.10) | collective-permute-done | bytes 81952 | tf_op jit(solution)/shard_map/ppermute | solution.py:592
  29.8 0.0 collective-permute-done.11.refs_4_
  29.8 0.0 copy-done
  29.8 0.9 %shard_map.110 = f32[2,5,32,128]{3,2,1,0:T(8,128)} custom-call(f32[128,256]{1,0:T(8,128)S(1)} %copy-done, f32[160,128]{1,0:T(8,128)S(1)} %collective-permute-done.6.refs_0_, f32[160,128]{1,0:T(8,128)S(1)} %collective-permute-done.7.refs_1_, f32[160,128]{1,0:T(8,128)S(1)} %collective-permute-done.9.refs_2_, f32[160,128]{1,0:T(8,128)S(1)} %collective-permute-done.10.refs_3_, ...), custom_call_target="tpu_custom_call" | custom-call | flops 100000000 | bytes 786432 | tf_op jit(solution)/shard_map/pallas_call | solution.py:509
  (1 shorter events, 0.0 us)
Async XLA Ops:
  2.3 7.0 %collective-permute-start.2 = (f32[128,128]{1,0:T(8,128)S(1)}, f32[128,128]{1,0:T(8,128)S(1)}, u32[]{:S(2)}, u32[]{:S(2)}) collective-permute-start(f32[128,128]{1,0:T(8,128)S(1)} %get-tuple-element.48.refs_0_), channel_id=1, source_target_pairs={{0,3},{1,2},{2,1},{3,0},{4,7},{5,6},{6,5},{7,4},{8,11},{9,10},{10,... | collective-permute-start | bytes 196616 | tf_op jit(solution)/shard_map/ppermute | solution.py:524
  4.8 4.7 %collective-permute-start.1 = (f32[128,128]{1,0:T(8,128)S(1)}, f32[128,128]{1,0:T(8,128)S(1)}, u32[]{:S(2)}, u32[]{:S(2)}) collective-permute-start(f32[128,128]{1,0:T(8,128)S(1)} %get-tuple-element.48.refs_0_), channel_id=1, source_target_pairs={{0,2},{1,3},{2,0},{3,1},{4,6},{5,7},{6,4},{7,5},{8,10},{9,11},{10,... | collective-permute-start | bytes 196616 | tf_op jit(solution)/shard_map/ppermute | solution.py:524
  5.4 4.0 %collective-permute-start = (f32[128,128]{1,0:T(8,128)S(1)}, f32[128,128]{1,0:T(8,128)S(1)}, u32[]{:S(2)}, u32[]{:S(2)}) collective-permute-start(f32[128,128]{1,0:T(8,128)S(1)} %get-tuple-element.48.refs_0_), channel_id=1, source_target_pairs={{0,1},{1,0},{2,3},{3,2},{4,5},{5,4},{6,7},{7,6},{8,9},{9,8},{10,11... | collective-permute-start | bytes 196616 | tf_op jit(solution)/shard_map/ppermute | solution.py:524
  7.1 5.1 %collective-permute-start.5 = (f32[120,128]{1,0:T(8,128)S(1)}, f32[120,128]{1,0:T(8,128)S(1)}, u32[]{:S(2)}, u32[]{:S(2)}) collective-permute-start(f32[120,128]{1,0:T(8,128)S(1)} %get-tuple-element.56), channel_id=1, source_target_pairs={{0,3},{1,2},{2,1},{3,0},{4,7},{5,6},{6,5},{7,4},{8,11},{9,10},{10,... | collective-permute-start | bytes 184328 | tf_op jit(solution)/shard_map/ppermute | solution.py:524
  8.7 4.3 %collective-permute-start.4 = (f32[120,128]{1,0:T(8,128)S(1)}, f32[120,128]{1,0:T(8,128)S(1)}, u32[]{:S(2)}, u32[]{:S(2)}) collective-permute-start(f32[120,128]{1,0:T(8,128)S(1)} %get-tuple-element.56), channel_id=1, source_target_pairs={{0,2},{1,3},{2,0},{3,1},{4,6},{5,7},{6,4},{7,5},{8,10},{9,11},{10,... | collective-permute-start | bytes 184328 | tf_op jit(solution)/shard_map/ppermute | solution.py:524
  9.3 3.7 %collective-permute-start.3 = (f32[120,128]{1,0:T(8,128)S(1)}, f32[120,128]{1,0:T(8,128)S(1)}, u32[]{:S(2)}, u32[]{:S(2)}) collective-permute-start(f32[120,128]{1,0:T(8,128)S(1)} %get-tuple-element.56), channel_id=1, source_target_pairs={{0,1},{1,0},{2,3},{3,2},{4,5},{5,4},{6,7},{7,6},{8,9},{9,8},{10,11... | collective-permute-start | bytes 184328 | tf_op jit(solution)/shard_map/ppermute | solution.py:524
  14.9 5.8 %collective-permute-start.8 = (f32[2,160,128]{2,1,0:T(8,128)S(1)}, f32[2,160,128]{2,1,0:T(8,128)S(1)}, u32[]{:S(2)}, u32[]{:S(2)}) collective-permute-start(f32[2,160,128]{2,1,0:T(8,128)S(1)} %get-tuple-element.60), channel_id=1, source_target_pairs={{0,4},{4,0},{8,12},{12,8},{16,20},{20,16},{24,28},{28,24},{1,5},{5... | collective-permute-start | bytes 491528 | tf_op jit(solution)/shard_map/ppermute | solution.py:592
  16.5 10.7 %collective-permute-start.6 = (f32[160,128]{1,0:T(8,128)S(1)}, f32[160,128]{1,0:T(8,128)S(1)}, u32[]{:S(2)}, u32[]{:S(2)}) collective-permute-start(f32[160,128]{1,0:T(8,128)S(1)} %get-tuple-element.58), channel_id=1, source_target_pairs={{0,16},{4,20},{8,24},{12,28},{16,0},{20,4},{24,8},{28,12},{1,17},{... | collective-permute-start | bytes 245768 | tf_op jit(solution)/shard_map/ppermute | solution.py:592
  19.1 10.0 %collective-permute-start.7 = (f32[160,128]{1,0:T(8,128)S(1)}, f32[160,128]{1,0:T(8,128)S(1)}, u32[]{:S(2)}, u32[]{:S(2)}) collective-permute-start(f32[160,128]{1,0:T(8,128)S(1)} %get-tuple-element.59), channel_id=1, source_target_pairs={{0,20},{4,16},{8,28},{12,24},{16,4},{20,0},{24,12},{28,8},{1,21},{... | collective-permute-start | bytes 245768 | tf_op jit(solution)/shard_map/ppermute | solution.py:592
  20.8 8.3 %collective-permute-start.9 = (f32[160,128]{1,0:T(8,128)S(1)}, f32[160,128]{1,0:T(8,128)S(1)}, u32[]{:S(2)}, u32[]{:S(2)}) collective-permute-start(f32[160,128]{1,0:T(8,128)S(1)} %get-tuple-element.64), channel_id=1, source_target_pairs={{0,24},{4,28},{8,16},{12,20},{16,8},{20,12},{24,0},{28,4},{1,25},{... | collective-permute-start | bytes 245768 | tf_op jit(solution)/shard_map/ppermute | solution.py:592
  24.5 5.2 %collective-permute-start.10 = (f32[160,128]{1,0:T(8,128)S(1)}, f32[160,128]{1,0:T(8,128)S(1)}, u32[]{:S(2)}, u32[]{:S(2)}) collective-permute-start(f32[160,128]{1,0:T(8,128)S(1)} %get-tuple-element.65), channel_id=1, source_target_pairs={{0,8},{4,12},{8,0},{12,4},{16,24},{20,28},{24,16},{28,20},{1,9},{5... | collective-permute-start | bytes 245768 | tf_op jit(solution)/shard_map/ppermute | solution.py:592
  25.0 4.8 %collective-permute-start.11 = (f32[160,128]{1,0:T(8,128)S(1)}, f32[160,128]{1,0:T(8,128)S(1)}, u32[]{:S(2)}, u32[]{:S(2)}) collective-permute-start(f32[160,128]{1,0:T(8,128)S(1)} %get-tuple-element.66), channel_id=1, source_target_pairs={{0,4},{4,0},{8,12},{12,8},{16,20},{20,16},{24,28},{28,24},{1,5},{5... | collective-permute-start | bytes 245768 | tf_op jit(solution)/shard_map/ppermute | solution.py:592
  26.4 3.3 %copy-start = (f32[128,256]{1,0:T(8,128)S(1)}, f32[128,256]{1,0:T(8,128)}, u32[]{:S(2)}) copy-start(f32[128,256]{1,0:T(8,128)} %constant.5.clone.table_ref) | copy-start | bytes 393220
